TPU v7x, 128 devices: a whole 4x4x4 slice. The times are simulated.
128 devices in a mesh: band: 16 (over x, y_hi, core), lon: 8 (over y_lo, z).
Axes of the slice: x: 4, y: 4 (y_hi: 2, y_lo: 2; y = y_hi * 2 + y_lo), z: 4, core: 2. Of those that a mesh axis runs over, the one named last changes fastest.
Arguments:
- src_tiles: bfloat16 [6, 65536, 128], P(None, ('band', 'lon')), may hold values from -6 to 6
- ent_tile: int32 [32768], P(('band', 'lon')), may hold values from 0 to 65535, as said below
- ent_block: int32 [32768], P(('band', 'lon')), may hold values from 0 to 16383, as said below
- ent_weight: bfloat16 [32768, 128, 128], P(('band', 'lon')), may hold values from 0 to 0.125
- live_count: int32 [128], P(('band', 'lon')), may hold values from 128 to 256, as said below
Outputs:
- remapped: bfloat16 [6, 256, 8192], P(None, 'band', 'lon')
- smoothed: float32 [256, 8192], P('band', 'lon')
Inputs may be any that keep to these rules, and one draw needn't show every extreme that they name: `ent_tile`: A slot of device d = b * 8 + l names a tile (b2 * 8 + l) * 512 + t of the same lon index l; of one device's 256 slots exactly 16 name tiles of each band index b2. `ent_block`: A slot of a device names a target block held by that device. `live_count`: devices of band index 0 and 15 have all slots live.
All inputs are finite; a program needn't handle non-finite values.
Results may differ from a plain program's by a relative error of at most 0.0028.
Values may be sent and summed in bfloat16 or wider, within the bound.
No kernel may reach another device: no remote copies, remote signals or barrier semaphores. Data moves between devices by JAX's collectives and lax.ppermute only.
A program may use at most 128 MiB of HBM per device.

v0:
```python
import jax
import jax.numpy as jnp
from jax import lax
from jax.sharding import PartitionSpec as P

BW = 128
R_DEV = 16
C_DEV = 1024
BLK_DEV = 128


lat_start = 0.5


def extended_2(x, sides, width, wrap):
    for axis, dim in sides:
        size, length = (lax.axis_size(axis), x.shape[dim])
        up = [(i, (i + 1) % size) for i in range(size if wrap else size - 1)]
        down = [(j, i) for i, j in up]
        last = lax.slice_in_dim(x, length - width, length, axis=dim)
        first = lax.slice_in_dim(x, 0, width, axis=dim)
        before = lax.ppermute(last, axis, up)
        after = lax.ppermute(first, axis, down)
        x = jnp.concatenate([before, x, after], axis=dim)
    return x


def keep_rows(field, first_row, overall_rows):
    row_index = first_row + jnp.arange(field.shape[0], dtype=jnp.int32)
    valid = (row_index >= 0) & (row_index < overall_rows)
    return jnp.where(valid[:, None], field, 0.0)


def vorticity(extended, first_row, overall_rows, grid_step):
    east_wind = extended[0].astype(jnp.float32)
    north_wind = extended[1].astype(jnp.float32)
    row_index = first_row + jnp.arange(extended.shape[1], dtype=jnp.int32)
    latitude = lat_start + (row_index.astype(jnp.float32) + 0.5) * grid_step
    cosine = jnp.cos(latitude)[:, None]
    wind_cos = east_wind * cosine
    result = (
        0.5
        * (
            north_wind[1:-1, 2:]
            - north_wind[1:-1, :-2]
            - (wind_cos[2:, 1:-1] - wind_cos[:-2, 1:-1])
        )
        / cosine[1:-1]
    )
    return keep_rows(result, first_row + 1, overall_rows)


def ninepoint_filter(extended):
    centre = extended[1:-1, 1:-1]
    sides = extended[2:, 1:-1] + extended[:-2, 1:-1] + extended[1:-1, 2:] + extended[1:-1, :-2]
    corners = extended[2:, 2:] + extended[2:, :-2] + extended[:-2, 2:] + extended[:-2, :-2]
    return (4.0 * centre + 2.0 * sides + corners) / 16.0


def on_device(src_tiles, ent_tile, ent_block, ent_weight, live_count):
    band_count = lax.axis_size("band")
    lon_count = lax.axis_size("lon")
    band_index = lax.axis_index("band")
    lon_index = lax.axis_index("lon")
    sparse_entries = ent_tile.shape[0]
    tiles_held = src_tiles.shape[1]
    live_mask = jnp.arange(sparse_entries, dtype=jnp.int32) < live_count[0]
    owner_band = ent_tile // (lon_count * tiles_held)
    tile_local = ent_tile % tiles_held
    band_position = owner_band * tiles_held + tile_local
    empty_tiles = jnp.zeros((src_tiles.shape[0], sparse_entries, src_tiles.shape[2]), jnp.bfloat16)
    shard_rows = lax.all_gather(src_tiles, "band", axis=1, tiled=True)
    offset_row = jnp.int32(0)
    tally_rows = shard_rows.shape[1]
    inside = (band_position >= offset_row) & (band_position < offset_row + tally_rows)
    local_index = jnp.clip(band_position, 0, tally_rows - 1)
    fetched = jnp.take(shard_rows, local_index, axis=1)
    picked = jnp.where(inside[None, :, None], fetched, empty_tiles)
    summand = jnp.einsum("cek,ekn->cen", picked, ent_weight, preferred_element_type=jnp.float32)
    blocks_row = C_DEV // BW
    row_global = ent_block // (blocks_row * lon_count)
    column_global = ent_block % (blocks_row * lon_count)
    block_local = (row_global - band_index * R_DEV) * blocks_row + (
        column_global - lon_index * blocks_row
    )
    block_onehot_flags = (
        (block_local[:, None] == jnp.arange(BLK_DEV, dtype=jnp.int32)[None, :]) & live_mask[:, None]
    ).astype(jnp.float32)
    per_block_totals = jnp.einsum(
        "vw,rva->rwa", block_onehot_flags, summand, precision=lax.Precision.HIGHEST
    )
    remapped = per_block_totals.reshape(src_tiles.shape[0], R_DEV, C_DEV).astype(jnp.bfloat16)
    overall_rows = R_DEV * band_count
    grid_step = 2.0 * jnp.pi / (C_DEV * lon_count)
    row_first = band_index * R_DEV
    wind_pair = remapped[2:4]
    extended = extended_2(wind_pair, (("lon", 2),), 1, True)
    extended = extended_2(extended, (("band", 1),), 1, False)
    field = vorticity(extended, row_first - 1, overall_rows, grid_step)
    for pass_index in range(2):
        widened = extended_2(field, (("lon", 1),), 1, True)
        widened = extended_2(widened, (("band", 0),), 1, False)
        field = ninepoint_filter(widened)
    return (remapped, field)


def solution(mesh):
    in_specs = (
        P(None, ("band", "lon"), None),
        P(("band", "lon")),
        P(("band", "lon")),
        P(("band", "lon"), None, None),
        P(("band", "lon")),
    )
    out_specs = (P(None, "band", "lon"), P("band", "lon"))
    return jax.shard_map(
        on_device, mesh=mesh, in_specs=in_specs, out_specs=out_specs, check_vma=False
    )
```

profile of v0, /device:TPU:2, one launch (start us, length us, event | category | flops | bytes accessed | tf_op | source)
XLA Modules:
  0.0 183.9 jit_solution(7659321325666659283)
XLA Ops:
  8.6 0.7 compare_and_fusion.1
  10.0 92.4 %all-gather.2.cloned.1.call-done = bf16[6,8192,128]{2,1,0:T(8,128)(2,1)} async-done(((bf16[6,512,128]{2,1,0:T(8,128)(2,1)}), bf16[6,8192,128]{2,1,0:T(8,128)(2,1)}) %all-gather.2.cloned.1.call-update) | async-done | bytes 12582928 | tf_op jit(solution)/shard_map/all_gather | solution.py:72
  102.4 13.8 %copy.10 = bf16[6,8192,128]{2,0,1:T(8,128)(2,1)} copy(bf16[6,8192,128]{2,1,0:T(8,128)(2,1)} %all-gather.2.cloned.1.call-done) | data formatting | bytes 25165824 | tf_op jit(solution)/shard_map/all_gather | solution.py:72
  116.2 6.6 %gather_fusion = bf16[256,6,128]{2,1,0:T(8,128)(2,1)S(1)} fusion(bf16[6,8192,128]{2,0,1:T(8,128)(2,1)} %copy.10, s32[1024]{0:T(1024)S(1)} %pad_clamp_fusion), kind=kCustom, calls=%fused_computation | custom fusion | bytes 787456 | tf_op jit(solution)/shard_map/jit(_take)/gather | solution.py:77
  122.8 4.7 %convolution_bitcast_fusion = f32[6,256,128]{2,0,1:T(8,128)S(1)} fusion(bf16[256,128,128]{2,1,0:T(8,128)(2,1)} %param.8, bf16[256,6,128]{2,1,0:T(8,128)(2,1)S(1)} %gather_fusion, pred[256]{0:T(512)(128)(4,1)S(1)} %compare_and_fusion.2, pred[256]{0:T(512)(128)(4,1)S(1)} %get-tuple-element.4), kind=kOutput, calls=%fused_computation.1 | convolution fusion | flops 50724864 | bytes 9568768 | tf_op jit(solution)/shard_map/cek,ekn->cen/dot_general | solution.py:79
  127.6 0.9 fusion
  128.8 1.6 collective-permute-start
  130.6 2.7 %collective-permute-start.1 = (bf16[2,16,1]{2,1,0:T(8,128)(2,1)S(1)}, bf16[2,16,1]{2,1,0:T(8,128)(2,1)S(1)}, u32[]{:S(2)}, u32[]{:S(2)}) collective-permute-start(bf16[2,16,1]{2,1,0:T(8,128)(2,1)S(1)} %get-tuple-element.6), channel_id=1, source_target_pairs={{1,0},{2,1},{3,2},{4,3},{5,4},{6,5},{7,6},{0,7},{9,8},{10,9},{11,1... | collective-permute-start | bytes 200 | tf_op jit(solution)/shard_map/ppermute | solution.py:23
  133.2 1.4 collective-permute-done
  134.8 3.0 %collective-permute-start.3 = (bf16[2,1,1026]{2,1,0:T(2,128)(2,1)S(1)}, bf16[2,1,1026]{2,1,0:T(2,128)(2,1)S(1)}, u32[]{:S(2)}, u32[]{:S(2)}) collective-permute-start(bf16[2,1,1026]{2,1,0:T(2,128)(2,1)S(1)} %get-tuple-element.13), channel_id=1, source_target_pairs={{8,0},{16,8},{24,16},{32,24},{40,32},{48,40},{56,48},{64,56},{72,6... | collective-permute-start | bytes 12320 | tf_op jit(solution)/shard_map/ppermute | solution.py:23
  137.8 1.9 %collective-permute-start.2 = (bf16[2,1,1026]{2,1,0:T(2,128)(2,1)S(1)}, bf16[2,1,1026]{2,1,0:T(2,128)(2,1)S(1)}, u32[]{:S(2)}, u32[]{:S(2)}) collective-permute-start(bf16[2,1,1026]{2,1,0:T(2,128)(2,1)S(1)} %get-tuple-element.12), channel_id=1, source_target_pairs={{0,8},{8,16},{16,24},{24,32},{32,40},{40,48},{48,56},{56,64},{64,7... | collective-permute-start | bytes 12320 | tf_op jit(solution)/shard_map/ppermute | solution.py:22
  139.9 5.3 %collective-permute-done.2 = bf16[2,1,1026]{2,1,0:T(2,128)(2,1)S(1)} collective-permute-done((bf16[2,1,1026]{2,1,0:T(2,128)(2,1)S(1)}, bf16[2,1,1026]{2,1,0:T(2,128)(2,1)S(1)}, u32[]{:S(2)}, u32[]{:S(2)}) %collective-permute-start.2) | collective-permute-done | bytes 4136 | tf_op jit(solution)/shard_map/ppermute | solution.py:22
  145.9 3.8 %collective-permute-start.5 = (f32[16,1]{1,0:T(8,128)S(1)}, f32[16,1]{1,0:T(8,128)S(1)}, u32[]{:S(2)}, u32[]{:S(2)}) collective-permute-start(f32[16,1]{1,0:T(8,128)S(1)} %get-tuple-element.16), channel_id=1, source_target_pairs={{1,0},{2,1},{3,2},{4,3},{5,4},{6,5},{7,6},{0,7},{9,8},{10,9},{11,1... | collective-permute-start | bytes 200 | tf_op jit(solution)/shard_map/ppermute | solution.py:23
  149.7 1.6 collective-permute-done.4
  151.4 1.9 %collective-permute-start.7 = (f32[1,1026]{1,0:T(1,128)S(1)}, f32[1,1026]{1,0:T(1,128)S(1)}, u32[]{:S(2)}, u32[]{:S(2)}) collective-permute-start(f32[1,1026]{1,0:T(1,128)S(1)} %get-tuple-element.11), channel_id=1, source_target_pairs={{0,8},{8,16},{16,24},{24,32},{32,40},{40,48},{48,56},{56,64},{64,7... | collective-permute-start | bytes 12320 | tf_op jit(solution)/shard_map/ppermute | solution.py:22
  153.4 6.0 %collective-permute-start.6 = (f32[1,1026]{1,0:T(1,128)S(1)}, f32[1,1026]{1,0:T(1,128)S(1)}, u32[]{:S(2)}, u32[]{:S(2)}) collective-permute-start(f32[1,1026]{1,0:T(1,128)S(1)} %get-tuple-element.10), channel_id=1, source_target_pairs={{8,0},{16,8},{24,16},{32,24},{40,32},{48,40},{56,48},{64,56},{72,6... | collective-permute-start | bytes 12320 | tf_op jit(solution)/shard_map/ppermute | solution.py:23
  159.4 1.3 collective-permute-done.6
  161.0 1.4 collective-permute-start.8
  162.4 2.8 %collective-permute-start.9 = (f32[16,1]{1,0:T(8,128)S(1)}, f32[16,1]{1,0:T(8,128)S(1)}, u32[]{:S(2)}, u32[]{:S(2)}) collective-permute-start(f32[16,1]{1,0:T(8,128)S(1)} %get-tuple-element.14), channel_id=1, source_target_pairs={{1,0},{2,1},{3,2},{4,3},{5,4},{6,5},{7,6},{0,7},{9,8},{10,9},{11,1... | collective-permute-start | bytes 200 | tf_op jit(solution)/shard_map/ppermute | solution.py:23
  165.3 1.5 collective-permute-done.8
  166.9 1.9 %collective-permute-start.11 = (f32[1,1026]{1,0:T(1,128)S(1)}, f32[1,1026]{1,0:T(1,128)S(1)}, u32[]{:S(2)}, u32[]{:S(2)}) collective-permute-start(f32[1,1026]{1,0:T(1,128)S(1)} %get-tuple-element.9), channel_id=1, source_target_pairs={{0,8},{8,16},{16,24},{24,32},{32,40},{40,48},{48,56},{56,64},{64,7... | collective-permute-start | bytes 12320 | tf_op jit(solution)/shard_map/ppermute | solution.py:22
  168.9 6.0 %collective-permute-start.10 = (f32[1,1026]{1,0:T(1,128)S(1)}, f32[1,1026]{1,0:T(1,128)S(1)}, u32[]{:S(2)}, u32[]{:S(2)}) collective-permute-start(f32[1,1026]{1,0:T(1,128)S(1)} %get-tuple-element.8), channel_id=1, source_target_pairs={{8,0},{16,8},{24,16},{32,24},{40,32},{48,40},{56,48},{64,56},{72,6... | collective-permute-start | bytes 12320 | tf_op jit(solution)/shard_map/ppermute | solution.py:23
  174.9 1.3 collective-permute-done.10
  176.2 0.8 fusion.16
  (38 shorter events, 3.4 us)
Async XLA Ops:
  7.2 95.3 %all-gather.2.cloned.1.call-start = ((), (), s32[]{:S(2)}) async-start(), calls=%async_computation | async-start | bytes 13369344 | tf_op jit(solution)/shard_map/all_gather | solution.py:72
  128.8 48.3 %copy-start = (bf16[6,16,1024]{2,1,0:T(8,128)(2,1)}, bf16[6,16,1024]{2,1,0:T(8,128)(2,1)S(1)}, u32[]{:S(2)}) copy-start(bf16[6,16,1024]{2,1,0:T(8,128)(2,1)S(1)} %convert_element_type.31) | copy-start | bytes 589828
  128.8 5.8 %collective-permute-start = (bf16[2,16,1]{2,1,0:T(8,128)(2,1)S(1)}, bf16[2,16,1]{2,1,0:T(8,128)(2,1)S(1)}, u32[]{:S(2)}, u32[]{:S(2)}) collective-permute-start(bf16[2,16,1]{2,1,0:T(8,128)(2,1)S(1)} %get-tuple-element.7), channel_id=1, source_target_pairs={{0,1},{1,2},{2,3},{3,4},{4,5},{5,6},{6,7},{7,0},{8,9},{9,10},{10,1... | collective-permute-start | bytes 200 | tf_op jit(solution)/shard_map/ppermute | solution.py:22
  130.6 4.0 %collective-permute-start.1 = (bf16[2,16,1]{2,1,0:T(8,128)(2,1)S(1)}, bf16[2,16,1]{2,1,0:T(8,128)(2,1)S(1)}, u32[]{:S(2)}, u32[]{:S(2)}) collective-permute-start(bf16[2,16,1]{2,1,0:T(8,128)(2,1)S(1)} %get-tuple-element.6), channel_id=1, source_target_pairs={{1,0},{2,1},{3,2},{4,3},{5,4},{6,5},{7,6},{0,7},{9,8},{10,9},{11,1... | collective-permute-start | bytes 200 | tf_op jit(solution)/shard_map/ppermute | solution.py:23
  134.8 5.1 %collective-permute-start.3 = (bf16[2,1,1026]{2,1,0:T(2,128)(2,1)S(1)}, bf16[2,1,1026]{2,1,0:T(2,128)(2,1)S(1)}, u32[]{:S(2)}, u32[]{:S(2)}) collective-permute-start(bf16[2,1,1026]{2,1,0:T(2,128)(2,1)S(1)} %get-tuple-element.13), channel_id=1, source_target_pairs={{8,0},{16,8},{24,16},{32,24},{40,32},{48,40},{56,48},{64,56},{72,6... | collective-permute-start | bytes 12320 | tf_op jit(solution)/shard_map/ppermute | solution.py:23
  137.8 7.4 %collective-permute-start.2 = (bf16[2,1,1026]{2,1,0:T(2,128)(2,1)S(1)}, bf16[2,1,1026]{2,1,0:T(2,128)(2,1)S(1)}, u32[]{:S(2)}, u32[]{:S(2)}) collective-permute-start(bf16[2,1,1026]{2,1,0:T(2,128)(2,1)S(1)} %get-tuple-element.12), channel_id=1, source_target_pairs={{0,8},{8,16},{16,24},{24,32},{32,40},{40,48},{48,56},{56,64},{64,7... | collective-permute-start | bytes 12320 | tf_op jit(solution)/shard_map/ppermute | solution.py:22
  145.6 5.8 %collective-permute-start.4 = (f32[16,1]{1,0:T(8,128)S(1)}, f32[16,1]{1,0:T(8,128)S(1)}, u32[]{:S(2)}, u32[]{:S(2)}) collective-permute-start(f32[16,1]{1,0:T(8,128)S(1)} %get-tuple-element.17), channel_id=1, source_target_pairs={{0,1},{1,2},{2,3},{3,4},{4,5},{5,6},{6,7},{7,0},{8,9},{9,10},{10,1... | collective-permute-start | bytes 200 | tf_op jit(solution)/shard_map/ppermute | solution.py:22
  145.9 5.4 %collective-permute-start.5 = (f32[16,1]{1,0:T(8,128)S(1)}, f32[16,1]{1,0:T(8,128)S(1)}, u32[]{:S(2)}, u32[]{:S(2)}) collective-permute-start(f32[16,1]{1,0:T(8,128)S(1)} %get-tuple-element.16), channel_id=1, source_target_pairs={{1,0},{2,1},{3,2},{4,3},{5,4},{6,5},{7,6},{0,7},{9,8},{10,9},{11,1... | collective-permute-start | bytes 200 | tf_op jit(solution)/shard_map/ppermute | solution.py:23
  151.4 8.0 %collective-permute-start.7 = (f32[1,1026]{1,0:T(1,128)S(1)}, f32[1,1026]{1,0:T(1,128)S(1)}, u32[]{:S(2)}, u32[]{:S(2)}) collective-permute-start(f32[1,1026]{1,0:T(1,128)S(1)} %get-tuple-element.11), channel_id=1, source_target_pairs={{0,8},{8,16},{16,24},{24,32},{32,40},{40,48},{48,56},{56,64},{64,7... | collective-permute-start | bytes 12320 | tf_op jit(solution)/shard_map/ppermute | solution.py:22
  153.4 7.4 %collective-permute-start.6 = (f32[1,1026]{1,0:T(1,128)S(1)}, f32[1,1026]{1,0:T(1,128)S(1)}, u32[]{:S(2)}, u32[]{:S(2)}) collective-permute-start(f32[1,1026]{1,0:T(1,128)S(1)} %get-tuple-element.10), channel_id=1, source_target_pairs={{8,0},{16,8},{24,16},{32,24},{40,32},{48,40},{56,48},{64,56},{72,6... | collective-permute-start | bytes 12320 | tf_op jit(solution)/shard_map/ppermute | solution.py:23
  161.0 5.8 %collective-permute-start.8 = (f32[16,1]{1,0:T(8,128)S(1)}, f32[16,1]{1,0:T(8,128)S(1)}, u32[]{:S(2)}, u32[]{:S(2)}) collective-permute-start(f32[16,1]{1,0:T(8,128)S(1)} %get-tuple-element.15), channel_id=1, source_target_pairs={{0,1},{1,2},{2,3},{3,4},{4,5},{5,6},{6,7},{7,0},{8,9},{9,10},{10,1... | collective-permute-start | bytes 200 | tf_op jit(solution)/shard_map/ppermute | solution.py:22
  162.4 4.4 %collective-permute-start.9 = (f32[16,1]{1,0:T(8,128)S(1)}, f32[16,1]{1,0:T(8,128)S(1)}, u32[]{:S(2)}, u32[]{:S(2)}) collective-permute-start(f32[16,1]{1,0:T(8,128)S(1)} %get-tuple-element.14), channel_id=1, source_target_pairs={{1,0},{2,1},{3,2},{4,3},{5,4},{6,5},{7,6},{0,7},{9,8},{10,9},{11,1... | collective-permute-start | bytes 200 | tf_op jit(solution)/shard_map/ppermute | solution.py:23
  166.9 8.0 %collective-permute-start.11 = (f32[1,1026]{1,0:T(1,128)S(1)}, f32[1,1026]{1,0:T(1,128)S(1)}, u32[]{:S(2)}, u32[]{:S(2)}) collective-permute-start(f32[1,1026]{1,0:T(1,128)S(1)} %get-tuple-element.9), channel_id=1, source_target_pairs={{0,8},{8,16},{16,24},{24,32},{32,40},{40,48},{48,56},{56,64},{64,7... | collective-permute-start | bytes 12320 | tf_op jit(solution)/shard_map/ppermute | solution.py:22
  168.9 7.4 %collective-permute-start.10 = (f32[1,1026]{1,0:T(1,128)S(1)}, f32[1,1026]{1,0:T(1,128)S(1)}, u32[]{:S(2)}, u32[]{:S(2)}) collective-permute-start(f32[1,1026]{1,0:T(1,128)S(1)} %get-tuple-element.8), channel_id=1, source_target_pairs={{8,0},{16,8},{24,16},{32,24},{40,32},{48,40},{56,48},{64,56},{72,6... | collective-permute-start | bytes 12320 | tf_op jit(solution)/shard_map/ppermute | solution.py:23
Sparse Core Ops, SparseCore 0:
  10.5 91.9 all-gather.1
where the time goes:
time: 187 us; the launch traced here: 184 us
  waiting for transfers between devices  106 us (57%)
  starting transfers between devices  33.5 us (18%)
  local copies, waits for them, and re-layouts  21.5 us (11%)
  between operations  14.9 us (8%)
  matrix products  5.64 us (3%)
  other arithmetic  2.79 us (1%)
    all_gather x1, waiting for transfers between devices, on_device(): shard_rows = lax.all_gather(src_tiles, 'band', axis=1, tiled=True)  92.4 us
    ppermute x6, starting transfers between devices, extended_2(): after = lax.ppermute(first, axis, down)  24.4 us
    all_gather x1, local copies, waits for them, and re-layouts, on_device(): shard_rows = lax.all_gather(src_tiles, 'band', axis=1, tiled=True)  13.8 us
    ppermute x6, waiting for transfers between devices, extended_2(): before = lax.ppermute(last, axis, up)  9.89 us
    ppermute x6, starting transfers between devices, extended_2(): before = lax.ppermute(last, axis, up)  9.05 us
    gather x1, local copies, waits for them, and re-layouts, on_device(): fetched = jnp.take(shard_rows, local_index, axis=1)  6.59 us
    dot_general x1, matrix products, on_device(): jnp.einsum('cek,ekn->cen', picked, ent_weight, preferred_element_type=jnp...  4.74 us
  transfers between devices with their start and end apart: 13, of which 7 were waited for; matrix products, arithmetic and copies ran while one was open for 1% of the time, Pallas kernels for 0%

commit v1 on v0

v1 whole, which is shorter than its diff:
```python
import functools
import math

import jax
import jax.numpy as jnp
from jax import lax
from jax.experimental import pallas as pl
from jax.experimental.pallas import tpu as pltpu
from jax.sharding import PartitionSpec as P

BW = 128
R_DEV = 16
C_DEV = 1024
BLK_ROW = C_DEV // BW
LAT_START = 0.5
HALO = 3
EXT = 24
CHUNK = 32

VM = pl.BlockSpec(memory_space=pltpu.VMEM)
SM = pl.BlockSpec(memory_space=pltpu.SMEM)


def dot(a, b):
    return jnp.dot(a, b, preferred_element_type=jnp.float32)


def dot_nt(a, b):
    return lax.dot_general(a, b, (((1,), (1,)), ((), ())), preferred_element_type=jnp.float32)


def iota(shape, dim):
    return lax.broadcasted_iota(jnp.int32, shape, dim)


def as_bf16(flags):
    return flags.astype(jnp.float32).astype(jnp.bfloat16)


def route_kernel(per_band, tiles_held, tile_ref, req_ref, pos_ref):
    tile = tile_ref[...]
    slots = tile.shape[1]
    bands = req_ref.shape[0]
    owner = tile // per_band
    local = tile % tiles_held
    hit = owner == iota((bands, slots), 0)
    before = as_bf16(iota((slots, slots), 0) < iota((slots, slots), 1))
    earlier = dot(as_bf16(hit), before)
    rank = jnp.sum(jnp.where(hit, earlier, 0.0), axis=0, keepdims=True).astype(jnp.int32)
    place = as_bf16(rank == iota((128, slots), 0))
    high = jnp.where(hit, (local // 16).astype(jnp.float32), 0.0).astype(jnp.bfloat16)
    low = jnp.where(hit, (local % 16).astype(jnp.float32), 0.0).astype(jnp.bfloat16)
    req_ref[...] = (dot_nt(high, place) * 16.0 + dot_nt(low, place)).astype(jnp.int32)
    pos_ref[...] = jnp.broadcast_to(owner * (slots // bands) + rank, (8, slots))


def pick_kernel(req_ref, src_ref, send_ref):
    channels, tiles, _ = src_ref.shape
    bands = req_ref.shape[0]
    each = send_ref.shape[1] // channels
    asked = jnp.transpose(req_ref[...].astype(jnp.float32)).astype(jnp.int32)
    cell = iota((each, tiles), 1)
    onehot = jnp.concatenate([as_bf16(asked[:each, d : d + 1] == cell) for d in range(bands)], axis=0)
    for c in range(channels):
        got = dot(onehot, src_ref[c]).astype(jnp.bfloat16)
        send_ref[:, c * each : (c + 1) * each, :] = got.reshape(bands, each, 128)


def remap_kernel(
    row_stride, place_ref, live_ref, recv_ref, pos_ref, block_ref, weight_hbm,
    out_ref, wind_ref, a_ref, b_ref, weight, xs, term, sems,
):
    bands = recv_ref.shape[0]
    slots = weight.shape[0]
    channels = out_ref.shape[0]
    each = slots // bands
    copies = []
    for g in range(slots // CHUNK):
        part = pl.ds(g * CHUNK, CHUNK)
        copies.append(pltpu.make_async_copy(weight_hbm.at[part], weight.at[part], sems.at[g]))
        copies[-1].start()
    where_from = jnp.transpose(pos_ref[...].astype(jnp.float32))[:, :1].astype(jnp.int32)
    perm = as_bf16(where_from == iota((slots, slots), 1))
    for c in range(channels):
        arrived = recv_ref[:, c * each : (c + 1) * each, :].reshape(slots, 128)
        xs[pl.ds(c, slots, stride=8), :] = dot(perm, arrived)
    upper = iota((16, 128), 0) < 8
    for g in range(slots // CHUNK):
        copies[g].wait()
        for s in range(g * CHUNK, (g + 1) * CHUNK, 2):
            x = xs[s * 8 : s * 8 + 16, :]
            pair = jnp.concatenate([jnp.where(upper, x, 0.0), jnp.where(upper, 0.0, x)], axis=1)
            term[s * 8 : s * 8 + 16, :] = dot(pair.astype(jnp.bfloat16), weight[s : s + 2].reshape(256, 128))
    block = block_ref[...]
    target = (block % BLK_ROW) * R_DEV + (block // row_stride) % R_DEV
    live = iota((1, slots), 1) < live_ref[0]
    chosen = as_bf16((target == iota((BLK_ROW * R_DEV, slots), 0)) & live)
    winds = []
    for c in (2, 3, 0, 1, 4, 5):
        rest = term[pl.ds(c, slots, stride=8), :]
        total = None
        for _ in range(3):
            part = rest.astype(jnp.bfloat16)
            rest = rest - part.astype(jnp.float32)
            share = dot(chosen, part)
            total = share if total is None else total + share
        field = jnp.concatenate([total[j * R_DEV : (j + 1) * R_DEV] for j in range(BLK_ROW)], axis=1)
        rounded = field.astype(jnp.bfloat16)
        out_ref[c] = rounded
        if c in (2, 3):
            wind_ref[c - 2] = rounded
            winds.append(rounded.astype(jnp.float32))
        if c == 3:
            pad = jnp.zeros((8 - 2 * HALO, C_DEV), jnp.float32)
            first = jnp.concatenate([w[:HALO] for w in winds] + [pad], axis=0)
            last = jnp.concatenate([w[R_DEV - HALO :] for w in winds] + [pad], axis=0)
            odd = place_ref[0] > 0
            a_ref[...] = jnp.where(odd, first, last).astype(jnp.bfloat16)
            b_ref[...] = jnp.where(odd, last, first).astype(jnp.bfloat16)


def extend_kernel(place_ref, wind_ref, from_a_ref, from_b_ref, ext_ref, a_ref, b_ref):
    from_a = from_a_ref[...].astype(jnp.float32)
    from_b = from_b_ref[...].astype(jnp.float32)
    odd = place_ref[0] > 0
    above = jnp.where(odd, from_a, from_b)
    below = jnp.where(odd, from_b, from_a)
    pad = jnp.zeros((EXT - R_DEV - 2 * HALO, C_DEV), jnp.float32)
    left, right = [], []
    for w in range(2):
        rows = slice(w * HALO, (w + 1) * HALO)
        full = jnp.concatenate([above[rows], wind_ref[w].astype(jnp.float32), below[rows], pad], axis=0)
        ext_ref[w] = full
        left.append(full[:, :128])
        right.append(full[:, C_DEV - 128 :])
    left = jnp.concatenate(left, axis=0)
    right = jnp.concatenate(right, axis=0)
    odd = place_ref[1] > 0
    a_ref[...] = jnp.where(odd, left, right).astype(jnp.bfloat16)
    b_ref[...] = jnp.where(odd, right, left).astype(jnp.bfloat16)


def smooth(x):
    rows, columns = x.shape
    x = 2.0 * x + (pltpu.roll(x, 1, 0) + pltpu.roll(x, rows - 1, 0))
    x = 2.0 * x + (pltpu.roll(x, 1, 1) + pltpu.roll(x, columns - 1, 1))
    return x * (1.0 / 16.0)


def smooth_kernel(grid_step, all_rows, place_ref, ext_ref, from_a_ref, from_b_ref, out_ref):
    from_a = from_a_ref[...].astype(jnp.float32)
    from_b = from_b_ref[...].astype(jnp.float32)
    odd = place_ref[1] > 0
    left = jnp.where(odd, from_a, from_b)
    right = jnp.where(odd, from_b, from_a)
    east, north = (
        jnp.concatenate([left[w * EXT : (w + 1) * EXT], ext_ref[w], right[w * EXT : (w + 1) * EXT]], axis=1)
        for w in range(2)
    )
    rows, columns = east.shape
    row = place_ref[2] - HALO + iota((rows, 128), 0)
    inside = jnp.tile((row >= 0) & (row < all_rows), (1, columns // 128))
    cosine = jnp.tile(jnp.cos(LAT_START + (row.astype(jnp.float32) + 0.5) * grid_step), (1, columns // 128))
    scaled = east * cosine
    along = pltpu.roll(north, columns - 1, 1) - pltpu.roll(north, 1, 1)
    across = pltpu.roll(scaled, rows - 1, 0) - pltpu.roll(scaled, 1, 0)
    field = jnp.where(inside, 0.5 * (along - across) / cosine, 0.0)
    field = jnp.where(inside, smooth(field), 0.0)
    field = smooth(field)
    out_ref[...] = field[HALO : HALO + R_DEV, 128 : 128 + C_DEV]


def call(kernel, outs, ins, scratch=(), vmem=None):
    return pl.pallas_call(
        kernel,
        out_shape=outs,
        in_specs=ins,
        out_specs=jax.tree.map(lambda _: VM, outs),
        scratch_shapes=scratch,
        compiler_params=pltpu.CompilerParams(vmem_limit_bytes=vmem),
    )


def on_device(src_tiles, ent_tile, ent_block, ent_weight, live_count):
    bands, lons = lax.axis_size("band"), lax.axis_size("lon")
    band, lon = lax.axis_index("band"), lax.axis_index("lon")
    channels, tiles, pixels = src_tiles.shape
    slots = ent_tile.shape[0]
    each = slots // bands
    shape = jax.ShapeDtypeStruct
    bf16, f32, i32 = jnp.bfloat16, jnp.float32, jnp.int32
    place = jnp.stack([band % 2, lon % 2, band * R_DEV]).astype(i32)

    req, pos = call(
        functools.partial(route_kernel, lons * tiles, tiles),
        (shape((bands, 128), i32), shape((8, slots), i32)),
        [VM],
    )(ent_tile.reshape(1, slots))
    asked = lax.all_to_all(req, "band", 0, 0, tiled=True)
    send = call(pick_kernel, shape((bands, channels * each, pixels), bf16), [VM, VM], vmem=16 << 20)(asked, src_tiles)
    recv = lax.all_to_all(send, "band", 0, 0, tiled=True)

    rows = shape((8, C_DEV), bf16)
    remapped, wind, to_a, to_b = call(
        functools.partial(remap_kernel, BLK_ROW * lons),
        (shape((channels, R_DEV, C_DEV), bf16), shape((2, R_DEV, C_DEV), bf16), rows, rows),
        [SM, SM, VM, VM, VM, pl.BlockSpec(memory_space=pl.ANY)],
        [
            pltpu.VMEM((slots, pixels, BW), bf16),
            pltpu.VMEM((slots * 8, pixels), f32),
            pltpu.VMEM((slots * 8, BW), f32),
            pltpu.SemaphoreType.DMA((slots // CHUNK,)),
        ],
        vmem=32 << 20,
    )(place, live_count, recv, pos, ent_block.reshape(1, slots), ent_weight)

    pairs_a = lambda size: [(i, i ^ 1) for i in range(size)]
    pairs_b = [(i, i + 1 if i % 2 else i - 1) for i in range(1, bands - 1)]
    ring_b = [(i, (i + 1 if i % 2 else i - 1) % lons) for i in range(lons)]
    from_b = lax.ppermute(to_b, "band", pairs_b)
    from_a = lax.ppermute(to_a, "band", pairs_a(bands))
    edge = shape((2 * EXT, 128), bf16)
    ext, to_a, to_b = call(extend_kernel, (shape((2, EXT, C_DEV), f32), edge, edge), [SM, VM, VM, VM])(
        place, wind, from_a, from_b
    )
    from_b = lax.ppermute(to_b, "lon", ring_b)
    from_a = lax.ppermute(to_a, "lon", pairs_a(lons))
    smoothed = call(
        functools.partial(smooth_kernel, 2.0 * math.pi / (C_DEV * lons), R_DEV * bands),
        shape((R_DEV, C_DEV), f32),
        [SM, VM, VM, VM],
    )(place, ext, from_a, from_b)
    return remapped, smoothed


def solution(mesh):
    in_specs = (
        P(None, ("band", "lon"), None),
        P(("band", "lon")),
        P(("band", "lon")),
        P(("band", "lon"), None, None),
        P(("band", "lon")),
    )
    out_specs = (P(None, "band", "lon"), P("band", "lon"))
    return jax.shard_map(on_device, mesh=mesh, in_specs=in_specs, out_specs=out_specs, check_vma=False)
```

time: 187 us -> 63.7 us (0.34)
  the two profiles are of different devices: /device:TPU:2 before, /device:TPU:1 now
where the time goes in v1:
time: 63.7 us; the launch traced here: 63.2 us
  waiting for transfers between devices  16.1 us (25%)
  blocking collectives  15.4 us (24%)
  Pallas kernels  11.6 us (18%)
  starting transfers between devices  11.1 us (17%)
  local copies, waits for them, and re-layouts  7.71 us (12%)
  between operations  1.34 us (2%)
    all_to_all x1, blocking collectives, on_device(): asked = lax.all_to_all(req, 'band', 0, 0, tiled=True)  15.4 us
    all_to_all x1, waiting for transfers between devices, on_device(): recv = lax.all_to_all(send, 'band', 0, 0, tiled=True)  9.4 us
    unnamed x20, local copies, waits for them, and re-layouts  7.71 us
    pallas_call x1, Pallas kernels, on_device(): call(functools.partial(remap_kernel, BLK_ROW * lons), (shape((channels, R...  4.95 us
    ppermute x1, waiting for transfers between devices, on_device(): from_b = lax.ppermute(to_b, 'band', pairs_b)  4.18 us
    all_to_all x1, starting transfers between devices, on_device(): recv = lax.all_to_all(send, 'band', 0, 0, tiled=True)  4.01 us
    ppermute x1, waiting for transfers between devices, on_device(): from_b = lax.ppermute(to_b, 'lon', ring_b)  2.49 us
    ppermute x1, starting transfers between devices, on_device(): from_b = lax.ppermute(to_b, 'lon', ring_b)  2.37 us
  transfers between devices with their start and end apart: 5, of which 3 were waited for; matrix products, arithmetic and copies ran while one was open for 0% of the time, Pallas kernels for 0%

profile of v1, /device:TPU:1, one launch (start us, length us, event | category | flops | bytes accessed | tf_op | source)
XLA Modules:
  0.0 63.2 jit_solution(13023120149595639134)
XLA Ops:
  0.6 1.6 %shard_map.68 = (s32[16,128]{1,0:T(8,128)}, s32[8,256]{1,0:T(8,128)}) custom-call(s32[1,256]{1,0:T(1,128)} %bitcast.12), custom_call_target="tpu_custom_call" | custom-call | tf_op jit(solution)/shard_map/pallas_call | solution.py:194
  2.2 15.4 %all_to_all.16 = s32[16,1,128]{2,1,0:T(1,128)S(1)} all-to-all(s32[16,1,128]{2,1,0:T(1,128)} %bitcast.11), channel_id=1, replica_groups=mesh['band'=16,'lon'=8] {'band'}, dimensions={0} | all-to-all | bytes 16384 | tf_op jit(solution)/shard_map/all_to_all | solution.py:199
  17.6 1.1 %copy-done.1 = bf16[6,512,128]{2,1,0:T(8,128)(2,1)S(1)} copy-done((bf16[6,512,128]{2,1,0:T(8,128)(2,1)S(1)}, bf16[6,512,128]{2,1,0:T(8,128)(2,1)}, u32[]{:S(2)}) %copy-start.1) | copy-done | bytes 786456
  18.7 1.4 %shard_map.69 = bf16[16,96,128]{2,1,0:T(8,128)(2,1)} custom-call(s32[16,128]{1,0:T(8,128)S(1)} %bitcast.9, bf16[6,512,128]{2,1,0:T(8,128)(2,1)S(1)} %copy-done.1), custom_call_target="tpu_custom_call" | custom-call | tf_op jit(solution)/shard_map/pallas_call | solution.py:200
  20.2 4.0 %all-to-all-start.1 = ((bf16[16,96,128]{2,1,0:T(8,128)(2,1)}), bf16[16,96,128]{2,1,0:T(8,128)(2,1)S(1)}, u32[]{:S(2)}, u32[]{:S(2)}) async-start(bf16[16,96,128]{2,1,0:T(8,128)(2,1)} %shard_map.69), calls=%async_computation.1 | async-start | bytes 786432 | tf_op jit(solution)/shard_map/all_to_all | solution.py:201
  24.8 0.1 pad_add_fusion.place_ref
  24.9 9.4 %all-to-all-done.1.recv_ref = bf16[16,96,128]{2,1,0:T(8,128)(2,1)S(1)} async-done(((bf16[16,96,128]{2,1,0:T(8,128)(2,1)}), bf16[16,96,128]{2,1,0:T(8,128)(2,1)S(1)}, u32[]{:S(2)}, u32[]{:S(2)}) %all-to-all-start.1) | async-done | bytes 393248 | tf_op jit(solution)/shard_map/all_to_all | solution.py:201
  34.3 3.4 %copy-done = bf16[256,128,128]{2,1,0:T(8,128)(2,1)S(1)} copy-done((bf16[256,128,128]{2,1,0:T(8,128)(2,1)S(1)}, bf16[256,128,128]{2,1,0:T(8,128)(2,1)}, u32[]{:S(2)}) %copy-start) | copy-done | bytes 8388632
  37.7 0.7 %copy-done.4 = s32[8,256]{1,0:T(8,128)S(1)} copy-done((s32[8,256]{1,0:T(8,128)S(1)}, s32[8,256]{1,0:T(8,128)}, u32[]{:S(2)}) %copy-start.4) | copy-done | bytes 8216
  38.4 0.7 %copy-done.5 = s32[256]{0:T(256)S(1)} copy-done((s32[256]{0:T(256)S(1)}, s32[256]{0:T(256)}, u32[]{:S(2)}) %copy-start.5) | copy-done | bytes 1048
  39.1 5.0 %shard_map.70 = (bf16[6,16,1024]{2,1,0:T(8,128)(2,1)}, bf16[2,16,1024]{2,1,0:T(8,128)(2,1)S(1)}, bf16[8,1024]{1,0:T(8,128)(2,1)S(1)}, bf16[8,1024]{1,0:T(8,128)(2,1)S(1)}) custom-call(s32[3]{0:T(128)S(1)} %pad_add_fusion.place_ref, s32[1]{0:T(128)S(6)} %copy.8.live_ref, bf16[16,96,128]{2,1,0:T(8,128)(2,1)S(1)} %all-to-all-done.1.recv_ref, ...), custom_call_target="tpu_custom_call" | custom-call | tf_op jit(solution)/shard_map/pallas_call | solution.py:204
  44.0 0.0 copy-start.2
  44.0 0.6 copy-done.2
  44.7 0.8 %collective-permute-start = (bf16[8,1024]{1,0:T(8,128)(2,1)S(1)}, bf16[8,1024]{1,0:T(8,128)(2,1)S(1)}, u32[]{:S(2)}, u32[]{:S(2)}) collective-permute-start(bf16[8,1024]{1,0:T(8,128)(2,1)S(1)} %get-tuple-element.15), channel_id=1, source_target_pairs={{0,8},{8,0},{16,24},{24,16},{32,40},{40,32},{48,56},{56,48},{64,72... | collective-permute-start | bytes 49160 | tf_op jit(solution)/shard_map/ppermute | solution.py:221
  45.4 2.3 %collective-permute-start.1 = (bf16[8,1024]{1,0:T(8,128)(2,1)S(1)}, bf16[8,1024]{1,0:T(8,128)(2,1)S(1)}, u32[]{:S(2)}, u32[]{:S(2)}) collective-permute-start(bf16[8,1024]{1,0:T(8,128)(2,1)S(1)} %get-tuple-element.16), channel_id=1, source_target_pairs={{8,16},{16,8},{24,32},{32,24},{40,48},{48,40},{56,64},{64,56},{72,... | collective-permute-start | bytes 49160 | tf_op jit(solution)/shard_map/ppermute | solution.py:220
  47.8 0.0 collective-permute-done.from_a_ref
  47.8 4.2 %collective-permute-done.1.from_b_ref = bf16[8,1024]{1,0:T(8,128)(2,1)S(1)} collective-permute-done((bf16[8,1024]{1,0:T(8,128)(2,1)S(1)}, bf16[8,1024]{1,0:T(8,128)(2,1)S(1)}, u32[]{:S(2)}, u32[]{:S(2)}) %collective-permute-start.1) | collective-permute-done | bytes 16416 | tf_op jit(solution)/shard_map/ppermute | solution.py:220
  52.0 0.6 copy-done.7
  52.6 1.6 %shard_map.71 = (f32[2,24,1024]{2,1,0:T(8,128)}, bf16[48,128]{1,0:T(8,128)(2,1)}, bf16[48,128]{1,0:T(8,128)(2,1)}) custom-call(s32[3]{0:T(128)} %copy-done.3, bf16[2,16,1024]{2,1,0:T(8,128)(2,1)} %copy-done.2, bf16[8,1024]{1,0:T(8,128)(2,1)} %copy-done.6, bf16[8,1024]{1,0:T(8,128)(2,1)} %copy-done.7), custom_call_target="tpu_custom_call" | custom-call | tf_op jit(solution)/shard_map/pallas_call | solution.py:223
  54.2 1.6 %collective-permute-start.2 = (bf16[48,128]{1,0:T(8,128)(2,1)}, bf16[48,128]{1,0:T(8,128)(2,1)S(1)}, u32[]{:S(2)}, u32[]{:S(2)}) collective-permute-start(bf16[48,128]{1,0:T(8,128)(2,1)} %get-tuple-element.18), channel_id=1, source_target_pairs={{0,1},{1,0},{2,3},{3,2},{4,5},{5,4},{6,7},{7,6},{8,9},{9,8},{10,11... | collective-permute-start | bytes 36872 | tf_op jit(solution)/shard_map/ppermute | solution.py:227
  55.8 2.4 %collective-permute-start.3 = (bf16[48,128]{1,0:T(8,128)(2,1)}, bf16[48,128]{1,0:T(8,128)(2,1)S(1)}, u32[]{:S(2)}, u32[]{:S(2)}) collective-permute-start(bf16[48,128]{1,0:T(8,128)(2,1)} %get-tuple-element.19), channel_id=1, source_target_pairs={{0,7},{1,2},{2,1},{3,4},{4,3},{5,6},{6,5},{7,0},{8,15},{9,10},{10,... | collective-permute-start | bytes 36872 | tf_op jit(solution)/shard_map/ppermute | solution.py:226
  58.2 2.5 %collective-permute-done.3.from_b_ref = bf16[48,128]{1,0:T(8,128)(2,1)S(1)} collective-permute-done((bf16[48,128]{1,0:T(8,128)(2,1)}, bf16[48,128]{1,0:T(8,128)(2,1)S(1)}, u32[]{:S(2)}, u32[]{:S(2)}) %collective-permute-start.3) | collective-permute-done | bytes 12320 | tf_op jit(solution)/shard_map/ppermute | solution.py:226
  60.7 0.6 copy-done.9
  61.3 2.0 %shard_map.72 = f32[16,1024]{1,0:T(8,128)} custom-call(s32[3]{0:T(128)} %copy-done.3, f32[2,24,1024]{2,1,0:T(8,128)} %get-tuple-element.17.ext_ref, bf16[48,128]{1,0:T(8,128)(2,1)} %copy-done.8, bf16[48,128]{1,0:T(8,128)(2,1)} %copy-done.9), custom_call_target="tpu_custom_call" | custom-call | tf_op jit(solution)/shard_map/pallas_call | solution.py:228
  (13 shorter events, 0.0 us)
Async XLA Ops:
  17.6 1.1 %copy-start.1 = (bf16[6,512,128]{2,1,0:T(8,128)(2,1)S(1)}, bf16[6,512,128]{2,1,0:T(8,128)(2,1)}, u32[]{:S(2)}) copy-start(bf16[6,512,128]{2,1,0:T(8,128)(2,1)} %src_ref.1) | copy-start | bytes 2359300
  20.2 14.1 %all-to-all-start.1 = ((bf16[16,96,128]{2,1,0:T(8,128)(2,1)}), bf16[16,96,128]{2,1,0:T(8,128)(2,1)S(1)}, u32[]{:S(2)}, u32[]{:S(2)}) async-start(bf16[16,96,128]{2,1,0:T(8,128)(2,1)} %shard_map.69), calls=%async_computation.1 | async-start | bytes 786432 | tf_op jit(solution)/shard_map/all_to_all | solution.py:201
  24.9 27.1 %copy-start.3 = (s32[3]{0:T(128)}, s32[3]{0:T(128)S(1)}, u32[]{:S(2)}) copy-start(s32[3]{0:T(128)S(1)} %pad_add_fusion.place_ref) | copy-start | bytes 40
  34.3 3.4 %copy-start = (bf16[256,128,128]{2,1,0:T(8,128)(2,1)S(1)}, bf16[256,128,128]{2,1,0:T(8,128)(2,1)}, u32[]{:S(2)}) copy-start(bf16[256,128,128]{2,1,0:T(8,128)(2,1)} %weight_hbm.1) | copy-start | bytes 25165828
  37.7 0.7 %copy-start.4 = (s32[8,256]{1,0:T(8,128)S(1)}, s32[8,256]{1,0:T(8,128)}, u32[]{:S(2)}) copy-start(s32[8,256]{1,0:T(8,128)} %get-tuple-element.12.pos_ref) | copy-start | bytes 24580
  38.4 0.7 %copy-start.5 = (s32[256]{0:T(256)S(1)}, s32[256]{0:T(256)}, u32[]{:S(2)}) copy-start(s32[256]{0:T(256)} %param.7) | copy-start | bytes 3076
  44.0 0.6 copy-start.2
  44.7 3.1 %collective-permute-start = (bf16[8,1024]{1,0:T(8,128)(2,1)S(1)}, bf16[8,1024]{1,0:T(8,128)(2,1)S(1)}, u32[]{:S(2)}, u32[]{:S(2)}) collective-permute-start(bf16[8,1024]{1,0:T(8,128)(2,1)S(1)} %get-tuple-element.15), channel_id=1, source_target_pairs={{0,8},{8,0},{16,24},{24,16},{32,40},{40,32},{48,56},{56,48},{64,72... | collective-permute-start | bytes 49160 | tf_op jit(solution)/shard_map/ppermute | solution.py:221
  45.4 6.5 %collective-permute-start.1 = (bf16[8,1024]{1,0:T(8,128)(2,1)S(1)}, bf16[8,1024]{1,0:T(8,128)(2,1)S(1)}, u32[]{:S(2)}, u32[]{:S(2)}) collective-permute-start(bf16[8,1024]{1,0:T(8,128)(2,1)S(1)} %get-tuple-element.16), channel_id=1, source_target_pairs={{8,16},{16,8},{24,32},{32,24},{40,48},{48,40},{56,64},{64,56},{72,... | collective-permute-start | bytes 49160 | tf_op jit(solution)/shard_map/ppermute | solution.py:220
  47.8 4.2 %copy-start.6 = (bf16[8,1024]{1,0:T(8,128)(2,1)}, bf16[8,1024]{1,0:T(8,128)(2,1)S(1)}, u32[]{:S(2)}) copy-start(bf16[8,1024]{1,0:T(8,128)(2,1)S(1)} %collective-permute-done.from_a_ref) | copy-start | bytes 49156
  52.0 0.6 copy-start.7
  54.2 4.0 %collective-permute-start.2 = (bf16[48,128]{1,0:T(8,128)(2,1)}, bf16[48,128]{1,0:T(8,128)(2,1)S(1)}, u32[]{:S(2)}, u32[]{:S(2)}) collective-permute-start(bf16[48,128]{1,0:T(8,128)(2,1)} %get-tuple-element.18), channel_id=1, source_target_pairs={{0,1},{1,0},{2,3},{3,2},{4,5},{5,4},{6,7},{7,6},{8,9},{9,8},{10,11... | collective-permute-start | bytes 36872 | tf_op jit(solution)/shard_map/ppermute | solution.py:227
  55.8 4.9 %collective-permute-start.3 = (bf16[48,128]{1,0:T(8,128)(2,1)}, bf16[48,128]{1,0:T(8,128)(2,1)S(1)}, u32[]{:S(2)}, u32[]{:S(2)}) collective-permute-start(bf16[48,128]{1,0:T(8,128)(2,1)} %get-tuple-element.19), channel_id=1, source_target_pairs={{0,7},{1,2},{2,1},{3,4},{4,3},{5,6},{6,5},{7,0},{8,15},{9,10},{10,... | collective-permute-start | bytes 36872 | tf_op jit(solution)/shard_map/ppermute | solution.py:226
  58.2 2.5 %copy-start.8 = (bf16[48,128]{1,0:T(8,128)(2,1)}, bf16[48,128]{1,0:T(8,128)(2,1)S(1)}, u32[]{:S(2)}) copy-start(bf16[48,128]{1,0:T(8,128)(2,1)S(1)} %collective-permute-done.2.from_a_ref) | copy-start | bytes 36868
  60.7 0.6 copy-start.9

commit v2 on v1

v2 whole, which is shorter than its diff:
```python
import functools
import math

import jax
import jax.numpy as jnp
from jax import lax
from jax.experimental import pallas as pl
from jax.experimental.pallas import tpu as pltpu
from jax.sharding import PartitionSpec as P

BW = 128
R_DEV = 16
C_DEV = 1024
BLK_ROW = C_DEV // BW
LAT_START = 0.5
HALO = 3
HELD = 80
CHUNK = 16
EXT = 24

VM = pl.BlockSpec(memory_space=pltpu.VMEM)
SM = pl.BlockSpec(memory_space=pltpu.SMEM)
HB = pl.BlockSpec(memory_space=pltpu.HBM)
ANY = pl.BlockSpec(memory_space=pl.ANY)


def dot(a, b):
    return jnp.dot(a, b, preferred_element_type=jnp.float32)


def dot_nt(a, b):
    return lax.dot_general(a, b, (((1,), (1,)), ((), ())), preferred_element_type=jnp.float32)


def iota(shape, dim):
    return lax.broadcasted_iota(jnp.int32, shape, dim)


def as_bf16(flags):
    return flags.astype(jnp.float32).astype(jnp.bfloat16)


def is_odd(axis):
    return lax.axis_index(axis) % 2 == 1


def first_row():
    return lax.axis_index("band") * R_DEV


def route_kernel(per_band, tiles_held, tile_ref, req_ref, pos_ref):
    tile = tile_ref[...]
    slots = tile.shape[1]
    bands = req_ref.shape[0]
    owner = tile // per_band
    local = tile % tiles_held
    hit = owner == iota((bands, slots), 0)
    before = as_bf16(iota((slots, slots), 0) < iota((slots, slots), 1))
    earlier = dot(as_bf16(hit), before)
    rank = jnp.sum(jnp.where(hit, earlier, 0.0), axis=0, keepdims=True).astype(jnp.int32)
    place = as_bf16(rank == iota((128, slots), 0))
    high = jnp.where(hit, (local // 16).astype(jnp.float32), 0.0).astype(jnp.bfloat16)
    low = jnp.where(hit, (local % 16).astype(jnp.float32), 0.0).astype(jnp.bfloat16)
    req_ref[...] = (dot_nt(high, place) * 16.0 + dot_nt(low, place)).astype(jnp.int32)
    pos_ref[...] = jnp.broadcast_to(owner * (slots // bands) + rank, (8, slots))


def pick_kernel(req_ref, src_ref, send_hbm, picked, sems):
    channels, tiles, _ = src_ref.shape
    _, bands, each, _ = picked.shape
    asked = jnp.transpose(req_ref[...].astype(jnp.float32)).astype(jnp.int32)
    cell = iota((each, tiles), 1)
    onehot = jnp.concatenate([as_bf16(asked[:each, d : d + 1] == cell) for d in range(bands)], axis=0)
    copies = []
    for c in range(channels):
        got = dot(onehot, src_ref[c]).astype(jnp.bfloat16)
        picked[c] = got.reshape(bands, each, 128)
        copies.append(pltpu.make_async_copy(picked.at[c], send_hbm.at[:, pl.ds(c * each, each)], sems.at[c]))
        copies[-1].start()
    for copy in copies:
        copy.wait()


def start_copies(source, target, sems, first=0):
    parts = sems.shape[0]
    size = target.shape[0] // parts
    copies = []
    for g in range(parts):
        part = source.at[pl.ds(first + g * size, size)]
        copies.append(pltpu.make_async_copy(part, target.at[pl.ds(g * size, size)], sems.at[g]))
        copies[-1].start()
    return copies


def stage_kernel(after_ref, source_hbm, held_ref, sems):
    for copy in start_copies(source_hbm, held_ref, sems):
        copy.wait()


def select_kernel(row_stride, grid_step, live_ref, pos_ref, block_ref, perm_ref, chosen_ref, cosine_ref):
    slots = pos_ref.shape[1]
    where_from = jnp.transpose(pos_ref[...].astype(jnp.float32))[:, :1].astype(jnp.int32)
    perm_ref[...] = as_bf16(where_from == iota((slots, slots), 1))
    block = block_ref[...]
    target = (block % BLK_ROW) * R_DEV + (block // row_stride) % R_DEV
    live = iota((1, slots), 1) < live_ref[0]
    chosen_ref[...] = as_bf16((target == iota((BLK_ROW * R_DEV, slots), 0)) & live)
    row = first_row() - HALO + iota(cosine_ref.shape, 0)
    cosine_ref[...] = jnp.cos(LAT_START + (row.astype(jnp.float32) + 0.5) * grid_step)


def add_blocks(chosen, rest):
    total = None
    for _ in range(3):
        part = rest.astype(jnp.bfloat16)
        rest = rest - part.astype(jnp.float32)
        share = dot(chosen, part)
        total = share if total is None else total + share
    field = jnp.concatenate([total[j * R_DEV : (j + 1) * R_DEV] for j in range(BLK_ROW)], axis=1)
    return field.astype(jnp.bfloat16)


def remap_kernel(
    recv_ref, perm_ref, chosen_ref, held_ref, weight_hbm,
    wind_ref, a_ref, b_ref, others_ref, weight, xs, term, sems,
):
    bands = recv_ref.shape[0]
    slots, held = perm_ref.shape[0], held_ref.shape[0]
    channels = 2 + others_ref.shape[0]
    each = slots // bands
    chunk = (slots - held) // sems.shape[0]
    copies = start_copies(weight_hbm, weight, sems, held)
    perm = perm_ref[...]
    for c in range(channels):
        xs[c] = dot(perm, recv_ref[:, c * each : (c + 1) * each, :].reshape(slots, 128))
    row = iota((8 * channels, 128), 0) % 8
    masks = [as_bf16(row == j) for j in range(8)]
    for s in range(0, slots, 8):
        if s >= held and (s - held) % chunk == 0:
            copies[(s - held) // chunk].wait()
        x = jnp.concatenate([xs[c, s : s + 8, :] for c in range(channels)], axis=0).astype(jnp.bfloat16)
        spread = jnp.concatenate([x * mask for mask in masks], axis=1)
        eight = held_ref[s : s + 8] if s < held else weight[s - held : s - held + 8]
        got = dot(spread, eight.reshape(8 * 128, 128))
        for c in range(channels):
            target = term.at[c - 2] if c in (2, 3) else others_ref.at[c if c < 2 else c - 2]
            target[s : s + 8, :] = got[c * 8 : (c + 1) * 8]
    winds = []
    for w in range(2):
        rounded = add_blocks(chosen_ref[...], term[w])
        wind_ref[w] = rounded
        winds.append(rounded.astype(jnp.float32))
    pad = jnp.zeros((8 - 2 * HALO, C_DEV), jnp.float32)
    first = jnp.concatenate([w[:HALO] for w in winds] + [pad], axis=0)
    last = jnp.concatenate([w[R_DEV - HALO :] for w in winds] + [pad], axis=0)
    odd = is_odd("band")
    a_ref[...] = jnp.where(odd, first, last).astype(jnp.bfloat16)
    b_ref[...] = jnp.where(odd, last, first).astype(jnp.bfloat16)


def finish_kernel(chosen_ref, others_ref, wind_ref, out_ref):
    for c in range(out_ref.shape[0]):
        if c in (2, 3):
            out_ref[c] = wind_ref[c - 2]
        else:
            out_ref[c] = add_blocks(chosen_ref[...], others_ref[c if c < 2 else c - 2])


def extend_kernel(after_ref, wind_ref, from_a_ref, from_b_ref, ext_ref, a_ref, b_ref):
    from_a = from_a_ref[...].astype(jnp.float32)
    from_b = from_b_ref[...].astype(jnp.float32)
    odd = is_odd("band")
    above = jnp.where(odd, from_a, from_b)
    below = jnp.where(odd, from_b, from_a)
    pad = jnp.zeros((EXT - R_DEV - 2 * HALO, C_DEV), jnp.float32)
    left, right = [], []
    for w in range(2):
        rows = slice(w * HALO, (w + 1) * HALO)
        full = jnp.concatenate([above[rows], wind_ref[w].astype(jnp.float32), below[rows], pad], axis=0)
        ext_ref[w] = full
        left.append(full[:, :128])
        right.append(full[:, C_DEV - 128 :])
    left = jnp.concatenate(left, axis=0)
    right = jnp.concatenate(right, axis=0)
    odd = is_odd("lon")
    a_ref[...] = jnp.where(odd, left, right).astype(jnp.bfloat16)
    b_ref[...] = jnp.where(odd, right, left).astype(jnp.bfloat16)


def smooth(x):
    rows, columns = x.shape
    x = 2.0 * x + (pltpu.roll(x, 1, 0) + pltpu.roll(x, rows - 1, 0))
    x = 2.0 * x + (pltpu.roll(x, 1, 1) + pltpu.roll(x, columns - 1, 1))
    return x * (1.0 / 16.0)


def smooth_kernel(all_rows, cosine_ref, ext_ref, from_a_ref, from_b_ref, out_ref):
    from_a = from_a_ref[...].astype(jnp.float32)
    from_b = from_b_ref[...].astype(jnp.float32)
    odd = is_odd("lon")
    left = jnp.where(odd, from_a, from_b)
    right = jnp.where(odd, from_b, from_a)
    east, north = (
        jnp.concatenate([left[w * EXT : (w + 1) * EXT], ext_ref[w], right[w * EXT : (w + 1) * EXT]], axis=1)
        for w in range(2)
    )
    rows, columns = east.shape
    row = first_row() - HALO + iota((rows, 128), 0)
    inside = jnp.tile((row >= 0) & (row < all_rows), (1, columns // 128))
    cosine = cosine_ref[...]
    scaled = east * jnp.tile(cosine, (1, columns // 128))
    half = jnp.tile(0.5 / cosine, (1, columns // 128))
    along = pltpu.roll(north, columns - 1, 1) - pltpu.roll(north, 1, 1)
    across = pltpu.roll(scaled, rows - 1, 0) - pltpu.roll(scaled, 1, 0)
    field = jnp.where(inside, (along - across) * half, 0.0)
    field = jnp.where(inside, smooth(field), 0.0)
    field = smooth(field)
    out_ref[...] = field[HALO : HALO + R_DEV, 128 : 128 + C_DEV]


def call(kernel, outs, ins, scratch=(), vmem=2 << 20, cycles=0, out_specs=None):
    return pl.pallas_call(
        kernel,
        out_shape=outs,
        in_specs=ins,
        out_specs=out_specs or jax.tree.map(lambda _: VM, outs),
        scratch_shapes=scratch,
        compiler_params=pltpu.CompilerParams(vmem_limit_bytes=vmem),
        cost_estimate=pl.CostEstimate(flops=cycles, bytes_accessed=cycles, transcendentals=0) if cycles else None,
    )


def on_device(src_tiles, ent_tile, ent_block, ent_weight, live_count):
    bands, lons = lax.axis_size("band"), lax.axis_size("lon")
    channels, tiles, pixels = src_tiles.shape
    slots = ent_tile.shape[0]
    each = slots // bands
    shape = jax.ShapeDtypeStruct
    bf16, f32, i32 = jnp.bfloat16, jnp.float32, jnp.int32
    dmas = pltpu.SemaphoreType.DMA
    held = pltpu.with_memory_space_constraint

    req, pos = call(
        functools.partial(route_kernel, lons * tiles, tiles),
        (shape((bands, 128), i32), shape((8, slots), i32)),
        [VM],
    )(ent_tile.reshape(1, slots))
    asked = lax.all_to_all(req, "band", 0, 0, tiled=True)
    tiles_held = call(
        stage_kernel, pltpu.VMEM(src_tiles.shape, bf16), [ANY, HB], [dmas((channels,))], cycles=2 * src_tiles.size
    )(req, held(src_tiles, pltpu.HBM))
    perm, chosen, cosine = call(
        functools.partial(select_kernel, BLK_ROW * lons, 2.0 * math.pi / (C_DEV * lons)),
        (shape((slots, slots), bf16), shape((BLK_ROW * R_DEV, slots), bf16), shape((EXT, 128), f32)),
        [SM, VM, VM],
        cycles=slots * slots * 8,
    )(live_count, pos, ent_block.reshape(1, slots))
    send = call(
        pick_kernel,
        pltpu.HBM((bands, channels * each, pixels), bf16),
        [VM, VM],
        [pltpu.VMEM((channels, bands, each, pixels), bf16), dmas((channels,))],
        out_specs=HB,
    )(asked, held(tiles_held, pltpu.VMEM))
    recv = lax.all_to_all(send, "band", 0, 0, tiled=True)
    weight_held = call(
        stage_kernel, pltpu.VMEM((HELD, pixels, BW), bf16), [ANY, HB], [dmas((4,))], cycles=2 * HELD * pixels * BW
    )(held(send, pltpu.HBM), held(ent_weight, pltpu.HBM))

    rows = shape((8, C_DEV), bf16)
    wind, to_a, to_b, others = call(
        remap_kernel,
        (shape((2, R_DEV, C_DEV), bf16), rows, rows, shape((channels - 2, slots, BW), f32)),
        [VM, VM, VM, VM, HB],
        [
            pltpu.VMEM((slots - HELD, pixels, BW), bf16),
            pltpu.VMEM((channels, slots, pixels), f32),
            pltpu.VMEM((2, slots, BW), f32),
            dmas(((slots - HELD) // CHUNK,)),
        ],
        vmem=16 << 20,
    )(recv, perm, chosen, held(weight_held, pltpu.VMEM), held(ent_weight, pltpu.HBM))
    remapped = call(
        finish_kernel, shape((channels, R_DEV, C_DEV), bf16), [VM, VM, VM], cycles=slots * slots * 16
    )(chosen, others, wind)

    pairs_a = lambda size: [(i, i ^ 1) for i in range(size)]
    pairs_b = [(i, i + 1 if i % 2 else i - 1) for i in range(1, bands - 1)]
    ring_b = [(i, (i + 1 if i % 2 else i - 1) % lons) for i in range(lons)]
    from_a = lax.ppermute(to_a, "band", pairs_a(bands))
    from_b = lax.ppermute(to_b, "band", pairs_b)
    edge = shape((2 * EXT, 128), bf16)
    ext, to_a, to_b = call(extend_kernel, (shape((2, EXT, C_DEV), f32), edge, edge), [ANY, VM, VM, VM])(
        held(remapped, pltpu.HBM), wind, from_a, from_b
    )
    from_a = lax.ppermute(to_a, "lon", pairs_a(lons))
    from_b = lax.ppermute(to_b, "lon", ring_b)
    smoothed = call(
        functools.partial(smooth_kernel, R_DEV * bands),
        shape((R_DEV, C_DEV), f32),
        [VM, VM, VM, VM],
    )(cosine, ext, from_a, from_b)
    return remapped, smoothed


def solution(mesh):
    in_specs = (
        P(None, ("band", "lon"), None),
        P(("band", "lon")),
        P(("band", "lon")),
        P(("band", "lon"), None, None),
        P(("band", "lon")),
    )
    out_specs = (P(None, "band", "lon"), P("band", "lon"))
    return jax.shard_map(on_device, mesh=mesh, in_specs=in_specs, out_specs=out_specs, check_vma=False)
```

time: 63.7 us -> 52.4 us (0.82)
  blocking collectives: 15.4 us -> 0 us
  starting transfers between devices: 11.1 us -> 19.8 us
  local copies, waits for them, and re-layouts: 7.71 us -> 1.35 us
  waiting for transfers between devices: 16.1 us -> 17.9 us
    all_to_all x1 -> x0, blocking collectives: 15.4 us -> none  [on_device(): asked = lax.all_to_all(req, 'band', 0, 0, tiled=True)]
    all_to_all x0 -> x1, starting transfers between devices: none -> 8.45 us  [on_device(): asked = lax.all_to_all(req, 'band', 0, 0, tiled=True)]
    unnamed x20 -> x4, local copies, waits for them, and re-layouts: 7.71 us -> 1.35 us
    all_to_all x0 -> x1, waiting for transfers between devices: none -> 5.66 us  [on_device(): asked = lax.all_to_all(req, 'band', 0, 0, tiled=True)]
    all_to_all x1, waiting for transfers between devices: 9.4 us -> 6.81 us  [on_device(): recv = lax.all_to_all(send, 'band', 0, 0, tiled=True)]
    ppermute x1, waiting for transfers between devices: 4.18 us -> 3.14 us  [on_device(): from_b = lax.ppermute(to_b, 'band', pairs_b)]
    pallas_call x4 -> x8, Pallas kernels: 9.96 us -> 10.8 us  [the longest x1 4.03 us: on_device(): call(remap_kernel, (shape((2, R_DEV, C_DEV), bf16), rows, rows, shape((ch...]
    pallas_call x1, Pallas kernels: 1.59 us -> 0.91 us  [on_device(): call(functools.partial(route_kernel, lons * tiles, tiles), (shape((bands,...]
  transfers between devices with their start and end apart: 5 -> 6, of which waited for: 3 -> 4; matrix products, arithmetic and copies ran while one was open for 0% -> 0% of each run, Pallas kernels for 0% -> 8%
where the time goes in v2:
time: 52.4 us; the launch traced here: 52 us
  starting transfers between devices  19.8 us (38%)
  waiting for transfers between devices  17.9 us (34%)
  Pallas kernels  11.7 us (22%)
  between operations  1.36 us (3%)
  local copies, waits for them, and re-layouts  1.35 us (3%)
    all_to_all x1, starting transfers between devices, on_device(): asked = lax.all_to_all(req, 'band', 0, 0, tiled=True)  8.45 us
    all_to_all x1, waiting for transfers between devices, on_device(): recv = lax.all_to_all(send, 'band', 0, 0, tiled=True)  6.81 us
    all_to_all x1, waiting for transfers between devices, on_device(): asked = lax.all_to_all(req, 'band', 0, 0, tiled=True)  5.66 us
    pallas_call x1, Pallas kernels, on_device(): call(remap_kernel, (shape((2, R_DEV, C_DEV), bf16), rows, rows, shape((ch...  4.03 us
    all_to_all x1, starting transfers between devices, on_device(): recv = lax.all_to_all(send, 'band', 0, 0, tiled=True)  4.02 us
    ppermute x1, waiting for transfers between devices, on_device(): from_b = lax.ppermute(to_b, 'band', pairs_b)  3.14 us
    ppermute x1, starting transfers between devices, on_device(): from_b = lax.ppermute(to_b, 'lon', ring_b)  2.36 us
    ppermute x1, starting transfers between devices, on_device(): from_b = lax.ppermute(to_b, 'band', pairs_b)  2.35 us
  transfers between devices with their start and end apart: 6, of which 4 were waited for; matrix products, arithmetic and copies ran while one was open for 0% of the time, Pallas kernels for 8%

profile of v2, /device:TPU:1, one launch (start us, length us, event | category | flops | bytes accessed | tf_op | source)
XLA Modules:
  0.0 52.0 jit_solution(290495590410931766)
XLA Ops:
  0.6 0.0 copy-start.1
  0.6 0.7 %copy-done.1 = s32[256]{0:T(256)S(1)} copy-done((s32[256]{0:T(256)S(1)}, s32[256]{0:T(256)}, u32[]{:S(2)}) %copy-start.1) | copy-done | bytes 1048
  1.3 0.9 %shard_map.68 = (s32[16,128]{1,0:T(8,128)}, s32[8,256]{1,0:T(8,128)S(1)}) custom-call(s32[1,256]{1,0:T(1,128)S(1)} %bitcast.8), custom_call_target="tpu_custom_call" | custom-call | tf_op jit(solution)/shard_map/pallas_call | solution.py:243
  2.2 8.4 %all-to-all-start = ((s32[16,1,128]{2,1,0:T(1,128)}), s32[16,1,128]{2,1,0:T(1,128)S(1)}, u32[]{:S(2)}, u32[]{:S(2)}) async-start(s32[16,1,128]{2,1,0:T(1,128)} %bitcast.3), calls=%async_computation | async-start | bytes 16384 | tf_op jit(solution)/shard_map/all_to_all | solution.py:248
  10.7 1.3 %shard_map.70.src_ref = bf16[6,512,128]{2,1,0:T(8,128)(2,1)S(1)} custom-call(s32[16,128]{1,0:T(8,128)} %get-tuple-element.16.after_ref, bf16[6,512,128]{2,1,0:T(8,128)(2,1)} %source_hbm.2), custom_call_target="tpu_custom_call" | custom-call | flops 786432 | bytes 786432 | tf_op jit(solution)/shard_map/pallas_call | solution.py:249
  11.9 5.7 %all-to-all-done = s32[16,1,128]{2,1,0:T(1,128)S(1)} async-done(((s32[16,1,128]{2,1,0:T(1,128)}), s32[16,1,128]{2,1,0:T(1,128)S(1)}, u32[]{:S(2)}, u32[]{:S(2)}) %all-to-all-start) | async-done | bytes 8224 | tf_op jit(solution)/shard_map/all_to_all | solution.py:248
  17.6 1.4 %shard_map.71.after_ref = bf16[16,96,128]{2,1,0:T(8,128)(2,1)} custom-call(s32[16,128]{1,0:T(8,128)S(1)} %bitcast.6, bf16[6,512,128]{2,1,0:T(8,128)(2,1)S(1)} %shard_map.70.src_ref), custom_call_target="tpu_custom_call" | custom-call | tf_op jit(solution)/shard_map/pallas_call | solution.py:258
  19.0 4.0 %all-to-all-start.1 = ((bf16[16,96,128]{2,1,0:T(8,128)(2,1)}), bf16[16,96,128]{2,1,0:T(8,128)(2,1)S(1)}, u32[]{:S(2)}, u32[]{:S(2)}) async-start(bf16[16,96,128]{2,1,0:T(8,128)(2,1)} %shard_map.71.after_ref), calls=%async_computation.1 | async-start | bytes 786432 | tf_op jit(solution)/shard_map/all_to_all | solution.py:265
  23.7 0.0 copy-start
  23.7 0.7 %copy-done = s32[256]{0:T(256)S(1)} copy-done((s32[256]{0:T(256)S(1)}, s32[256]{0:T(256)}, u32[]{:S(2)}) %copy-start) | copy-done | bytes 1048
  24.3 0.3 shard_map.69
  24.6 1.7 %shard_map.72.held_ref = bf16[80,128,128]{2,1,0:T(8,128)(2,1)S(1)} custom-call(bf16[16,96,128]{2,1,0:T(8,128)(2,1)} %shard_map.71.after_ref, bf16[256,128,128]{2,1,0:T(8,128)(2,1)} %weight_hbm.1), custom_call_target="tpu_custom_call" | custom-call | flops 2621440 | bytes 2621440 | tf_op jit(solution)/shard_map/pallas_call | solution.py:266
  26.3 6.8 %all-to-all-done.1.recv_ref = bf16[16,96,128]{2,1,0:T(8,128)(2,1)S(1)} async-done(((bf16[16,96,128]{2,1,0:T(8,128)(2,1)}), bf16[16,96,128]{2,1,0:T(8,128)(2,1)S(1)}, u32[]{:S(2)}, u32[]{:S(2)}) %all-to-all-start.1) | async-done | bytes 393248 | tf_op jit(solution)/shard_map/all_to_all | solution.py:265
  33.1 4.0 %shard_map.73 = (bf16[2,16,1024]{2,1,0:T(8,128)(2,1)S(1)}, bf16[8,1024]{1,0:T(8,128)(2,1)S(1)}, bf16[8,1024]{1,0:T(8,128)(2,1)S(1)}, f32[4,256,128]{2,1,0:T(8,128)S(1)}) custom-call(bf16[16,96,128]{2,1,0:T(8,128)(2,1)S(1)} %all-to-all-done.1.recv_ref, bf16[256,256]{1,0:T(8,128)(2,1)S(1)} %get-tuple-element.17.perm_ref, ...), custom_call_target="tpu_custom_call" | custom-call | tf_op jit(solution)/shard_map/pallas_call | solution.py:271
  37.2 0.9 %collective-permute-start = (bf16[8,1024]{1,0:T(8,128)(2,1)S(1)}, bf16[8,1024]{1,0:T(8,128)(2,1)S(1)}, u32[]{:S(2)}, u32[]{:S(2)}) collective-permute-start(bf16[8,1024]{1,0:T(8,128)(2,1)S(1)} %get-tuple-element.21), channel_id=1, source_target_pairs={{0,8},{8,0},{16,24},{24,16},{32,40},{40,32},{48,56},{56,48},{64,72... | collective-permute-start | bytes 49160 | tf_op jit(solution)/shard_map/ppermute | solution.py:290
  38.0 2.4 %collective-permute-start.1 = (bf16[8,1024]{1,0:T(8,128)(2,1)S(1)}, bf16[8,1024]{1,0:T(8,128)(2,1)S(1)}, u32[]{:S(2)}, u32[]{:S(2)}) collective-permute-start(bf16[8,1024]{1,0:T(8,128)(2,1)S(1)} %get-tuple-element.22), channel_id=1, source_target_pairs={{8,16},{16,8},{24,32},{32,24},{40,48},{48,40},{56,64},{64,56},{72,... | collective-permute-start | bytes 49160 | tf_op jit(solution)/shard_map/ppermute | solution.py:291
  40.4 1.0 %shard_map.74.after_ref = bf16[6,16,1024]{2,1,0:T(8,128)(2,1)} custom-call(bf16[128,256]{1,0:T(8,128)(2,1)S(1)} %get-tuple-element.15.chosen_ref, f32[4,256,128]{2,1,0:T(8,128)S(1)} %get-tuple-element.18.others_ref, bf16[2,16,1024]{2,1,0:T(8,128)(2,1)S(1)} %get-tuple-element.19.wind_ref), custom_call_target="tpu_custom_call" | custom-call | flops 1048576 | bytes 1048576 | tf_op jit(solution)/shard_map/pallas_call | solution.py:283
  41.5 0.0 collective-permute-done.from_a_ref
  41.5 3.1 %collective-permute-done.1.from_b_ref = bf16[8,1024]{1,0:T(8,128)(2,1)S(1)} collective-permute-done((bf16[8,1024]{1,0:T(8,128)(2,1)S(1)}, bf16[8,1024]{1,0:T(8,128)(2,1)S(1)}, u32[]{:S(2)}, u32[]{:S(2)}) %collective-permute-start.1) | collective-permute-done | bytes 16416 | tf_op jit(solution)/shard_map/ppermute | solution.py:291
  44.6 1.7 %collective-permute-start.2 = (bf16[48,128]{1,0:T(8,128)(2,1)S(1)}, bf16[48,128]{1,0:T(8,128)(2,1)S(1)}, u32[]{:S(2)}, u32[]{:S(2)}) collective-permute-start(bf16[48,128]{1,0:T(8,128)(2,1)S(1)} %get-tuple-element.24), channel_id=1, source_target_pairs={{0,1},{1,0},{2,3},{3,2},{4,5},{5,4},{6,7},{7,6},{8,9},{9,8},{10,11... | collective-permute-start | bytes 36872 | tf_op jit(solution)/shard_map/ppermute | solution.py:296
  46.3 2.4 %collective-permute-start.3 = (bf16[48,128]{1,0:T(8,128)(2,1)S(1)}, bf16[48,128]{1,0:T(8,128)(2,1)S(1)}, u32[]{:S(2)}, u32[]{:S(2)}) collective-permute-start(bf16[48,128]{1,0:T(8,128)(2,1)S(1)} %get-tuple-element.25), channel_id=1, source_target_pairs={{0,7},{1,2},{2,1},{3,4},{4,3},{5,6},{6,5},{7,0},{8,15},{9,10},{10,... | collective-permute-start | bytes 36872 | tf_op jit(solution)/shard_map/ppermute | solution.py:297
  48.7 0.0 collective-permute-done.2.from_a_ref
  48.7 2.3 %collective-permute-done.3.from_b_ref = bf16[48,128]{1,0:T(8,128)(2,1)S(1)} collective-permute-done((bf16[48,128]{1,0:T(8,128)(2,1)S(1)}, bf16[48,128]{1,0:T(8,128)(2,1)S(1)}, u32[]{:S(2)}, u32[]{:S(2)}) %collective-permute-start.3) | collective-permute-done | bytes 12320 | tf_op jit(solution)/shard_map/ppermute | solution.py:297
  51.0 1.0 %shard_map.76 = f32[16,1024]{1,0:T(8,128)} custom-call(f32[24,128]{1,0:T(8,128)S(1)} %get-tuple-element.20.cosine_ref, f32[2,24,1024]{2,1,0:T(8,128)S(1)} %get-tuple-element.23.ext_ref, bf16[48,128]{1,0:T(8,128)(2,1)S(1)} %collective-permute-done.2.from_a_ref, bf16[48,128]{1,0:T(8,128)(2,1)S(1)} %collective-permute-done.3.from_b_ref), custom_call_target="tpu_custom_call" | custom-call | tf_op jit(solution)/shard_map/pallas_call | solution.py:298
  (1 shorter events, 0.0 us)
Async XLA Ops:
  0.6 0.7 %copy-start.1 = (s32[256]{0:T(256)S(1)}, s32[256]{0:T(256)}, u32[]{:S(2)}) copy-start(s32[256]{0:T(256)} %param.6) | copy-start | bytes 3076
  2.2 15.4 %all-to-all-start = ((s32[16,1,128]{2,1,0:T(1,128)}), s32[16,1,128]{2,1,0:T(1,128)S(1)}, u32[]{:S(2)}, u32[]{:S(2)}) async-start(s32[16,1,128]{2,1,0:T(1,128)} %bitcast.3), calls=%async_computation | async-start | bytes 16384 | tf_op jit(solution)/shard_map/all_to_all | solution.py:248
  19.0 14.2 %all-to-all-start.1 = ((bf16[16,96,128]{2,1,0:T(8,128)(2,1)}), bf16[16,96,128]{2,1,0:T(8,128)(2,1)S(1)}, u32[]{:S(2)}, u32[]{:S(2)}) async-start(bf16[16,96,128]{2,1,0:T(8,128)(2,1)} %shard_map.71.after_ref), calls=%async_computation.1 | async-start | bytes 786432 | tf_op jit(solution)/shard_map/all_to_all | solution.py:265
  23.7 0.7 %copy-start = (s32[256]{0:T(256)S(1)}, s32[256]{0:T(256)}, u32[]{:S(2)}) copy-start(s32[256]{0:T(256)} %param.7) | copy-start | bytes 3076
  37.2 4.3 %collective-permute-start = (bf16[8,1024]{1,0:T(8,128)(2,1)S(1)}, bf16[8,1024]{1,0:T(8,128)(2,1)S(1)}, u32[]{:S(2)}, u32[]{:S(2)}) collective-permute-start(bf16[8,1024]{1,0:T(8,128)(2,1)S(1)} %get-tuple-element.21), channel_id=1, source_target_pairs={{0,8},{8,0},{16,24},{24,16},{32,40},{40,32},{48,56},{56,48},{64,72... | collective-permute-start | bytes 49160 | tf_op jit(solution)/shard_map/ppermute | solution.py:290
  38.0 6.5 %collective-permute-start.1 = (bf16[8,1024]{1,0:T(8,128)(2,1)S(1)}, bf16[8,1024]{1,0:T(8,128)(2,1)S(1)}, u32[]{:S(2)}, u32[]{:S(2)}) collective-permute-start(bf16[8,1024]{1,0:T(8,128)(2,1)S(1)} %get-tuple-element.22), channel_id=1, source_target_pairs={{8,16},{16,8},{24,32},{32,24},{40,48},{48,40},{56,64},{64,56},{72,... | collective-permute-start | bytes 49160 | tf_op jit(solution)/shard_map/ppermute | solution.py:291
  44.6 4.1 %collective-permute-start.2 = (bf16[48,128]{1,0:T(8,128)(2,1)S(1)}, bf16[48,128]{1,0:T(8,128)(2,1)S(1)}, u32[]{:S(2)}, u32[]{:S(2)}) collective-permute-start(bf16[48,128]{1,0:T(8,128)(2,1)S(1)} %get-tuple-element.24), channel_id=1, source_target_pairs={{0,1},{1,0},{2,3},{3,2},{4,5},{5,4},{6,7},{7,6},{8,9},{9,8},{10,11... | collective-permute-start | bytes 36872 | tf_op jit(solution)/shard_map/ppermute | solution.py:296
  46.3 4.7 %collective-permute-start.3 = (bf16[48,128]{1,0:T(8,128)(2,1)S(1)}, bf16[48,128]{1,0:T(8,128)(2,1)S(1)}, u32[]{:S(2)}, u32[]{:S(2)}) collective-permute-start(bf16[48,128]{1,0:T(8,128)(2,1)S(1)} %get-tuple-element.25), channel_id=1, source_target_pairs={{0,7},{1,2},{2,1},{3,4},{4,3},{5,6},{6,5},{7,0},{8,15},{9,10},{10,... | collective-permute-start | bytes 36872 | tf_op jit(solution)/shard_map/ppermute | solution.py:297

commit v3 on v2

--- a/solution.py
+++ b/solution.py
@@ -14,8 +14,9 @@
 BLK_ROW = C_DEV // BW
 LAT_START = 0.5
 HALO = 3
-HELD = 80
-CHUNK = 16
+RIM = 8
+HELD = 88
+CHUNK = 24
 EXT = 24
 
 VM = pl.BlockSpec(memory_space=pltpu.VMEM)
@@ -81,32 +82,67 @@
         copy.wait()
 
 
-def start_copies(source, target, sems, first=0):
-    parts = sems.shape[0]
-    size = target.shape[0] // parts
-    copies = []
-    for g in range(parts):
-        part = source.at[pl.ds(first + g * size, size)]
-        copies.append(pltpu.make_async_copy(part, target.at[pl.ds(g * size, size)], sems.at[g]))
-        copies[-1].start()
-    return copies
-
-
 def stage_kernel(after_ref, source_hbm, held_ref, sems):
-    for copy in start_copies(source_hbm, held_ref, sems):
+    copies = [pltpu.make_async_copy(source_hbm.at[c], held_ref.at[c], sems.at[c]) for c in range(sems.shape[0])]
+    for copy in copies:
+        copy.start()
+    for copy in copies:
         copy.wait()
 
 
-def select_kernel(row_stride, grid_step, live_ref, pos_ref, block_ref, perm_ref, chosen_ref, cosine_ref):
+def fetch_weights(order_ref, weight_hbm, target, sem, first, count, offset):
+    for i in range(count):
+        slot = order_ref[0, first + i]
+        pltpu.make_async_copy(weight_hbm.at[slot], target.at[offset + i], sem).start()
+
+
+def await_weights(weight_hbm, target, sem, count, offset):
+    pltpu.make_async_copy(weight_hbm.at[pl.ds(0, count)], target.at[pl.ds(offset, count)], sem).wait()
+
+
+def hold_kernel(order_ref, after_ref, weight_hbm, held_ref, sems):
+    for g in range(sems.shape[0]):
+        fetch_weights(order_ref, weight_hbm, held_ref, sems.at[g], g * 8, 8, g * 8)
+    for g in range(sems.shape[0]):
+        await_weights(weight_hbm, held_ref, sems.at[g], 8, g * 8)
+
+
+def select_kernel(
+    row_stride, grid_step, live_ref, pos_ref, block_ref,
+    perm_ref, chosen_ref, rim_ref, order_smem, cosine_ref, order_ref, sem,
+):
     slots = pos_ref.shape[1]
-    where_from = jnp.transpose(pos_ref[...].astype(jnp.float32))[:, :1].astype(jnp.int32)
+    block = block_ref[...]
+    row, column = (block // row_stride) % R_DEV, block % BLK_ROW
+    lane = iota((1, slots), 1)
+    live = lane < live_ref[0]
+    at_rim = (row < HALO) | (row >= R_DEV - HALO)
+    kind = jnp.where(live, jnp.where(at_rim, 0, 1), 2)
+    kinds = iota((8, slots), 0)
+    hit = kind == kinds
+    earlier = dot(as_bf16(hit), as_bf16(iota((slots, slots), 0) < iota((slots, slots), 1)))
+    n_rim = jnp.sum(jnp.where(kind == 0, 1.0, 0.0), axis=1, keepdims=True)
+    n_live = jnp.sum(jnp.where(kind < 2, 1.0, 0.0), axis=1, keepdims=True)
+    start = jnp.where(kinds == 1, n_rim, jnp.where(kinds == 2, n_live, 0.0))
+    place = jnp.sum(jnp.where(hit, earlier + start, 0.0), axis=0, keepdims=True).astype(jnp.int32)
+    move = as_bf16(place == iota((slots, slots), 0))
+    where_from = dot_nt(move, pos_ref[...].astype(jnp.float32).astype(jnp.bfloat16))[:, :1].astype(jnp.int32)
     perm_ref[...] = as_bf16(where_from == iota((slots, slots), 1))
-    block = block_ref[...]
-    target = (block % BLK_ROW) * R_DEV + (block // row_stride) % R_DEV
-    live = iota((1, slots), 1) < live_ref[0]
-    chosen_ref[...] = as_bf16((target == iota((BLK_ROW * R_DEV, slots), 0)) & live)
+    target = column * R_DEV + row
+    rim_target = jnp.where(at_rim, column * RIM + jnp.where(row < HALO, row, row - (R_DEV - 2 * HALO)), 255)
+    facts = [lane, target, live.astype(jnp.int32), rim_target]
+    facts = jnp.concatenate([f.astype(jnp.float32) for f in facts + [lane] * 4], axis=0).astype(jnp.bfloat16)
+    moved = dot_nt(facts, move).astype(jnp.int32)
+    used = moved[2:3] > 0
+    chosen_ref[...] = as_bf16((moved[1:2] == iota((BLK_ROW * R_DEV, slots), 0)) & used)
+    rim_ref[...] = as_bf16((moved[3:4] == iota((BLK_ROW * RIM, slots), 0)) & used)
+    counts = [jnp.broadcast_to(n.astype(jnp.int32), (1, slots)) for n in (n_rim, n_live)]
+    order_ref[...] = jnp.concatenate([moved[:1]] + counts + [moved[:1]] * 5, axis=0)
+    copy = pltpu.make_async_copy(order_ref, order_smem, sem)
+    copy.start()
     row = first_row() - HALO + iota(cosine_ref.shape, 0)
     cosine_ref[...] = jnp.cos(LAT_START + (row.astype(jnp.float32) + 0.5) * grid_step)
+    copy.wait()
 
 
 def add_blocks(chosen, rest):
@@ -116,49 +152,99 @@
         rest = rest - part.astype(jnp.float32)
         share = dot(chosen, part)
         total = share if total is None else total + share
-    field = jnp.concatenate([total[j * R_DEV : (j + 1) * R_DEV] for j in range(BLK_ROW)], axis=1)
+    rows = chosen.shape[0] // BLK_ROW
+    field = jnp.concatenate([total[j * rows : (j + 1) * rows] for j in range(BLK_ROW)], axis=1)
     return field.astype(jnp.bfloat16)
 
 
-def remap_kernel(
-    recv_ref, perm_ref, chosen_ref, held_ref, weight_hbm,
-    wind_ref, a_ref, b_ref, others_ref, weight, xs, term, sems,
-):
-    bands = recv_ref.shape[0]
-    slots, held = perm_ref.shape[0], held_ref.shape[0]
-    channels = 2 + others_ref.shape[0]
-    each = slots // bands
-    chunk = (slots - held) // sems.shape[0]
-    copies = start_copies(weight_hbm, weight, sems, held)
-    perm = perm_ref[...]
-    for c in range(channels):
-        xs[c] = dot(perm, recv_ref[:, c * each : (c + 1) * each, :].reshape(slots, 128))
+def order_tiles(xs, perm_ref, recv_ref, first, count):
+    slots = perm_ref.shape[0]
+    each = slots // recv_ref.shape[0]
+    for c in range(xs.shape[0]):
+        xs[c, first : first + count] = dot(
+            perm_ref[first : first + count], recv_ref[:, c * each : (c + 1) * each, :].reshape(slots, 128)
+        )
+
+
+def multiply(xs, eight, terms, first, count):
+    channels = xs.shape[0]
     row = iota((8 * channels, 128), 0) % 8
     masks = [as_bf16(row == j) for j in range(8)]
-    for s in range(0, slots, 8):
-        if s >= held and (s - held) % chunk == 0:
-            copies[(s - held) // chunk].wait()
-        x = jnp.concatenate([xs[c, s : s + 8, :] for c in range(channels)], axis=0).astype(jnp.bfloat16)
+    for g in range(0, count, 8):
+        rows = pl.ds(first + g, 8)
+        x = jnp.concatenate([xs[c, rows, :] for c in range(channels)], axis=0).astype(jnp.bfloat16)
         spread = jnp.concatenate([x * mask for mask in masks], axis=1)
-        eight = held_ref[s : s + 8] if s < held else weight[s - held : s - held + 8]
-        got = dot(spread, eight.reshape(8 * 128, 128))
+        got = dot(spread, eight(g))
         for c in range(channels):
-            target = term.at[c - 2] if c in (2, 3) else others_ref.at[c if c < 2 else c - 2]
-            target[s : s + 8, :] = got[c * 8 : (c + 1) * 8]
-    winds = []
-    for w in range(2):
-        rounded = add_blocks(chosen_ref[...], term[w])
-        wind_ref[w] = rounded
-        winds.append(rounded.astype(jnp.float32))
+            terms[c][rows, :] = got[c * 8 : (c + 1) * 8]
+
+
+def chunks_of(slots, count):
+    return jnp.clip((count - HELD + CHUNK - 1) // CHUNK, 0, (slots - HELD) // CHUNK)
+
+
+def chunk_steps(order, weight_hbm, weight, xs, terms, sems):
+    def fetch(k, carry):
+        fetch_weights(order, weight_hbm, weight, sems.at[k], HELD + k * CHUNK, CHUNK, k * CHUNK)
+        return carry
+
+    def step(k, carry):
+        await_weights(weight_hbm, weight, sems.at[k], CHUNK, k * CHUNK)
+        eight = lambda g: weight[pl.ds(k * CHUNK + g, 8)].reshape(8 * 128, 128)
+        multiply(xs, eight, terms, pl.multiple_of(HELD + k * CHUNK, 8), CHUNK)
+        return carry
+
+    return fetch, step
+
+
+def rim_kernel(
+    order, recv_ref, perm_ref, rim_ref, held_ref, weight_hbm, first_ref, b_ref, term_ref,
+    weight, xs, sems,
+):
+    channels, slots, _ = term_ref.shape
+    terms = [term_ref.at[c] for c in range(channels)]
+    half = slots // 2
+    chunks = chunks_of(slots, order[1, 0])
+
+    fetch, step = chunk_steps(order, weight_hbm, weight, xs, terms, sems)
+    lax.fori_loop(0, chunks, fetch, 0)
+    order_tiles(xs, perm_ref, recv_ref, 0, half)
+
+    @pl.when(HELD + chunks * CHUNK > half)
+    def _():
+        order_tiles(xs, perm_ref, recv_ref, half, half)
+
+    for term in terms:
+        term[HELD:slots, :] = jnp.zeros((slots - HELD, 128), jnp.float32)
+    multiply(xs, lambda g: held_ref[g : g + 8].reshape(8 * 128, 128), terms, 0, HELD)
+    lax.fori_loop(0, chunks, step, 0)
+    winds = [add_blocks(rim_ref[...], term_ref[c]).astype(jnp.float32) for c in (2, 3)]
     pad = jnp.zeros((8 - 2 * HALO, C_DEV), jnp.float32)
     first = jnp.concatenate([w[:HALO] for w in winds] + [pad], axis=0)
-    last = jnp.concatenate([w[R_DEV - HALO :] for w in winds] + [pad], axis=0)
+    last = jnp.concatenate([w[HALO : 2 * HALO] for w in winds] + [pad], axis=0)
     odd = is_odd("band")
-    a_ref[...] = jnp.where(odd, first, last).astype(jnp.bfloat16)
+    first_ref[...] = jnp.where(odd, first, last).astype(jnp.bfloat16)
     b_ref[...] = jnp.where(odd, last, first).astype(jnp.bfloat16)
 
 
-def finish_kernel(chosen_ref, others_ref, wind_ref, out_ref):
+def rest_kernel(
+    after_ref, order, recv_ref, perm_ref, chosen_ref, term_ref, weight_hbm,
+    wind_ref, others_ref, weight, xs, term, sems,
+):
+    channels, slots, _ = term_ref.shape
+    terms = [term.at[c - 2] if c in (2, 3) else others_ref.at[c if c < 2 else c - 2] for c in range(channels)]
+    first, last = chunks_of(slots, order[1, 0]), chunks_of(slots, order[2, 0])
+    fetch, step = chunk_steps(order, weight_hbm, weight, xs, terms, sems)
+    lax.fori_loop(first, last, fetch, 0)
+    order_tiles(xs, perm_ref, recv_ref, 0, slots)
+    for c in range(channels):
+        terms[c][...] = term_ref[c]
+    lax.fori_loop(first, last, step, 0)
+    for w in range(2):
+        wind_ref[w] = add_blocks(chosen_ref[...], term[w])
+
+
+def finish_kernel(after_ref, chosen_ref, others_ref, wind_ref, out_ref):
     for c in range(out_ref.shape[0]):
         if c in (2, 3):
             out_ref[c] = wind_ref[c - 2]
@@ -166,7 +252,7 @@
             out_ref[c] = add_blocks(chosen_ref[...], others_ref[c if c < 2 else c - 2])
 
 
-def extend_kernel(after_ref, wind_ref, from_a_ref, from_b_ref, ext_ref, a_ref, b_ref):
+def extend_kernel(wind_ref, from_a_ref, from_b_ref, ext_ref, a_ref, b_ref):
     from_a = from_a_ref[...].astype(jnp.float32)
     from_b = from_b_ref[...].astype(jnp.float32)
     odd = is_odd("band")
@@ -249,12 +335,22 @@
     tiles_held = call(
         stage_kernel, pltpu.VMEM(src_tiles.shape, bf16), [ANY, HB], [dmas((channels,))], cycles=2 * src_tiles.size
     )(req, held(src_tiles, pltpu.HBM))
-    perm, chosen, cosine = call(
+    perm, chosen, rim, order, cosine = call(
         functools.partial(select_kernel, BLK_ROW * lons, 2.0 * math.pi / (C_DEV * lons)),
-        (shape((slots, slots), bf16), shape((BLK_ROW * R_DEV, slots), bf16), shape((EXT, 128), f32)),
+        (
+            shape((slots, slots), bf16),
+            shape((BLK_ROW * R_DEV, slots), bf16),
+            shape((BLK_ROW * RIM, slots), bf16),
+            pltpu.SMEM((8, slots), i32),
+            shape((EXT, 128), f32),
+        ),
         [SM, VM, VM],
+        [pltpu.VMEM((8, slots), i32), dmas],
+        out_specs=(VM, VM, VM, SM, VM),
         cycles=slots * slots * 8,
     )(live_count, pos, ent_block.reshape(1, slots))
+    order = held(order, pltpu.SMEM)
+    weight_hbm = held(ent_weight, pltpu.HBM)
     send = call(
         pick_kernel,
         pltpu.HBM((bands, channels * each, pixels), bf16),
@@ -264,25 +360,34 @@
     )(asked, held(tiles_held, pltpu.VMEM))
     recv = lax.all_to_all(send, "band", 0, 0, tiled=True)
     weight_held = call(
-        stage_kernel, pltpu.VMEM((HELD, pixels, BW), bf16), [ANY, HB], [dmas((4,))], cycles=2 * HELD * pixels * BW
-    )(held(send, pltpu.HBM), held(ent_weight, pltpu.HBM))
+        hold_kernel,
+        pltpu.VMEM((HELD, pixels, BW), bf16),
+        [SM, ANY, HB],
+        [dmas((HELD // 8,))],
+        cycles=2 * HELD * pixels * BW,
+    )(order, held(send, pltpu.HBM), weight_hbm)
 
     rows = shape((8, C_DEV), bf16)
-    wind, to_a, to_b, others = call(
-        remap_kernel,
-        (shape((2, R_DEV, C_DEV), bf16), rows, rows, shape((channels - 2, slots, BW), f32)),
-        [VM, VM, VM, VM, HB],
-        [
-            pltpu.VMEM((slots - HELD, pixels, BW), bf16),
-            pltpu.VMEM((channels, slots, pixels), f32),
-            pltpu.VMEM((2, slots, BW), f32),
-            dmas(((slots - HELD) // CHUNK,)),
-        ],
-        vmem=16 << 20,
-    )(recv, perm, chosen, held(weight_held, pltpu.VMEM), held(ent_weight, pltpu.HBM))
-    remapped = call(
-        finish_kernel, shape((channels, R_DEV, C_DEV), bf16), [VM, VM, VM], cycles=slots * slots * 16
-    )(chosen, others, wind)
+    chunks = (slots - HELD) // CHUNK
+    work = [
+        pltpu.VMEM((slots - HELD, pixels, BW), bf16),
+        pltpu.VMEM((channels, slots, pixels), f32),
+    ]
+    to_a, to_b, term = call(
+        rim_kernel,
+        (rows, rows, shape((channels, slots, BW), f32)),
+        [SM, VM, VM, VM, VM, HB],
+        work + [dmas((chunks,))],
+        vmem=12 << 20,
+    )(order, recv, perm, rim, held(weight_held, pltpu.VMEM), weight_hbm)
+    wind, others = call(
+        rest_kernel,
+        (shape((2, R_DEV, C_DEV), bf16), shape((channels - 2, slots, BW), f32)),
+        [ANY, SM, VM, VM, VM, VM, HB],
+        work + [pltpu.VMEM((2, slots, BW), f32), dmas((chunks,))],
+        vmem=12 << 20,
+        cycles=slots * pixels * BW,
+    )(to_a, order, recv, perm, chosen, term, weight_hbm)
 
     pairs_a = lambda size: [(i, i ^ 1) for i in range(size)]
     pairs_b = [(i, i + 1 if i % 2 else i - 1) for i in range(1, bands - 1)]
@@ -290,9 +395,12 @@
     from_a = lax.ppermute(to_a, "band", pairs_a(bands))
     from_b = lax.ppermute(to_b, "band", pairs_b)
     edge = shape((2 * EXT, 128), bf16)
-    ext, to_a, to_b = call(extend_kernel, (shape((2, EXT, C_DEV), f32), edge, edge), [ANY, VM, VM, VM])(
-        held(remapped, pltpu.HBM), wind, from_a, from_b
+    ext, to_a, to_b = call(extend_kernel, (shape((2, EXT, C_DEV), f32), edge, edge), [VM, VM, VM])(
+        wind, from_a, from_b
     )
+    remapped = call(
+        finish_kernel, shape((channels, R_DEV, C_DEV), bf16), [ANY, VM, VM, VM], cycles=slots * slots * 16
+    )(to_a, chosen, others, wind)
     from_a = lax.ppermute(to_a, "lon", pairs_a(lons))
     from_b = lax.ppermute(to_b, "lon", ring_b)
     smoothed = call(

time: 52.4 us -> 49 us (0.935)
  the two profiles are of different devices: /device:TPU:1 before, /device:TPU:2 now
where the time goes in v3:
time: 49 us; the launch traced here: 48 us
  starting transfers between devices  20.9 us (43%)
  Pallas kernels  12.3 us (25%)
  waiting for transfers between devices  12.1 us (25%)
  between operations  1.37 us (3%)
  local copies, waits for them, and re-layouts  1.35 us (3%)
    all_to_all x1, starting transfers between devices, on_device(): asked = lax.all_to_all(req, 'band', 0, 0, tiled=True)  7.48 us
    all_to_all x1, waiting for transfers between devices, on_device(): asked = lax.all_to_all(req, 'band', 0, 0, tiled=True)  4.86 us
    all_to_all x1, starting transfers between devices, on_device(): recv = lax.all_to_all(send, 'band', 0, 0, tiled=True)  4.84 us
    ppermute x1, starting transfers between devices, on_device(): from_b = lax.ppermute(to_b, 'band', pairs_b)  4.23 us
    ppermute x1, starting transfers between devices, on_device(): from_b = lax.ppermute(to_b, 'lon', ring_b)  4.23 us
    all_to_all x1, waiting for transfers between devices, on_device(): recv = lax.all_to_all(send, 'band', 0, 0, tiled=True)  4.21 us
    pallas_call x1, Pallas kernels, on_device(): call(rest_kernel, (shape((2, R_DEV, C_DEV), bf16), shape((channels - 2, s...  2.72 us
    ppermute x1, waiting for transfers between devices, on_device(): from_a = lax.ppermute(to_a, 'lon', pairs_a(lons))  2.02 us
  transfers between devices with their start and end apart: 6, of which 5 were waited for; matrix products, arithmetic and copies ran while one was open for 0% of the time, Pallas kernels for 17%

profile of v3, /device:TPU:2, one launch (start us, length us, event | category | flops | bytes accessed | tf_op | source)
XLA Modules:
  0.0 48.0 jit_solution(327755599738026575)
XLA Ops:
  0.6 0.7 %copy-done.1 = s32[256]{0:T(256)S(1)} copy-done((s32[256]{0:T(256)S(1)}, s32[256]{0:T(256)}, u32[]{:S(2)}) %copy-start.1) | copy-done | bytes 1048
  1.3 0.9 %shard_map.68 = (s32[16,128]{1,0:T(8,128)}, s32[8,256]{1,0:T(8,128)S(1)}) custom-call(s32[1,256]{1,0:T(1,128)S(1)} %bitcast.8), custom_call_target="tpu_custom_call" | custom-call | tf_op jit(solution)/shard_map/pallas_call | solution.py:329
  2.2 7.5 %all-to-all-start = ((s32[16,1,128]{2,1,0:T(1,128)}), s32[16,1,128]{2,1,0:T(1,128)S(1)}, u32[]{:S(2)}, u32[]{:S(2)}) async-start(s32[16,1,128]{2,1,0:T(1,128)} %bitcast.3), calls=%async_computation | async-start | bytes 16384 | tf_op jit(solution)/shard_map/all_to_all | solution.py:334
  9.7 1.3 %shard_map.70.src_ref = bf16[6,512,128]{2,1,0:T(8,128)(2,1)S(1)} custom-call(s32[16,128]{1,0:T(8,128)} %get-tuple-element.19.after_ref, bf16[6,512,128]{2,1,0:T(8,128)(2,1)} %source_hbm.1), custom_call_target="tpu_custom_call" | custom-call | flops 786432 | bytes 786432 | tf_op jit(solution)/shard_map/pallas_call | solution.py:335
  11.0 4.9 %all-to-all-done = s32[16,1,128]{2,1,0:T(1,128)S(1)} async-done(((s32[16,1,128]{2,1,0:T(1,128)}), s32[16,1,128]{2,1,0:T(1,128)S(1)}, u32[]{:S(2)}, u32[]{:S(2)}) %all-to-all-start) | async-done | bytes 8224 | tf_op jit(solution)/shard_map/all_to_all | solution.py:334
  15.8 1.4 %shard_map.71.after_ref = bf16[16,96,128]{2,1,0:T(8,128)(2,1)} custom-call(s32[16,128]{1,0:T(8,128)S(1)} %bitcast.6, bf16[6,512,128]{2,1,0:T(8,128)(2,1)S(1)} %shard_map.70.src_ref), custom_call_target="tpu_custom_call" | custom-call | tf_op jit(solution)/shard_map/pallas_call | solution.py:354
  17.2 4.8 %all-to-all-start.1 = ((bf16[16,96,128]{2,1,0:T(8,128)(2,1)}), bf16[16,96,128]{2,1,0:T(8,128)(2,1)S(1)}, u32[]{:S(2)}, u32[]{:S(2)}) async-start(bf16[16,96,128]{2,1,0:T(8,128)(2,1)} %shard_map.71.after_ref), calls=%async_computation.1 | async-start | bytes 786432 | tf_op jit(solution)/shard_map/all_to_all | solution.py:361
  22.7 0.0 copy-start
  22.7 0.7 %copy-done = s32[256]{0:T(256)S(1)} copy-done((s32[256]{0:T(256)S(1)}, s32[256]{0:T(256)}, u32[]{:S(2)}) %copy-start) | copy-done | bytes 1048
  23.4 1.1 %shard_map.69 = (bf16[256,256]{1,0:T(8,128)(2,1)S(1)}, bf16[128,256]{1,0:T(8,128)(2,1)S(1)}, bf16[64,256]{1,0:T(8,128)(2,1)S(1)}, s32[8,256]{1,0:T(8,128)S(4)}, f32[24,128]{1,0:T(8,128)S(1)}) custom-call(s32[1]{0:T(128)S(6)} %copy.8.live_ref, s32[8,256]{1,0:T(8,128)S(1)} %get-tuple-element.17.pos_ref, s32[1,256]{1,0:T(1,128)S(1)} %bitcast.7), custom_call_target="tpu_custom_call" | custom-call | flops 524288 | bytes 524288 | tf_op jit(solution)/shard_map/pallas_call | solution.py:338
  24.5 1.8 %shard_map.72.held_ref = bf16[88,128,128]{2,1,0:T(8,128)(2,1)S(1)} custom-call(s32[8,256]{1,0:T(8,128)S(4)} %get-tuple-element.18.order_ref.order, bf16[16,96,128]{2,1,0:T(8,128)(2,1)} %shard_map.71.after_ref, bf16[256,128,128]{2,1,0:T(8,128)(2,1)} %weight_hbm.5), custom_call_target="tpu_custom_call" | custom-call | flops 2883584 | bytes 2883584 | tf_op jit(solution)/shard_map/pallas_call | solution.py:362
  26.3 4.2 %all-to-all-done.1.recv_ref = bf16[16,96,128]{2,1,0:T(8,128)(2,1)S(1)} async-done(((bf16[16,96,128]{2,1,0:T(8,128)(2,1)}), bf16[16,96,128]{2,1,0:T(8,128)(2,1)S(1)}, u32[]{:S(2)}, u32[]{:S(2)}) %all-to-all-start.1) | async-done | bytes 393248 | tf_op jit(solution)/shard_map/all_to_all | solution.py:361
  30.5 1.1 %shard_map.73 = (bf16[8,1024]{1,0:T(8,128)(2,1)S(1)}, bf16[8,1024]{1,0:T(8,128)(2,1)S(1)}, f32[6,256,128]{2,1,0:T(8,128)S(1)}) custom-call(s32[8,256]{1,0:T(8,128)S(4)} %get-tuple-element.18.order_ref.order, bf16[16,96,128]{2,1,0:T(8,128)(2,1)S(1)} %all-to-all-done.1.recv_ref, bf16[256,256]{1,0:T(8,128)(2,1)S(1)} %get-tuple-element.20.perm_ref, ...), custom_call_target="tpu_custom_call" | custom-call | tf_op jit(solution)/shard_map/pallas_call | solution.py:376
  31.6 4.2 %collective-permute-start.1 = (bf16[8,1024]{1,0:T(8,128)(2,1)S(1)}, bf16[8,1024]{1,0:T(8,128)(2,1)S(1)}, u32[]{:S(2)}, u32[]{:S(2)}) collective-permute-start(bf16[8,1024]{1,0:T(8,128)(2,1)S(1)} %get-tuple-element.26), channel_id=1, source_target_pairs={{8,16},{16,8},{24,32},{32,24},{40,48},{48,40},{56,64},{64,56},{72,... | collective-permute-start | bytes 49160 | tf_op jit(solution)/shard_map/ppermute | solution.py:396
  35.8 0.1 collective-permute-start
  35.9 2.7 %shard_map.74 = (bf16[2,16,1024]{2,1,0:T(8,128)(2,1)S(1)}, f32[4,256,128]{2,1,0:T(8,128)S(1)}) custom-call(bf16[8,1024]{1,0:T(8,128)(2,1)S(1)} %get-tuple-element.22.after_ref, s32[8,256]{1,0:T(8,128)S(4)} %get-tuple-element.18.order_ref.order, bf16[16,96,128]{2,1,0:T(8,128)(2,1)S(1)} %all-to-all-done.1.recv_ref, ...), custom_call_target="tpu_custom_call" | custom-call | flops 4194304 | bytes 4194304 | tf_op jit(solution)/shard_map/pallas_call | solution.py:383
  38.6 0.4 collective-permute-done.1.from_b_ref
  39.0 0.0 collective-permute-done.from_a_ref
  39.1 4.2 %collective-permute-start.3 = (bf16[48,128]{1,0:T(8,128)(2,1)S(1)}, bf16[48,128]{1,0:T(8,128)(2,1)S(1)}, u32[]{:S(2)}, u32[]{:S(2)}) collective-permute-start(bf16[48,128]{1,0:T(8,128)(2,1)S(1)} %get-tuple-element.31), channel_id=1, source_target_pairs={{0,7},{1,2},{2,1},{3,4},{4,3},{5,6},{6,5},{7,0},{8,15},{9,10},{10,... | collective-permute-start | bytes 36872 | tf_op jit(solution)/shard_map/ppermute | solution.py:405
  43.3 0.0 collective-permute-start.2
  43.3 1.0 %shard_map.76 = bf16[6,16,1024]{2,1,0:T(8,128)(2,1)} custom-call(bf16[48,128]{1,0:T(8,128)(2,1)S(1)} %get-tuple-element.27.after_ref, bf16[128,256]{1,0:T(8,128)(2,1)S(1)} %get-tuple-element.23.chosen_ref, f32[4,256,128]{2,1,0:T(8,128)S(1)} %get-tuple-element.28.others_ref, bf16[2,16,1024]{2,1,0:T(8,128)(2,1)S(1)} %get-tuple-element.25.wind_ref), custom_call_target="tpu_custom_call" | custom-call | flops 1048576 | bytes 1048576 | tf_op jit(solution)/shard_map/pallas_call | solution.py:401
  44.4 0.6 %collective-permute-done.3.from_b_ref = bf16[48,128]{1,0:T(8,128)(2,1)S(1)} collective-permute-done((bf16[48,128]{1,0:T(8,128)(2,1)S(1)}, bf16[48,128]{1,0:T(8,128)(2,1)S(1)}, u32[]{:S(2)}, u32[]{:S(2)}) %collective-permute-start.3) | collective-permute-done | bytes 12320 | tf_op jit(solution)/shard_map/ppermute | solution.py:405
  45.0 2.0 %collective-permute-done.2.from_a_ref = bf16[48,128]{1,0:T(8,128)(2,1)S(1)} collective-permute-done((bf16[48,128]{1,0:T(8,128)(2,1)S(1)}, bf16[48,128]{1,0:T(8,128)(2,1)S(1)}, u32[]{:S(2)}, u32[]{:S(2)}) %collective-permute-start.2) | collective-permute-done | bytes 12320 | tf_op jit(solution)/shard_map/ppermute | solution.py:404
  47.0 1.0 %shard_map.77 = f32[16,1024]{1,0:T(8,128)} custom-call(f32[24,128]{1,0:T(8,128)S(1)} %get-tuple-element.29.cosine_ref, f32[2,24,1024]{2,1,0:T(8,128)S(1)} %get-tuple-element.30.ext_ref, bf16[48,128]{1,0:T(8,128)(2,1)S(1)} %collective-permute-done.2.from_a_ref, bf16[48,128]{1,0:T(8,128)(2,1)S(1)} %collective-permute-done.3.from_b_ref), custom_call_target="tpu_custom_call" | custom-call | tf_op jit(solution)/shard_map/pallas_call | solution.py:406
  (2 shorter events, 0.0 us)
Async XLA Ops:
  0.6 0.7 %copy-start.1 = (s32[256]{0:T(256)S(1)}, s32[256]{0:T(256)}, u32[]{:S(2)}) copy-start(s32[256]{0:T(256)} %param.6) | copy-start | bytes 3076
  2.2 13.6 %all-to-all-start = ((s32[16,1,128]{2,1,0:T(1,128)}), s32[16,1,128]{2,1,0:T(1,128)S(1)}, u32[]{:S(2)}, u32[]{:S(2)}) async-start(s32[16,1,128]{2,1,0:T(1,128)} %bitcast.3), calls=%async_computation | async-start | bytes 16384 | tf_op jit(solution)/shard_map/all_to_all | solution.py:334
  17.2 13.3 %all-to-all-start.1 = ((bf16[16,96,128]{2,1,0:T(8,128)(2,1)}), bf16[16,96,128]{2,1,0:T(8,128)(2,1)S(1)}, u32[]{:S(2)}, u32[]{:S(2)}) async-start(bf16[16,96,128]{2,1,0:T(8,128)(2,1)} %shard_map.71.after_ref), calls=%async_computation.1 | async-start | bytes 786432 | tf_op jit(solution)/shard_map/all_to_all | solution.py:361
  22.7 0.7 %copy-start = (s32[256]{0:T(256)S(1)}, s32[256]{0:T(256)}, u32[]{:S(2)}) copy-start(s32[256]{0:T(256)} %param.7) | copy-start | bytes 3076
  31.6 7.5 %collective-permute-start.1 = (bf16[8,1024]{1,0:T(8,128)(2,1)S(1)}, bf16[8,1024]{1,0:T(8,128)(2,1)S(1)}, u32[]{:S(2)}, u32[]{:S(2)}) collective-permute-start(bf16[8,1024]{1,0:T(8,128)(2,1)S(1)} %get-tuple-element.26), channel_id=1, source_target_pairs={{8,16},{16,8},{24,32},{32,24},{40,48},{48,40},{56,64},{64,56},{72,... | collective-permute-start | bytes 49160 | tf_op jit(solution)/shard_map/ppermute | solution.py:396
  35.8 3.2 %collective-permute-start = (bf16[8,1024]{1,0:T(8,128)(2,1)S(1)}, bf16[8,1024]{1,0:T(8,128)(2,1)S(1)}, u32[]{:S(2)}, u32[]{:S(2)}) collective-permute-start(bf16[8,1024]{1,0:T(8,128)(2,1)S(1)} %get-tuple-element.22.after_ref), channel_id=1, source_target_pairs={{0,8},{8,0},{16,24},{24,16},{32,40},{40,32},{48,56},{56,48},{64,72... | collective-permute-start | bytes 49160 | tf_op jit(solution)/shard_map/ppermute | solution.py:395
  39.1 5.9 %collective-permute-start.3 = (bf16[48,128]{1,0:T(8,128)(2,1)S(1)}, bf16[48,128]{1,0:T(8,128)(2,1)S(1)}, u32[]{:S(2)}, u32[]{:S(2)}) collective-permute-start(bf16[48,128]{1,0:T(8,128)(2,1)S(1)} %get-tuple-element.31), channel_id=1, source_target_pairs={{0,7},{1,2},{2,1},{3,4},{4,3},{5,6},{6,5},{7,0},{8,15},{9,10},{10,... | collective-permute-start | bytes 36872 | tf_op jit(solution)/shard_map/ppermute | solution.py:405
  43.3 3.7 %collective-permute-start.2 = (bf16[48,128]{1,0:T(8,128)(2,1)S(1)}, bf16[48,128]{1,0:T(8,128)(2,1)S(1)}, u32[]{:S(2)}, u32[]{:S(2)}) collective-permute-start(bf16[48,128]{1,0:T(8,128)(2,1)S(1)} %get-tuple-element.27.after_ref), channel_id=1, source_target_pairs={{0,1},{1,0},{2,3},{3,2},{4,5},{5,4},{6,7},{7,6},{8,9},{9,8},{10,11... | collective-permute-start | bytes 36872 | tf_op jit(solution)/shard_map/ppermute | solution.py:404

commit v4 on v3

--- a/solution.py
+++ b/solution.py
@@ -14,7 +14,6 @@
 BLK_ROW = C_DEV // BW
 LAT_START = 0.5
 HALO = 3
-RIM = 8
 HELD = 88
 CHUNK = 24
 EXT = 24
@@ -52,10 +51,11 @@
 def route_kernel(per_band, tiles_held, tile_ref, req_ref, pos_ref):
     tile = tile_ref[...]
     slots = tile.shape[1]
-    bands = req_ref.shape[0]
-    owner = tile // per_band
-    local = tile % tiles_held
-    hit = owner == iota((bands, slots), 0)
+    chips = req_ref.shape[0]
+    band = tile // per_band
+    local = band % 2 * tiles_held + tile % tiles_held
+    owner = band // 2
+    hit = owner == iota((chips, slots), 0)
     before = as_bf16(iota((slots, slots), 0) < iota((slots, slots), 1))
     earlier = dot(as_bf16(hit), before)
     rank = jnp.sum(jnp.where(hit, earlier, 0.0), axis=0, keepdims=True).astype(jnp.int32)
@@ -63,21 +63,27 @@
     high = jnp.where(hit, (local // 16).astype(jnp.float32), 0.0).astype(jnp.bfloat16)
     low = jnp.where(hit, (local % 16).astype(jnp.float32), 0.0).astype(jnp.bfloat16)
     req_ref[...] = (dot_nt(high, place) * 16.0 + dot_nt(low, place)).astype(jnp.int32)
-    pos_ref[...] = jnp.broadcast_to(owner * (slots // bands) + rank, (8, slots))
-
-
-def pick_kernel(req_ref, src_ref, send_hbm, picked, sems):
-    channels, tiles, _ = src_ref.shape
-    _, bands, each, _ = picked.shape
+    pos_ref[...] = jnp.broadcast_to(owner * (slots // chips) + rank, (8, slots))
+
+
+def pick_kernel(req_ref, own_ref, mate_ref, send_hbm, picked, sems):
+    channels, tiles, _ = own_ref.shape
+    _, chips, each, _ = picked.shape
     asked = jnp.transpose(req_ref[...].astype(jnp.float32)).astype(jnp.int32)
+    mine = jnp.where(is_odd("band"), tiles, 0)
     cell = iota((each, tiles), 1)
-    onehot = jnp.concatenate([as_bf16(asked[:each, d : d + 1] == cell) for d in range(bands)], axis=0)
+    columns = [jnp.broadcast_to(asked[:each, d : d + 1], (each, tiles)) for d in range(chips)]
+    own = jnp.concatenate([as_bf16(column == cell + mine) for column in columns], axis=0)
+    mate = jnp.concatenate([as_bf16(column == cell + (tiles - mine)) for column in columns], axis=0)
     copies = []
-    for c in range(channels):
-        got = dot(onehot, src_ref[c]).astype(jnp.bfloat16)
-        picked[c] = got.reshape(bands, each, 128)
-        copies.append(pltpu.make_async_copy(picked.at[c], send_hbm.at[:, pl.ds(c * each, each)], sems.at[c]))
-        copies[-1].start()
+    for c in range(0, channels, 2):
+        pair = lambda ref: jnp.concatenate([ref[c], ref[c + 1]], axis=1)
+        got = (dot(own, pair(own_ref)) + dot(mate, pair(mate_ref))).astype(jnp.bfloat16)
+        for k in range(2):
+            picked[c + k] = got[:, k * 128 : (k + 1) * 128].reshape(chips, each, 128)
+            target = send_hbm.at[:, pl.ds((c + k) * each, each)]
+            copies.append(pltpu.make_async_copy(picked.at[c + k], target, sems.at[c + k]))
+            copies[-1].start()
     for copy in copies:
         copy.wait()
 
@@ -108,7 +114,7 @@
 
 
 def select_kernel(
-    row_stride, grid_step, live_ref, pos_ref, block_ref,
+    row_stride, grid_step, after_ref, live_ref, pos_ref, block_ref,
     perm_ref, chosen_ref, rim_ref, order_smem, cosine_ref, order_ref, sem,
 ):
     slots = pos_ref.shape[1]
@@ -116,7 +122,7 @@
     row, column = (block // row_stride) % R_DEV, block % BLK_ROW
     lane = iota((1, slots), 1)
     live = lane < live_ref[0]
-    at_rim = (row < HALO) | (row >= R_DEV - HALO)
+    at_rim = (column == 0) | (column == BLK_ROW - 1)
     kind = jnp.where(live, jnp.where(at_rim, 0, 1), 2)
     kinds = iota((8, slots), 0)
     hit = kind == kinds
@@ -129,13 +135,13 @@
     where_from = dot_nt(move, pos_ref[...].astype(jnp.float32).astype(jnp.bfloat16))[:, :1].astype(jnp.int32)
     perm_ref[...] = as_bf16(where_from == iota((slots, slots), 1))
     target = column * R_DEV + row
-    rim_target = jnp.where(at_rim, column * RIM + jnp.where(row < HALO, row, row - (R_DEV - 2 * HALO)), 255)
+    rim_target = jnp.where(at_rim, jnp.where(column == 0, row, R_DEV + row), 255)
     facts = [lane, target, live.astype(jnp.int32), rim_target]
     facts = jnp.concatenate([f.astype(jnp.float32) for f in facts + [lane] * 4], axis=0).astype(jnp.bfloat16)
     moved = dot_nt(facts, move).astype(jnp.int32)
     used = moved[2:3] > 0
     chosen_ref[...] = as_bf16((moved[1:2] == iota((BLK_ROW * R_DEV, slots), 0)) & used)
-    rim_ref[...] = as_bf16((moved[3:4] == iota((BLK_ROW * RIM, slots), 0)) & used)
+    rim_ref[...] = as_bf16((moved[3:4] == iota(rim_ref.shape, 0)) & used)
     counts = [jnp.broadcast_to(n.astype(jnp.int32), (1, slots)) for n in (n_rim, n_live)]
     order_ref[...] = jnp.concatenate([moved[:1]] + counts + [moved[:1]] * 5, axis=0)
     copy = pltpu.make_async_copy(order_ref, order_smem, sem)
@@ -145,15 +151,19 @@
     copy.wait()
 
 
-def add_blocks(chosen, rest):
+def add_terms(chosen, rest):
     total = None
     for _ in range(3):
         part = rest.astype(jnp.bfloat16)
         rest = rest - part.astype(jnp.float32)
         share = dot(chosen, part)
         total = share if total is None else total + share
-    rows = chosen.shape[0] // BLK_ROW
-    field = jnp.concatenate([total[j * rows : (j + 1) * rows] for j in range(BLK_ROW)], axis=1)
+    return total
+
+
+def add_blocks(chosen, rest):
+    total = add_terms(chosen, rest)
+    field = jnp.concatenate([total[j * R_DEV : (j + 1) * R_DEV] for j in range(BLK_ROW)], axis=1)
     return field.astype(jnp.bfloat16)
 
 
@@ -198,7 +208,7 @@
 
 
 def rim_kernel(
-    order, recv_ref, perm_ref, rim_ref, held_ref, weight_hbm, first_ref, b_ref, term_ref,
+    order, recv_ref, perm_ref, rim_ref, held_ref, weight_hbm, a_ref, b_ref, term_ref,
     weight, xs, sems,
 ):
     channels, slots, _ = term_ref.shape
@@ -218,13 +228,12 @@
         term[HELD:slots, :] = jnp.zeros((slots - HELD, 128), jnp.float32)
     multiply(xs, lambda g: held_ref[g : g + 8].reshape(8 * 128, 128), terms, 0, HELD)
     lax.fori_loop(0, chunks, step, 0)
-    winds = [add_blocks(rim_ref[...], term_ref[c]).astype(jnp.float32) for c in (2, 3)]
-    pad = jnp.zeros((8 - 2 * HALO, C_DEV), jnp.float32)
-    first = jnp.concatenate([w[:HALO] for w in winds] + [pad], axis=0)
-    last = jnp.concatenate([w[HALO : 2 * HALO] for w in winds] + [pad], axis=0)
-    odd = is_odd("band")
-    first_ref[...] = jnp.where(odd, first, last).astype(jnp.bfloat16)
-    b_ref[...] = jnp.where(odd, last, first).astype(jnp.bfloat16)
+    winds = [add_terms(rim_ref[...], term_ref[c]) for c in (2, 3)]
+    left = jnp.concatenate([w[:R_DEV] for w in winds], axis=0)
+    right = jnp.concatenate([w[R_DEV:] for w in winds], axis=0)
+    odd = is_odd("lon")
+    a_ref[...] = jnp.where(odd, left, right).astype(jnp.bfloat16)
+    b_ref[...] = jnp.where(odd, right, left).astype(jnp.bfloat16)
 
 
 def rest_kernel(
@@ -255,22 +264,20 @@
 def extend_kernel(wind_ref, from_a_ref, from_b_ref, ext_ref, a_ref, b_ref):
     from_a = from_a_ref[...].astype(jnp.float32)
     from_b = from_b_ref[...].astype(jnp.float32)
+    odd = is_odd("lon")
+    left = jnp.where(odd, from_a, from_b)
+    right = jnp.where(odd, from_b, from_a)
+    winds = []
+    for w in range(2):
+        rows = slice(w * R_DEV, (w + 1) * R_DEV)
+        winds.append(jnp.concatenate([left[rows], wind_ref[w].astype(jnp.float32), right[rows]], axis=1))
+        ext_ref[w] = winds[w]
+    pad = jnp.zeros((8 - 2 * HALO, winds[0].shape[1]), jnp.float32)
+    first = jnp.concatenate([w[:HALO] for w in winds] + [pad], axis=0)
+    last = jnp.concatenate([w[R_DEV - HALO :] for w in winds] + [pad], axis=0)
     odd = is_odd("band")
-    above = jnp.where(odd, from_a, from_b)
-    below = jnp.where(odd, from_b, from_a)
-    pad = jnp.zeros((EXT - R_DEV - 2 * HALO, C_DEV), jnp.float32)
-    left, right = [], []
-    for w in range(2):
-        rows = slice(w * HALO, (w + 1) * HALO)
-        full = jnp.concatenate([above[rows], wind_ref[w].astype(jnp.float32), below[rows], pad], axis=0)
-        ext_ref[w] = full
-        left.append(full[:, :128])
-        right.append(full[:, C_DEV - 128 :])
-    left = jnp.concatenate(left, axis=0)
-    right = jnp.concatenate(right, axis=0)
-    odd = is_odd("lon")
-    a_ref[...] = jnp.where(odd, left, right).astype(jnp.bfloat16)
-    b_ref[...] = jnp.where(odd, right, left).astype(jnp.bfloat16)
+    a_ref[...] = jnp.where(odd, first, last).astype(jnp.bfloat16)
+    b_ref[...] = jnp.where(odd, last, first).astype(jnp.bfloat16)
 
 
 def smooth(x):
@@ -283,11 +290,12 @@
 def smooth_kernel(all_rows, cosine_ref, ext_ref, from_a_ref, from_b_ref, out_ref):
     from_a = from_a_ref[...].astype(jnp.float32)
     from_b = from_b_ref[...].astype(jnp.float32)
-    odd = is_odd("lon")
-    left = jnp.where(odd, from_a, from_b)
-    right = jnp.where(odd, from_b, from_a)
+    odd = is_odd("band")
+    above = jnp.where(odd, from_a, from_b)
+    below = jnp.where(odd, from_b, from_a)
+    pad = jnp.zeros((EXT - R_DEV - 2 * HALO, above.shape[1]), jnp.float32)
     east, north = (
-        jnp.concatenate([left[w * EXT : (w + 1) * EXT], ext_ref[w], right[w * EXT : (w + 1) * EXT]], axis=1)
+        jnp.concatenate([above[w * HALO : (w + 1) * HALO], ext_ref[w], below[w * HALO : (w + 1) * HALO], pad], axis=0)
         for w in range(2)
     )
     rows, columns = east.shape
@@ -320,45 +328,50 @@
     bands, lons = lax.axis_size("band"), lax.axis_size("lon")
     channels, tiles, pixels = src_tiles.shape
     slots = ent_tile.shape[0]
-    each = slots // bands
+    each = 2 * slots // bands
     shape = jax.ShapeDtypeStruct
     bf16, f32, i32 = jnp.bfloat16, jnp.float32, jnp.int32
     dmas = pltpu.SemaphoreType.DMA
     held = pltpu.with_memory_space_constraint
 
+    chips = bands // 2
+    same_core = [[chip * 2 + core for chip in range(chips)] for core in range(2)]
+    exchange = lambda x: lax.all_to_all(x, "band", 0, 0, tiled=True, axis_index_groups=same_core)
+    pairs_a = lambda size: [(i, i ^ 1) for i in range(size)]
+    mate_tiles = lax.ppermute(src_tiles, "band", pairs_a(bands))
     req, pos = call(
         functools.partial(route_kernel, lons * tiles, tiles),
-        (shape((bands, 128), i32), shape((8, slots), i32)),
+        (shape((chips, 128), i32), shape((8, slots), i32)),
         [VM],
     )(ent_tile.reshape(1, slots))
-    asked = lax.all_to_all(req, "band", 0, 0, tiled=True)
-    tiles_held = call(
+    asked = exchange(req)
+    own_tiles = call(
         stage_kernel, pltpu.VMEM(src_tiles.shape, bf16), [ANY, HB], [dmas((channels,))], cycles=2 * src_tiles.size
     )(req, held(src_tiles, pltpu.HBM))
+    send = call(
+        pick_kernel,
+        pltpu.HBM((chips, channels * each, pixels), bf16),
+        [VM, VM, VM],
+        [pltpu.VMEM((channels, chips, each, pixels), bf16), dmas((channels,))],
+        out_specs=HB,
+    )(asked, held(own_tiles, pltpu.VMEM), held(mate_tiles, pltpu.VMEM))
     perm, chosen, rim, order, cosine = call(
         functools.partial(select_kernel, BLK_ROW * lons, 2.0 * math.pi / (C_DEV * lons)),
         (
             shape((slots, slots), bf16),
             shape((BLK_ROW * R_DEV, slots), bf16),
-            shape((BLK_ROW * RIM, slots), bf16),
+            shape((2 * R_DEV, slots), bf16),
             pltpu.SMEM((8, slots), i32),
             shape((EXT, 128), f32),
         ),
-        [SM, VM, VM],
+        [ANY, SM, VM, VM],
         [pltpu.VMEM((8, slots), i32), dmas],
         out_specs=(VM, VM, VM, SM, VM),
         cycles=slots * slots * 8,
-    )(live_count, pos, ent_block.reshape(1, slots))
+    )(held(send, pltpu.HBM), live_count, pos, ent_block.reshape(1, slots))
     order = held(order, pltpu.SMEM)
     weight_hbm = held(ent_weight, pltpu.HBM)
-    send = call(
-        pick_kernel,
-        pltpu.HBM((bands, channels * each, pixels), bf16),
-        [VM, VM],
-        [pltpu.VMEM((channels, bands, each, pixels), bf16), dmas((channels,))],
-        out_specs=HB,
-    )(asked, held(tiles_held, pltpu.VMEM))
-    recv = lax.all_to_all(send, "band", 0, 0, tiled=True)
+    recv = exchange(send)
     weight_held = call(
         hold_kernel,
         pltpu.VMEM((HELD, pixels, BW), bf16),
@@ -367,7 +380,7 @@
         cycles=2 * HELD * pixels * BW,
     )(order, held(send, pltpu.HBM), weight_hbm)
 
-    rows = shape((8, C_DEV), bf16)
+    sides, rows = shape((2 * R_DEV, 128), bf16), shape((8, C_DEV + 256), bf16)
     chunks = (slots - HELD) // CHUNK
     work = [
         pltpu.VMEM((slots - HELD, pixels, BW), bf16),
@@ -375,7 +388,7 @@
     ]
     to_a, to_b, term = call(
         rim_kernel,
-        (rows, rows, shape((channels, slots, BW), f32)),
+        (sides, sides, shape((channels, slots, BW), f32)),
         [SM, VM, VM, VM, VM, HB],
         work + [dmas((chunks,))],
         vmem=12 << 20,
@@ -389,20 +402,18 @@
         cycles=slots * pixels * BW,
     )(to_a, order, recv, perm, chosen, term, weight_hbm)
 
-    pairs_a = lambda size: [(i, i ^ 1) for i in range(size)]
     pairs_b = [(i, i + 1 if i % 2 else i - 1) for i in range(1, bands - 1)]
     ring_b = [(i, (i + 1 if i % 2 else i - 1) % lons) for i in range(lons)]
-    from_a = lax.ppermute(to_a, "band", pairs_a(bands))
-    from_b = lax.ppermute(to_b, "band", pairs_b)
-    edge = shape((2 * EXT, 128), bf16)
-    ext, to_a, to_b = call(extend_kernel, (shape((2, EXT, C_DEV), f32), edge, edge), [VM, VM, VM])(
+    from_a = lax.ppermute(to_a, "lon", pairs_a(lons))
+    from_b = lax.ppermute(to_b, "lon", ring_b)
+    ext, to_a, to_b = call(extend_kernel, (shape((2, R_DEV, C_DEV + 256), f32), rows, rows), [VM, VM, VM])(
         wind, from_a, from_b
     )
     remapped = call(
         finish_kernel, shape((channels, R_DEV, C_DEV), bf16), [ANY, VM, VM, VM], cycles=slots * slots * 16
     )(to_a, chosen, others, wind)
-    from_a = lax.ppermute(to_a, "lon", pairs_a(lons))
-    from_b = lax.ppermute(to_b, "lon", ring_b)
+    from_a = lax.ppermute(to_a, "band", pairs_a(bands))
+    from_b = lax.ppermute(to_b, "band", pairs_b)
     smoothed = call(
         functools.partial(smooth_kernel, R_DEV * bands),
         shape((R_DEV, C_DEV), f32),

time: 49 us -> 48 us (0.980)
    ppermute x1, starting transfers between devices: 4.23 us -> 1.92 us  [on_device(): from_b = lax.ppermute(to_b, 'band', pairs_b)]
    ppermute x1, starting transfers between devices: 0.09 us -> 2.22 us  [on_device(): from_a = lax.ppermute(to_a, 'band', pairs_a(bands))]
    ppermute x1, waiting for transfers between devices: 0.4 us -> 2.31 us  [on_device(): from_b = lax.ppermute(to_b, 'band', pairs_b)]
    ppermute x1, waiting for transfers between devices: 2.02 us -> 1.19 us  [on_device(): from_a = lax.ppermute(to_a, 'lon', pairs_a(lons))]
    all_to_all x2, waiting for transfers between devices: 9.06 us -> 8.34 us  [on_device(): lax.all_to_all(x, 'band', 0, 0, tiled=True, axis_index_groups=same_core)]
    ppermute x1, waiting for transfers between devices: 0.63 us -> 0.01 us  [on_device(): from_b = lax.ppermute(to_b, 'lon', ring_b)]
  transfers between devices with their start and end apart: 6 -> 7, of which waited for: 5 -> 4; matrix products, arithmetic and copies ran while one was open for 0% -> 0% of each run, Pallas kernels for 17% -> 18%
where the time goes in v4:
time: 48 us; the launch traced here: 47.4 us
  starting transfers between devices  20.8 us (43%)
  Pallas kernels  12.1 us (25%)
  waiting for transfers between devices  11.9 us (25%)
  between operations  1.38 us (3%)
  local copies, waits for them, and re-layouts  1.35 us (3%)
    all_to_all x2, starting transfers between devices, on_device(): lax.all_to_all(x, 'band', 0, 0, tiled=True, axis_index_groups=same_core)  12.3 us
    all_to_all x2, waiting for transfers between devices, on_device(): lax.all_to_all(x, 'band', 0, 0, tiled=True, axis_index_groups=same_core)  8.34 us
    ppermute x1, starting transfers between devices, on_device(): from_b = lax.ppermute(to_b, 'lon', ring_b)  4.23 us
    pallas_call x1, Pallas kernels, on_device(): call(rest_kernel, (shape((2, R_DEV, C_DEV), bf16), shape((channels - 2, s...  2.44 us
    ppermute x1, waiting for transfers between devices, on_device(): from_b = lax.ppermute(to_b, 'band', pairs_b)  2.31 us
    ppermute x1, starting transfers between devices, on_device(): from_a = lax.ppermute(to_a, 'band', pairs_a(bands))  2.22 us
    ppermute x1, starting transfers between devices, on_device(): from_b = lax.ppermute(to_b, 'band', pairs_b)  1.92 us
    pallas_call x1, Pallas kernels, on_device(): call(hold_kernel, pltpu.VMEM((HELD, pixels, BW), bf16), [SM, ANY, HB], [d...  1.83 us
  transfers between devices with their start and end apart: 7, of which 4 were waited for; matrix products, arithmetic and copies ran while one was open for 0% of the time, Pallas kernels for 18%

profile of v4, /device:TPU:2, one launch (start us, length us, event | category | flops | bytes accessed | tf_op | source)
XLA Modules:
  0.0 47.4 jit_solution(13381652605698988763)
XLA Ops:
  0.6 0.1 collective-permute-start
  0.7 0.7 %copy-done.1 = s32[256]{0:T(256)S(1)} copy-done((s32[256]{0:T(256)S(1)}, s32[256]{0:T(256)}, u32[]{:S(2)}) %copy-start.1) | copy-done | bytes 1048
  1.4 0.9 %shard_map.68 = (s32[8,128]{1,0:T(8,128)}, s32[8,256]{1,0:T(8,128)S(1)}) custom-call(s32[1,256]{1,0:T(1,128)S(1)} %bitcast.8), custom_call_target="tpu_custom_call" | custom-call | tf_op jit(solution)/shard_map/pallas_call | solution.py:342
  2.3 7.5 %all-to-all-start = ((s32[8,1,128]{2,1,0:T(1,128)}), s32[8,1,128]{2,1,0:T(1,128)S(1)}, u32[]{:S(2)}, u32[]{:S(2)}) async-start(s32[8,1,128]{2,1,0:T(1,128)} %bitcast.2), calls=%async_computation | async-start | bytes 8192 | tf_op jit(solution)/shard_map/all_to_all | solution.py:339
  9.8 1.3 %shard_map.69.own_ref = bf16[6,512,128]{2,1,0:T(8,128)(2,1)S(1)} custom-call(s32[8,128]{1,0:T(8,128)} %get-tuple-element.17.after_ref, bf16[6,512,128]{2,1,0:T(8,128)(2,1)} %source_hbm.1), custom_call_target="tpu_custom_call" | custom-call | flops 786432 | bytes 786432 | tf_op jit(solution)/shard_map/pallas_call | solution.py:348
  11.0 4.9 %all-to-all-done = s32[8,1,128]{2,1,0:T(1,128)S(1)} async-done(((s32[8,1,128]{2,1,0:T(1,128)}), s32[8,1,128]{2,1,0:T(1,128)S(1)}, u32[]{:S(2)}, u32[]{:S(2)}) %all-to-all-start) | async-done | bytes 4128 | tf_op jit(solution)/shard_map/all_to_all | solution.py:339
  15.9 0.0 collective-permute-done.mate_ref
  15.9 1.4 %shard_map.70.after_ref = bf16[8,192,128]{2,1,0:T(8,128)(2,1)} custom-call(s32[8,128]{1,0:T(8,128)S(1)} %bitcast.6, bf16[6,512,128]{2,1,0:T(8,128)(2,1)S(1)} %shard_map.69.own_ref, bf16[6,512,128]{2,1,0:T(8,128)(2,1)S(1)} %collective-permute-done.mate_ref), custom_call_target="tpu_custom_call" | custom-call | tf_op jit(solution)/shard_map/pallas_call | solution.py:351
  17.4 4.8 %all-to-all-start.1 = ((bf16[8,192,128]{2,1,0:T(8,128)(2,1)}), bf16[8,192,128]{2,1,0:T(8,128)(2,1)S(1)}, u32[]{:S(2)}, u32[]{:S(2)}) async-start(bf16[8,192,128]{2,1,0:T(8,128)(2,1)} %shard_map.70.after_ref), calls=%async_computation.1 | async-start | bytes 786432 | tf_op jit(solution)/shard_map/all_to_all | solution.py:339
  22.8 0.0 copy-start
  22.8 0.7 %copy-done = s32[256]{0:T(256)S(1)} copy-done((s32[256]{0:T(256)S(1)}, s32[256]{0:T(256)}, u32[]{:S(2)}) %copy-start) | copy-done | bytes 1048
  23.5 1.1 %shard_map.71 = (bf16[256,256]{1,0:T(8,128)(2,1)S(1)}, bf16[128,256]{1,0:T(8,128)(2,1)S(1)}, bf16[32,256]{1,0:T(8,128)(2,1)S(1)}, s32[8,256]{1,0:T(8,128)S(4)}, f32[24,128]{1,0:T(8,128)S(1)}) custom-call(bf16[8,192,128]{2,1,0:T(8,128)(2,1)} %shard_map.70.after_ref, s32[1]{0:T(128)S(6)} %copy.8.live_ref, s32[8,256]{1,0:T(8,128)S(1)} %get-tuple-element.18.pos_ref, ...), custom_call_target="tpu_custom_call" | custom-call | flops 524288 | bytes 524288 | tf_op jit(solution)/shard_map/pallas_call | solution.py:358
  24.6 1.8 %shard_map.72.held_ref = bf16[88,128,128]{2,1,0:T(8,128)(2,1)S(1)} custom-call(s32[8,256]{1,0:T(8,128)S(4)} %get-tuple-element.19.order_ref.order, bf16[8,192,128]{2,1,0:T(8,128)(2,1)} %shard_map.70.after_ref, bf16[256,128,128]{2,1,0:T(8,128)(2,1)} %weight_hbm.5), custom_call_target="tpu_custom_call" | custom-call | flops 2883584 | bytes 2883584 | tf_op jit(solution)/shard_map/pallas_call | solution.py:375
  26.4 3.5 %all-to-all-done.1.recv_ref = bf16[8,192,128]{2,1,0:T(8,128)(2,1)S(1)} async-done(((bf16[8,192,128]{2,1,0:T(8,128)(2,1)}), bf16[8,192,128]{2,1,0:T(8,128)(2,1)S(1)}, u32[]{:S(2)}, u32[]{:S(2)}) %all-to-all-start.1) | async-done | bytes 393248 | tf_op jit(solution)/shard_map/all_to_all | solution.py:339
  29.9 1.0 %shard_map.73 = (bf16[32,128]{1,0:T(8,128)(2,1)S(1)}, bf16[32,128]{1,0:T(8,128)(2,1)S(1)}, f32[6,256,128]{2,1,0:T(8,128)S(1)}) custom-call(s32[8,256]{1,0:T(8,128)S(4)} %get-tuple-element.19.order_ref.order, bf16[8,192,128]{2,1,0:T(8,128)(2,1)S(1)} %all-to-all-done.1.recv_ref, bf16[256,256]{1,0:T(8,128)(2,1)S(1)} %get-tuple-element.20.perm_ref, ...), custom_call_target="tpu_custom_call" | custom-call | tf_op jit(solution)/shard_map/pallas_call | solution.py:389
  31.0 4.2 %collective-permute-start.2 = (bf16[32,128]{1,0:T(8,128)(2,1)S(1)}, bf16[32,128]{1,0:T(8,128)(2,1)S(1)}, u32[]{:S(2)}, u32[]{:S(2)}) collective-permute-start(bf16[32,128]{1,0:T(8,128)(2,1)S(1)} %get-tuple-element.26), channel_id=1, source_target_pairs={{0,7},{1,2},{2,1},{3,4},{4,3},{5,6},{6,5},{7,0},{8,15},{9,10},{10,... | collective-permute-start | bytes 24584 | tf_op jit(solution)/shard_map/ppermute | solution.py:408
  35.2 2.4 %shard_map.74 = (bf16[2,16,1024]{2,1,0:T(8,128)(2,1)S(1)}, f32[4,256,128]{2,1,0:T(8,128)S(1)}) custom-call(bf16[32,128]{1,0:T(8,128)(2,1)S(1)} %get-tuple-element.22.after_ref, s32[8,256]{1,0:T(8,128)S(4)} %get-tuple-element.19.order_ref.order, bf16[8,192,128]{2,1,0:T(8,128)(2,1)S(1)} %all-to-all-done.1.recv_ref, ...), custom_call_target="tpu_custom_call" | custom-call | flops 4194304 | bytes 4194304 | tf_op jit(solution)/shard_map/pallas_call | solution.py:396
  37.7 0.0 collective-permute-done.2.from_b_ref
  37.7 1.2 %collective-permute-done.1.from_a_ref = bf16[32,128]{1,0:T(8,128)(2,1)S(1)} collective-permute-done((bf16[32,128]{1,0:T(8,128)(2,1)S(1)}, bf16[32,128]{1,0:T(8,128)(2,1)S(1)}, u32[]{:S(2)}, u32[]{:S(2)}) %collective-permute-start.1) | collective-permute-done | bytes 8224 | tf_op jit(solution)/shard_map/ppermute | solution.py:407
  38.9 1.9 %collective-permute-start.4 = (bf16[8,1280]{1,0:T(8,128)(2,1)S(1)}, bf16[8,1280]{1,0:T(8,128)(2,1)S(1)}, u32[]{:S(2)}, u32[]{:S(2)}) collective-permute-start(bf16[8,1280]{1,0:T(8,128)(2,1)S(1)} %get-tuple-element.31), channel_id=1, source_target_pairs={{8,16},{16,8},{24,32},{32,24},{40,48},{48,40},{56,64},{64,56},{72,... | collective-permute-start | bytes 61448 | tf_op jit(solution)/shard_map/ppermute | solution.py:416
  40.8 2.2 %collective-permute-start.3 = (bf16[8,1280]{1,0:T(8,128)(2,1)S(1)}, bf16[8,1280]{1,0:T(8,128)(2,1)S(1)}, u32[]{:S(2)}, u32[]{:S(2)}) collective-permute-start(bf16[8,1280]{1,0:T(8,128)(2,1)S(1)} %get-tuple-element.27.after_ref), channel_id=1, source_target_pairs={{0,8},{8,0},{16,24},{24,16},{32,40},{40,32},{48,56},{56,48},{64,72... | collective-permute-start | bytes 61448 | tf_op jit(solution)/shard_map/ppermute | solution.py:415
  43.0 1.0 %shard_map.76 = bf16[6,16,1024]{2,1,0:T(8,128)(2,1)} custom-call(bf16[8,1280]{1,0:T(8,128)(2,1)S(1)} %get-tuple-element.27.after_ref, bf16[128,256]{1,0:T(8,128)(2,1)S(1)} %get-tuple-element.23.chosen_ref, f32[4,256,128]{2,1,0:T(8,128)S(1)} %get-tuple-element.28.others_ref, bf16[2,16,1024]{2,1,0:T(8,128)(2,1)S(1)} %get-tuple-element.25.wind_ref), custom_call_target="tpu_custom_call" | custom-call | flops 1048576 | bytes 1048576 | tf_op jit(solution)/shard_map/pallas_call | solution.py:412
  44.1 2.3 %collective-permute-done.4.from_b_ref = bf16[8,1280]{1,0:T(8,128)(2,1)S(1)} collective-permute-done((bf16[8,1280]{1,0:T(8,128)(2,1)S(1)}, bf16[8,1280]{1,0:T(8,128)(2,1)S(1)}, u32[]{:S(2)}, u32[]{:S(2)}) %collective-permute-start.4) | collective-permute-done | bytes 20512 | tf_op jit(solution)/shard_map/ppermute | solution.py:416
  46.4 1.0 %shard_map.77 = f32[16,1024]{1,0:T(8,128)} custom-call(f32[24,128]{1,0:T(8,128)S(1)} %get-tuple-element.29.cosine_ref, f32[2,16,1280]{2,1,0:T(8,128)S(1)} %get-tuple-element.30.ext_ref, bf16[8,1280]{1,0:T(8,128)(2,1)S(1)} %collective-permute-done.3.from_a_ref, bf16[8,1280]{1,0:T(8,128)(2,1)S(1)} %collective-permute-done.4.from_b_ref), custom_call_target="tpu_custom_call" | custom-call | tf_op jit(solution)/shard_map/pallas_call | solution.py:417
  (4 shorter events, 0.0 us)
Async XLA Ops:
  0.6 15.3 %collective-permute-start = (bf16[6,512,128]{2,1,0:T(8,128)(2,1)}, bf16[6,512,128]{2,1,0:T(8,128)(2,1)S(1)}, u32[]{:S(2)}, u32[]{:S(2)}) collective-permute-start(bf16[6,512,128]{2,1,0:T(8,128)(2,1)} %source_hbm.1), channel_id=1, source_target_pairs={{0,8},{8,0},{16,24},{24,16},{32,40},{40,32},{48,56},{56,48},{64,72... | collective-permute-start | bytes 2359304 | tf_op jit(solution)/shard_map/ppermute | solution.py:341
  0.7 0.7 %copy-start.1 = (s32[256]{0:T(256)S(1)}, s32[256]{0:T(256)}, u32[]{:S(2)}) copy-start(s32[256]{0:T(256)} %param.6) | copy-start | bytes 3076
  2.3 13.6 %all-to-all-start = ((s32[8,1,128]{2,1,0:T(1,128)}), s32[8,1,128]{2,1,0:T(1,128)S(1)}, u32[]{:S(2)}, u32[]{:S(2)}) async-start(s32[8,1,128]{2,1,0:T(1,128)} %bitcast.2), calls=%async_computation | async-start | bytes 8192 | tf_op jit(solution)/shard_map/all_to_all | solution.py:339
  17.4 12.6 %all-to-all-start.1 = ((bf16[8,192,128]{2,1,0:T(8,128)(2,1)}), bf16[8,192,128]{2,1,0:T(8,128)(2,1)S(1)}, u32[]{:S(2)}, u32[]{:S(2)}) async-start(bf16[8,192,128]{2,1,0:T(8,128)(2,1)} %shard_map.70.after_ref), calls=%async_computation.1 | async-start | bytes 786432 | tf_op jit(solution)/shard_map/all_to_all | solution.py:339
  22.8 0.7 %copy-start = (s32[256]{0:T(256)S(1)}, s32[256]{0:T(256)}, u32[]{:S(2)}) copy-start(s32[256]{0:T(256)} %param.7) | copy-start | bytes 3076
  31.0 6.7 %collective-permute-start.2 = (bf16[32,128]{1,0:T(8,128)(2,1)S(1)}, bf16[32,128]{1,0:T(8,128)(2,1)S(1)}, u32[]{:S(2)}, u32[]{:S(2)}) collective-permute-start(bf16[32,128]{1,0:T(8,128)(2,1)S(1)} %get-tuple-element.26), channel_id=1, source_target_pairs={{0,7},{1,2},{2,1},{3,4},{4,3},{5,6},{6,5},{7,0},{8,15},{9,10},{10,... | collective-permute-start | bytes 24584 | tf_op jit(solution)/shard_map/ppermute | solution.py:408
  35.2 3.7 %collective-permute-start.1 = (bf16[32,128]{1,0:T(8,128)(2,1)S(1)}, bf16[32,128]{1,0:T(8,128)(2,1)S(1)}, u32[]{:S(2)}, u32[]{:S(2)}) collective-permute-start(bf16[32,128]{1,0:T(8,128)(2,1)S(1)} %get-tuple-element.22.after_ref), channel_id=1, source_target_pairs={{0,1},{1,0},{2,3},{3,2},{4,5},{5,4},{6,7},{7,6},{8,9},{9,8},{10,11... | collective-permute-start | bytes 24584 | tf_op jit(solution)/shard_map/ppermute | solution.py:407
  38.9 7.5 %collective-permute-start.4 = (bf16[8,1280]{1,0:T(8,128)(2,1)S(1)}, bf16[8,1280]{1,0:T(8,128)(2,1)S(1)}, u32[]{:S(2)}, u32[]{:S(2)}) collective-permute-start(bf16[8,1280]{1,0:T(8,128)(2,1)S(1)} %get-tuple-element.31), channel_id=1, source_target_pairs={{8,16},{16,8},{24,32},{32,24},{40,48},{48,40},{56,64},{64,56},{72,... | collective-permute-start | bytes 61448 | tf_op jit(solution)/shard_map/ppermute | solution.py:416
  40.8 5.6 %collective-permute-start.3 = (bf16[8,1280]{1,0:T(8,128)(2,1)S(1)}, bf16[8,1280]{1,0:T(8,128)(2,1)S(1)}, u32[]{:S(2)}, u32[]{:S(2)}) collective-permute-start(bf16[8,1280]{1,0:T(8,128)(2,1)S(1)} %get-tuple-element.27.after_ref), channel_id=1, source_target_pairs={{0,8},{8,0},{16,24},{24,16},{32,40},{40,32},{48,56},{56,48},{64,72... | collective-permute-start | bytes 61448 | tf_op jit(solution)/shard_map/ppermute | solution.py:415

commit v5 on v4

--- a/solution.py
+++ b/solution.py
@@ -48,7 +48,15 @@
     return lax.axis_index("band") * R_DEV
 
 
-def route_kernel(per_band, tiles_held, tile_ref, req_ref, pos_ref):
+def route_kernel(per_band, tiles_held, tile_hbm, src_hbm, req_ref, pos_ref, src_ref, tile_ref, tile_sem, sems):
+    tile_copy = pltpu.make_async_copy(tile_hbm, tile_ref, tile_sem)
+    tile_copy.start()
+    copies = []
+    for h in range(2):
+        half = pl.ds(h * (src_ref.shape[0] // 2), src_ref.shape[0] // 2)
+        copies.append(pltpu.make_async_copy(src_hbm.at[half], src_ref.at[half], sems.at[h]))
+        copies[-1].start()
+    tile_copy.wait()
     tile = tile_ref[...]
     slots = tile.shape[1]
     chips = req_ref.shape[0]
@@ -64,6 +72,8 @@
     low = jnp.where(hit, (local % 16).astype(jnp.float32), 0.0).astype(jnp.bfloat16)
     req_ref[...] = (dot_nt(high, place) * 16.0 + dot_nt(low, place)).astype(jnp.int32)
     pos_ref[...] = jnp.broadcast_to(owner * (slots // chips) + rank, (8, slots))
+    for copy in copies:
+        copy.wait()
 
 
 def pick_kernel(req_ref, own_ref, mate_ref, send_hbm, picked, sems):
@@ -84,14 +94,6 @@
             target = send_hbm.at[:, pl.ds((c + k) * each, each)]
             copies.append(pltpu.make_async_copy(picked.at[c + k], target, sems.at[c + k]))
             copies[-1].start()
-    for copy in copies:
-        copy.wait()
-
-
-def stage_kernel(after_ref, source_hbm, held_ref, sems):
-    copies = [pltpu.make_async_copy(source_hbm.at[c], held_ref.at[c], sems.at[c]) for c in range(sems.shape[0])]
-    for copy in copies:
-        copy.start()
     for copy in copies:
         copy.wait()
 
@@ -167,26 +169,26 @@
     return field.astype(jnp.bfloat16)
 
 
-def order_tiles(xs, perm_ref, recv_ref, first, count):
+def order_tiles(xs, perm_ref, recv_ref, channels, first, count):
     slots = perm_ref.shape[0]
     each = slots // recv_ref.shape[0]
-    for c in range(xs.shape[0]):
-        xs[c, first : first + count] = dot(
+    for i, c in enumerate(channels):
+        xs[i, first : first + count] = dot(
             perm_ref[first : first + count], recv_ref[:, c * each : (c + 1) * each, :].reshape(slots, 128)
         )
 
 
-def multiply(xs, eight, terms, first, count):
-    channels = xs.shape[0]
-    row = iota((8 * channels, 128), 0) % 8
+def multiply(xs, eight, terms, first, count, channels=None):
+    channels = channels or range(xs.shape[0])
+    row = iota((8 * len(channels), 128), 0) % 8
     masks = [as_bf16(row == j) for j in range(8)]
     for g in range(0, count, 8):
         rows = pl.ds(first + g, 8)
-        x = jnp.concatenate([xs[c, rows, :] for c in range(channels)], axis=0).astype(jnp.bfloat16)
+        x = jnp.concatenate([xs[c, rows, :] for c in channels], axis=0).astype(jnp.bfloat16)
         spread = jnp.concatenate([x * mask for mask in masks], axis=1)
         got = dot(spread, eight(g))
-        for c in range(channels):
-            terms[c][rows, :] = got[c * 8 : (c + 1) * 8]
+        for i, c in enumerate(channels):
+            terms[c][rows, :] = got[i * 8 : (i + 1) * 8]
 
 
 def chunks_of(slots, count):
@@ -211,24 +213,23 @@
     order, recv_ref, perm_ref, rim_ref, held_ref, weight_hbm, a_ref, b_ref, term_ref,
     weight, xs, sems,
 ):
-    channels, slots, _ = term_ref.shape
-    terms = [term_ref.at[c] for c in range(channels)]
+    slots = term_ref.shape[1]
+    terms = [term_ref.at[w] for w in range(2)]
     half = slots // 2
     chunks = chunks_of(slots, order[1, 0])
-
     fetch, step = chunk_steps(order, weight_hbm, weight, xs, terms, sems)
     lax.fori_loop(0, chunks, fetch, 0)
-    order_tiles(xs, perm_ref, recv_ref, 0, half)
+    order_tiles(xs, perm_ref, recv_ref, (2, 3), 0, half)
 
     @pl.when(HELD + chunks * CHUNK > half)
     def _():
-        order_tiles(xs, perm_ref, recv_ref, half, half)
+        order_tiles(xs, perm_ref, recv_ref, (2, 3), half, half)
 
     for term in terms:
         term[HELD:slots, :] = jnp.zeros((slots - HELD, 128), jnp.float32)
     multiply(xs, lambda g: held_ref[g : g + 8].reshape(8 * 128, 128), terms, 0, HELD)
     lax.fori_loop(0, chunks, step, 0)
-    winds = [add_terms(rim_ref[...], term_ref[c]) for c in (2, 3)]
+    winds = [add_terms(rim_ref[...], term[...]) for term in terms]
     left = jnp.concatenate([w[:R_DEV] for w in winds], axis=0)
     right = jnp.concatenate([w[R_DEV:] for w in winds], axis=0)
     odd = is_odd("lon")
@@ -237,18 +238,24 @@
 
 
 def rest_kernel(
-    after_ref, order, recv_ref, perm_ref, chosen_ref, term_ref, weight_hbm,
+    after_ref, order, recv_ref, perm_ref, chosen_ref, term_ref, held_ref, weight_hbm,
     wind_ref, others_ref, weight, xs, term, sems,
 ):
-    channels, slots, _ = term_ref.shape
+    slots = term_ref.shape[1]
+    channels = 2 + others_ref.shape[0]
     terms = [term.at[c - 2] if c in (2, 3) else others_ref.at[c if c < 2 else c - 2] for c in range(channels)]
-    first, last = chunks_of(slots, order[1, 0]), chunks_of(slots, order[2, 0])
+    last = chunks_of(slots, order[2, 0])
     fetch, step = chunk_steps(order, weight_hbm, weight, xs, terms, sems)
-    lax.fori_loop(first, last, fetch, 0)
-    order_tiles(xs, perm_ref, recv_ref, 0, slots)
-    for c in range(channels):
-        terms[c][...] = term_ref[c]
-    lax.fori_loop(first, last, step, 0)
+
+    lax.fori_loop(0, last, fetch, 0)
+    order_tiles(xs, perm_ref, recv_ref, range(channels), 0, slots)
+    for target in terms:
+        target[HELD:slots, :] = jnp.zeros((slots - HELD, 128), jnp.float32)
+    for w in range(2):
+        term[w, :HELD] = term_ref[w, :HELD]
+    eight = lambda g: held_ref[g : g + 8].reshape(8 * 128, 128)
+    multiply(xs, eight, terms, 0, HELD, [c for c in range(channels) if c not in (2, 3)])
+    lax.fori_loop(0, last, step, 0)
     for w in range(2):
         wind_ref[w] = add_blocks(chosen_ref[...], term[w])
 
@@ -339,15 +346,13 @@
     exchange = lambda x: lax.all_to_all(x, "band", 0, 0, tiled=True, axis_index_groups=same_core)
     pairs_a = lambda size: [(i, i ^ 1) for i in range(size)]
     mate_tiles = lax.ppermute(src_tiles, "band", pairs_a(bands))
-    req, pos = call(
+    req, pos, own_tiles = call(
         functools.partial(route_kernel, lons * tiles, tiles),
-        (shape((chips, 128), i32), shape((8, slots), i32)),
-        [VM],
-    )(ent_tile.reshape(1, slots))
+        (shape((chips, 128), i32), shape((8, slots), i32), shape(src_tiles.shape, bf16)),
+        [HB, HB],
+        [pltpu.VMEM((1, slots), i32), dmas, dmas((2,))],
+    )(held(ent_tile.reshape(1, slots), pltpu.HBM), held(src_tiles, pltpu.HBM))
     asked = exchange(req)
-    own_tiles = call(
-        stage_kernel, pltpu.VMEM(src_tiles.shape, bf16), [ANY, HB], [dmas((channels,))], cycles=2 * src_tiles.size
-    )(req, held(src_tiles, pltpu.HBM))
     send = call(
         pick_kernel,
         pltpu.HBM((chips, channels * each, pixels), bf16),
@@ -382,25 +387,24 @@
 
     sides, rows = shape((2 * R_DEV, 128), bf16), shape((8, C_DEV + 256), bf16)
     chunks = (slots - HELD) // CHUNK
-    work = [
-        pltpu.VMEM((slots - HELD, pixels, BW), bf16),
-        pltpu.VMEM((channels, slots, pixels), f32),
-    ]
+    weight = pltpu.VMEM((slots - HELD, pixels, BW), bf16)
+    per_slot = lambda count: pltpu.VMEM((count, slots, 128), f32)
+    weight_held = held(weight_held, pltpu.VMEM)
     to_a, to_b, term = call(
         rim_kernel,
-        (sides, sides, shape((channels, slots, BW), f32)),
+        (sides, sides, shape((2, slots, BW), f32)),
         [SM, VM, VM, VM, VM, HB],
-        work + [dmas((chunks,))],
+        [weight, per_slot(2), dmas((chunks,))],
         vmem=12 << 20,
-    )(order, recv, perm, rim, held(weight_held, pltpu.VMEM), weight_hbm)
+    )(order, recv, perm, rim, weight_held, weight_hbm)
     wind, others = call(
         rest_kernel,
         (shape((2, R_DEV, C_DEV), bf16), shape((channels - 2, slots, BW), f32)),
-        [ANY, SM, VM, VM, VM, VM, HB],
-        work + [pltpu.VMEM((2, slots, BW), f32), dmas((chunks,))],
+        [ANY, SM, VM, VM, VM, VM, VM, HB],
+        [weight, per_slot(channels), per_slot(2), dmas((chunks,))],
         vmem=12 << 20,
         cycles=slots * pixels * BW,
-    )(to_a, order, recv, perm, chosen, term, weight_hbm)
+    )(to_a, order, recv, perm, chosen, term, weight_held, weight_hbm)
 
     pairs_b = [(i, i + 1 if i % 2 else i - 1) for i in range(1, bands - 1)]
     ring_b = [(i, (i + 1 if i % 2 else i - 1) % lons) for i in range(lons)]

time: 48 us -> 47.4 us (0.987)
  blocking collectives: 0 us -> 13.5 us
  starting transfers between devices: 20.8 us -> 13.3 us
  waiting for transfers between devices: 11.9 us -> 7.52 us
  Pallas kernels: 12.1 us -> 10.5 us
  local copies, waits for them, and re-layouts: 1.35 us -> 0.67 us
    all_to_all x0 -> x1, blocking collectives: none -> 13.5 us  [on_device(): lax.all_to_all(x, 'band', 0, 0, tiled=True, axis_index_groups=same_core)]
    all_to_all x2 -> x1, starting transfers between devices: 12.3 us -> 4.83 us  [on_device(): lax.all_to_all(x, 'band', 0, 0, tiled=True, axis_index_groups=same_core)]
    all_to_all x2 -> x1, waiting for transfers between devices: 8.34 us -> 3.48 us  [on_device(): lax.all_to_all(x, 'band', 0, 0, tiled=True, axis_index_groups=same_core)]
    pallas_call x2 -> x1, Pallas kernels: 2.3 us -> 0.93 us  [on_device(): call(rim_kernel, (sides, sides, shape((2, slots, BW), f32)), [SM, VM, VM,...]
    unnamed x4 -> x2, local copies, waits for them, and re-layouts: 1.35 us -> 0.67 us
    ppermute x1, waiting for transfers between devices: 1.19 us -> 1.71 us  [on_device(): from_a = lax.ppermute(to_a, 'lon', pairs_a(lons))]
    pallas_call x1, Pallas kernels: 2.44 us -> 1.92 us  [on_device(): call(rest_kernel, (shape((2, R_DEV, C_DEV), bf16), shape((channels - 2, s...]
  transfers between devices with their start and end apart: 7 -> 6, of which waited for: 4 -> 3; matrix products, arithmetic and copies ran while one was open for 0% -> 0% of each run, Pallas kernels for 18% -> 15%
where the time goes in v5:
time: 47.4 us; the launch traced here: 46.8 us
  blocking collectives  13.5 us (28%)
  starting transfers between devices  13.3 us (28%)
  Pallas kernels  10.5 us (22%)
  waiting for transfers between devices  7.52 us (16%)
  between operations  1.37 us (3%)
  local copies, waits for them, and re-layouts  0.67 us (1%)
    all_to_all x1, blocking collectives, on_device(): lax.all_to_all(x, 'band', 0, 0, tiled=True, axis_index_groups=same_core)  13.5 us
    all_to_all x1, starting transfers between devices, on_device(): lax.all_to_all(x, 'band', 0, 0, tiled=True, axis_index_groups=same_core)  4.83 us
    ppermute x1, starting transfers between devices, on_device(): from_b = lax.ppermute(to_b, 'lon', ring_b)  4.23 us
    all_to_all x1, waiting for transfers between devices, on_device(): lax.all_to_all(x, 'band', 0, 0, tiled=True, axis_index_groups=same_core)  3.48 us
    ppermute x1, waiting for transfers between devices, on_device(): from_b = lax.ppermute(to_b, 'band', pairs_b)  2.32 us
    ppermute x1, starting transfers between devices, on_device(): from_a = lax.ppermute(to_a, 'band', pairs_a(bands))  2.21 us
    ppermute x1, starting transfers between devices, on_device(): from_b = lax.ppermute(to_b, 'band', pairs_b)  1.92 us
    pallas_call x1, Pallas kernels, on_device(): call(rest_kernel, (shape((2, R_DEV, C_DEV), bf16), shape((channels - 2, s...  1.92 us
  transfers between devices with their start and end apart: 6, of which 3 were waited for; matrix products, arithmetic and copies ran while one was open for 0% of the time, Pallas kernels for 15%

profile of v5, /device:TPU:2, one launch (start us, length us, event | category | flops | bytes accessed | tf_op | source)
XLA Modules:
  0.0 46.8 jit_solution(18161455232837661309)
XLA Ops:
  0.6 0.1 collective-permute-start
  0.7 1.2 %shard_map.68 = (s32[8,128]{1,0:T(8,128)S(1)}, s32[8,256]{1,0:T(8,128)S(1)}, bf16[6,512,128]{2,1,0:T(8,128)(2,1)S(1)}) custom-call(s32[1,256]{1,0:T(1,128)} %bitcast.9, bf16[6,512,128]{2,1,0:T(8,128)(2,1)} %src_hbm.1), custom_call_target="tpu_custom_call" | custom-call | tf_op jit(solution)/shard_map/pallas_call | solution.py:349
  1.9 13.5 %all_to_all.16 = s32[8,1,128]{2,1,0:T(1,128)S(1)} all-to-all(s32[8,1,128]{2,1,0:T(1,128)S(1)} %bitcast.7), channel_id=1, replica_groups={{0,16,32,48,64,80,96,112},{8,24,40,56,72,88,104,120},{1,17,33,49,65,81,..., dimensions={0} | all-to-all | bytes 8192 | tf_op jit(solution)/shard_map/all_to_all | solution.py:346
  15.3 0.0 collective-permute-done.mate_ref
  15.4 1.5 %shard_map.69.after_ref = bf16[8,192,128]{2,1,0:T(8,128)(2,1)} custom-call(s32[8,128]{1,0:T(8,128)S(1)} %bitcast.6, bf16[6,512,128]{2,1,0:T(8,128)(2,1)S(1)} %get-tuple-element.19.own_ref, bf16[6,512,128]{2,1,0:T(8,128)(2,1)S(1)} %collective-permute-done.mate_ref), custom_call_target="tpu_custom_call" | custom-call | tf_op jit(solution)/shard_map/pallas_call | solution.py:356
  16.8 4.8 %all-to-all-start.1 = ((bf16[8,192,128]{2,1,0:T(8,128)(2,1)}), bf16[8,192,128]{2,1,0:T(8,128)(2,1)S(1)}, u32[]{:S(2)}, u32[]{:S(2)}) async-start(bf16[8,192,128]{2,1,0:T(8,128)(2,1)} %shard_map.69.after_ref), calls=%async_computation.1 | async-start | bytes 786432 | tf_op jit(solution)/shard_map/all_to_all | solution.py:346
  22.3 0.0 copy-start
  22.3 0.7 %copy-done = s32[256]{0:T(256)S(1)} copy-done((s32[256]{0:T(256)S(1)}, s32[256]{0:T(256)}, u32[]{:S(2)}) %copy-start) | copy-done | bytes 1048
  23.0 1.1 %shard_map.70 = (bf16[256,256]{1,0:T(8,128)(2,1)S(1)}, bf16[128,256]{1,0:T(8,128)(2,1)S(1)}, bf16[32,256]{1,0:T(8,128)(2,1)S(1)}, s32[8,256]{1,0:T(8,128)S(4)}, f32[24,128]{1,0:T(8,128)S(1)}) custom-call(bf16[8,192,128]{2,1,0:T(8,128)(2,1)} %shard_map.69.after_ref, s32[1]{0:T(128)S(6)} %copy.8.live_ref, s32[8,256]{1,0:T(8,128)S(1)} %get-tuple-element.20.pos_ref, ...), custom_call_target="tpu_custom_call" | custom-call | flops 524288 | bytes 524288 | tf_op jit(solution)/shard_map/pallas_call | solution.py:363
  24.1 1.8 %shard_map.71.held_ref = bf16[88,128,128]{2,1,0:T(8,128)(2,1)S(1)} custom-call(s32[8,256]{1,0:T(8,128)S(4)} %get-tuple-element.21.order_ref.order, bf16[8,192,128]{2,1,0:T(8,128)(2,1)} %shard_map.69.after_ref, bf16[256,128,128]{2,1,0:T(8,128)(2,1)} %weight_hbm.5), custom_call_target="tpu_custom_call" | custom-call | flops 2883584 | bytes 2883584 | tf_op jit(solution)/shard_map/pallas_call | solution.py:380
  25.9 3.5 %all-to-all-done.1.recv_ref = bf16[8,192,128]{2,1,0:T(8,128)(2,1)S(1)} async-done(((bf16[8,192,128]{2,1,0:T(8,128)(2,1)}), bf16[8,192,128]{2,1,0:T(8,128)(2,1)S(1)}, u32[]{:S(2)}, u32[]{:S(2)}) %all-to-all-start.1) | async-done | bytes 393248 | tf_op jit(solution)/shard_map/all_to_all | solution.py:346
  29.4 0.9 %shard_map.72 = (bf16[32,128]{1,0:T(8,128)(2,1)S(1)}, bf16[32,128]{1,0:T(8,128)(2,1)S(1)}, f32[2,256,128]{2,1,0:T(8,128)S(1)}) custom-call(s32[8,256]{1,0:T(8,128)S(4)} %get-tuple-element.21.order_ref.order, bf16[8,192,128]{2,1,0:T(8,128)(2,1)S(1)} %all-to-all-done.1.recv_ref, bf16[256,256]{1,0:T(8,128)(2,1)S(1)} %get-tuple-element.22.perm_ref, ...), custom_call_target="tpu_custom_call" | custom-call | tf_op jit(solution)/shard_map/pallas_call | solution.py:393
  30.3 4.2 %collective-permute-start.2 = (bf16[32,128]{1,0:T(8,128)(2,1)S(1)}, bf16[32,128]{1,0:T(8,128)(2,1)S(1)}, u32[]{:S(2)}, u32[]{:S(2)}) collective-permute-start(bf16[32,128]{1,0:T(8,128)(2,1)S(1)} %get-tuple-element.28), channel_id=1, source_target_pairs={{0,7},{1,2},{2,1},{3,4},{4,3},{5,6},{6,5},{7,0},{8,15},{9,10},{10,... | collective-permute-start | bytes 24584 | tf_op jit(solution)/shard_map/ppermute | solution.py:412
  34.6 0.0 collective-permute-start.1
  34.6 1.9 %shard_map.73 = (bf16[2,16,1024]{2,1,0:T(8,128)(2,1)S(1)}, f32[4,256,128]{2,1,0:T(8,128)S(1)}) custom-call(bf16[32,128]{1,0:T(8,128)(2,1)S(1)} %get-tuple-element.24.after_ref, s32[8,256]{1,0:T(8,128)S(4)} %get-tuple-element.21.order_ref.order, bf16[8,192,128]{2,1,0:T(8,128)(2,1)S(1)} %all-to-all-done.1.recv_ref, ...), custom_call_target="tpu_custom_call" | custom-call | flops 4194304 | bytes 4194304 | tf_op jit(solution)/shard_map/pallas_call | solution.py:400
  36.5 0.0 collective-permute-done.2.from_b_ref
  36.5 1.7 %collective-permute-done.1.from_a_ref = bf16[32,128]{1,0:T(8,128)(2,1)S(1)} collective-permute-done((bf16[32,128]{1,0:T(8,128)(2,1)S(1)}, bf16[32,128]{1,0:T(8,128)(2,1)S(1)}, u32[]{:S(2)}, u32[]{:S(2)}) %collective-permute-start.1) | collective-permute-done | bytes 8224 | tf_op jit(solution)/shard_map/ppermute | solution.py:411
  38.3 1.9 %collective-permute-start.4 = (bf16[8,1280]{1,0:T(8,128)(2,1)S(1)}, bf16[8,1280]{1,0:T(8,128)(2,1)S(1)}, u32[]{:S(2)}, u32[]{:S(2)}) collective-permute-start(bf16[8,1280]{1,0:T(8,128)(2,1)S(1)} %get-tuple-element.33), channel_id=1, source_target_pairs={{8,16},{16,8},{24,32},{32,24},{40,48},{48,40},{56,64},{64,56},{72,... | collective-permute-start | bytes 61448 | tf_op jit(solution)/shard_map/ppermute | solution.py:420
  40.2 2.2 %collective-permute-start.3 = (bf16[8,1280]{1,0:T(8,128)(2,1)S(1)}, bf16[8,1280]{1,0:T(8,128)(2,1)S(1)}, u32[]{:S(2)}, u32[]{:S(2)}) collective-permute-start(bf16[8,1280]{1,0:T(8,128)(2,1)S(1)} %get-tuple-element.29.after_ref), channel_id=1, source_target_pairs={{0,8},{8,0},{16,24},{24,16},{32,40},{40,32},{48,56},{56,48},{64,72... | collective-permute-start | bytes 61448 | tf_op jit(solution)/shard_map/ppermute | solution.py:419
  42.4 1.0 %shard_map.75 = bf16[6,16,1024]{2,1,0:T(8,128)(2,1)} custom-call(bf16[8,1280]{1,0:T(8,128)(2,1)S(1)} %get-tuple-element.29.after_ref, bf16[128,256]{1,0:T(8,128)(2,1)S(1)} %get-tuple-element.25.chosen_ref, f32[4,256,128]{2,1,0:T(8,128)S(1)} %get-tuple-element.30.others_ref, bf16[2,16,1024]{2,1,0:T(8,128)(2,1)S(1)} %get-tuple-element.27.wind_ref), custom_call_target="tpu_custom_call" | custom-call | flops 1048576 | bytes 1048576 | tf_op jit(solution)/shard_map/pallas_call | solution.py:416
  43.4 2.3 %collective-permute-done.4.from_b_ref = bf16[8,1280]{1,0:T(8,128)(2,1)S(1)} collective-permute-done((bf16[8,1280]{1,0:T(8,128)(2,1)S(1)}, bf16[8,1280]{1,0:T(8,128)(2,1)S(1)}, u32[]{:S(2)}, u32[]{:S(2)}) %collective-permute-start.4) | collective-permute-done | bytes 20512 | tf_op jit(solution)/shard_map/ppermute | solution.py:420
  45.8 0.0 collective-permute-done.3.from_a_ref
  45.8 1.0 %shard_map.76 = f32[16,1024]{1,0:T(8,128)} custom-call(f32[24,128]{1,0:T(8,128)S(1)} %get-tuple-element.31.cosine_ref, f32[2,16,1280]{2,1,0:T(8,128)S(1)} %get-tuple-element.32.ext_ref, bf16[8,1280]{1,0:T(8,128)(2,1)S(1)} %collective-permute-done.3.from_a_ref, bf16[8,1280]{1,0:T(8,128)(2,1)S(1)} %collective-permute-done.4.from_b_ref), custom_call_target="tpu_custom_call" | custom-call | tf_op jit(solution)/shard_map/pallas_call | solution.py:421
  (1 shorter events, 0.0 us)
Async XLA Ops:
  0.6 14.7 %collective-permute-start = (bf16[6,512,128]{2,1,0:T(8,128)(2,1)}, bf16[6,512,128]{2,1,0:T(8,128)(2,1)S(1)}, u32[]{:S(2)}, u32[]{:S(2)}) collective-permute-start(bf16[6,512,128]{2,1,0:T(8,128)(2,1)} %src_hbm.1), channel_id=1, source_target_pairs={{0,8},{8,0},{16,24},{24,16},{32,40},{40,32},{48,56},{56,48},{64,72... | collective-permute-start | bytes 2359304 | tf_op jit(solution)/shard_map/ppermute | solution.py:348
  16.8 12.6 %all-to-all-start.1 = ((bf16[8,192,128]{2,1,0:T(8,128)(2,1)}), bf16[8,192,128]{2,1,0:T(8,128)(2,1)S(1)}, u32[]{:S(2)}, u32[]{:S(2)}) async-start(bf16[8,192,128]{2,1,0:T(8,128)(2,1)} %shard_map.69.after_ref), calls=%async_computation.1 | async-start | bytes 786432 | tf_op jit(solution)/shard_map/all_to_all | solution.py:346
  22.3 0.7 %copy-start = (s32[256]{0:T(256)S(1)}, s32[256]{0:T(256)}, u32[]{:S(2)}) copy-start(s32[256]{0:T(256)} %param.7) | copy-start | bytes 3076
  30.3 6.2 %collective-permute-start.2 = (bf16[32,128]{1,0:T(8,128)(2,1)S(1)}, bf16[32,128]{1,0:T(8,128)(2,1)S(1)}, u32[]{:S(2)}, u32[]{:S(2)}) collective-permute-start(bf16[32,128]{1,0:T(8,128)(2,1)S(1)} %get-tuple-element.28), channel_id=1, source_target_pairs={{0,7},{1,2},{2,1},{3,4},{4,3},{5,6},{6,5},{7,0},{8,15},{9,10},{10,... | collective-permute-start | bytes 24584 | tf_op jit(solution)/shard_map/ppermute | solution.py:412
  34.6 3.7 %collective-permute-start.1 = (bf16[32,128]{1,0:T(8,128)(2,1)S(1)}, bf16[32,128]{1,0:T(8,128)(2,1)S(1)}, u32[]{:S(2)}, u32[]{:S(2)}) collective-permute-start(bf16[32,128]{1,0:T(8,128)(2,1)S(1)} %get-tuple-element.24.after_ref), channel_id=1, source_target_pairs={{0,1},{1,0},{2,3},{3,2},{4,5},{5,4},{6,7},{7,6},{8,9},{9,8},{10,11... | collective-permute-start | bytes 24584 | tf_op jit(solution)/shard_map/ppermute | solution.py:411
  38.3 7.5 %collective-permute-start.4 = (bf16[8,1280]{1,0:T(8,128)(2,1)S(1)}, bf16[8,1280]{1,0:T(8,128)(2,1)S(1)}, u32[]{:S(2)}, u32[]{:S(2)}) collective-permute-start(bf16[8,1280]{1,0:T(8,128)(2,1)S(1)} %get-tuple-element.33), channel_id=1, source_target_pairs={{8,16},{16,8},{24,32},{32,24},{40,48},{48,40},{56,64},{64,56},{72,... | collective-permute-start | bytes 61448 | tf_op jit(solution)/shard_map/ppermute | solution.py:420
  40.2 5.6 %collective-permute-start.3 = (bf16[8,1280]{1,0:T(8,128)(2,1)S(1)}, bf16[8,1280]{1,0:T(8,128)(2,1)S(1)}, u32[]{:S(2)}, u32[]{:S(2)}) collective-permute-start(bf16[8,1280]{1,0:T(8,128)(2,1)S(1)} %get-tuple-element.29.after_ref), channel_id=1, source_target_pairs={{0,8},{8,0},{16,24},{24,16},{32,40},{40,32},{48,56},{56,48},{64,72... | collective-permute-start | bytes 61448 | tf_op jit(solution)/shard_map/ppermute | solution.py:419

commit v6 on v5

--- a/solution.py
+++ b/solution.py
@@ -404,7 +404,7 @@
         [weight, per_slot(channels), per_slot(2), dmas((chunks,))],
         vmem=12 << 20,
         cycles=slots * pixels * BW,
-    )(to_a, order, recv, perm, chosen, term, weight_held, weight_hbm)
+    )(to_b, order, recv, perm, chosen, term, weight_held, weight_hbm)
 
     pairs_b = [(i, i + 1 if i % 2 else i - 1) for i in range(1, bands - 1)]
     ring_b = [(i, (i + 1 if i % 2 else i - 1) % lons) for i in range(lons)]

time: 47.4 us -> 47.3 us (level)
  Pallas kernels: 10.5 us -> 11.3 us
  waiting for transfers between devices: 7.52 us -> 6.77 us
    ppermute x1, starting transfers between devices: 0.01 us -> 2 us  [on_device(): from_a = lax.ppermute(to_a, 'lon', pairs_a(lons))]
    ppermute x1, waiting for transfers between devices: 1.71 us -> 0.01 us  [on_device(): from_a = lax.ppermute(to_a, 'lon', pairs_a(lons))]
    ppermute x1, starting transfers between devices: 4.23 us -> 2.63 us  [on_device(): from_b = lax.ppermute(to_b, 'lon', ring_b)]
    pallas_call x1, Pallas kernels: 1.92 us -> 2.75 us  [on_device(): call(rest_kernel, (shape((2, R_DEV, C_DEV), bf16), shape((channels - 2, s...]
    ppermute x1, waiting for transfers between devices: 2.32 us -> 2.93 us  [on_device(): from_b = lax.ppermute(to_b, 'band', pairs_b)]
    ppermute x1, starting transfers between devices: 2.21 us -> 1.6 us  [on_device(): from_a = lax.ppermute(to_a, 'band', pairs_a(bands))]
  transfers between devices with their start and end apart: 6 -> 6, of which waited for: 3 -> 3; matrix products, arithmetic and copies ran while one was open for 0% -> 0% of each run, Pallas kernels for 15% -> 17%
where the time goes in v6:
time: 47.3 us; the launch traced here: 46.7 us
  blocking collectives  13.5 us (29%)
  starting transfers between devices  13.1 us (28%)
  Pallas kernels  11.3 us (24%)
  waiting for transfers between devices  6.77 us (14%)
  between operations  1.37 us (3%)
  local copies, waits for them, and re-layouts  0.67 us (1%)
    all_to_all x1, blocking collectives, on_device(): lax.all_to_all(x, 'band', 0, 0, tiled=True, axis_index_groups=same_core)  13.5 us
    all_to_all x1, starting transfers between devices, on_device(): lax.all_to_all(x, 'band', 0, 0, tiled=True, axis_index_groups=same_core)  4.83 us
    all_to_all x1, waiting for transfers between devices, on_device(): lax.all_to_all(x, 'band', 0, 0, tiled=True, axis_index_groups=same_core)  3.48 us
    ppermute x1, waiting for transfers between devices, on_device(): from_b = lax.ppermute(to_b, 'band', pairs_b)  2.93 us
    pallas_call x1, Pallas kernels, on_device(): call(rest_kernel, (shape((2, R_DEV, C_DEV), bf16), shape((channels - 2, s...  2.75 us
    ppermute x1, starting transfers between devices, on_device(): from_b = lax.ppermute(to_b, 'lon', ring_b)  2.63 us
    ppermute x1, starting transfers between devices, on_device(): from_a = lax.ppermute(to_a, 'lon', pairs_a(lons))  2 us
    ppermute x1, starting transfers between devices, on_device(): from_b = lax.ppermute(to_b, 'band', pairs_b)  1.92 us
  transfers between devices with their start and end apart: 6, of which 3 were waited for; matrix products, arithmetic and copies ran while one was open for 0% of the time, Pallas kernels for 17%

profile of v6, /device:TPU:2, one launch (start us, length us, event | category | flops | bytes accessed | tf_op | source)
XLA Modules:
  0.0 46.7 jit_solution(5659404567889802424)
XLA Ops:
  0.6 0.1 collective-permute-start
  0.7 1.2 %shard_map.68 = (s32[8,128]{1,0:T(8,128)S(1)}, s32[8,256]{1,0:T(8,128)S(1)}, bf16[6,512,128]{2,1,0:T(8,128)(2,1)S(1)}) custom-call(s32[1,256]{1,0:T(1,128)} %bitcast.9, bf16[6,512,128]{2,1,0:T(8,128)(2,1)} %src_hbm.1), custom_call_target="tpu_custom_call" | custom-call | tf_op jit(solution)/shard_map/pallas_call | solution.py:349
  1.9 13.5 %all_to_all.16 = s32[8,1,128]{2,1,0:T(1,128)S(1)} all-to-all(s32[8,1,128]{2,1,0:T(1,128)S(1)} %bitcast.7), channel_id=1, replica_groups={{0,16,32,48,64,80,96,112},{8,24,40,56,72,88,104,120},{1,17,33,49,65,81,..., dimensions={0} | all-to-all | bytes 8192 | tf_op jit(solution)/shard_map/all_to_all | solution.py:346
  15.3 0.0 collective-permute-done.mate_ref
  15.4 1.5 %shard_map.69.after_ref = bf16[8,192,128]{2,1,0:T(8,128)(2,1)} custom-call(s32[8,128]{1,0:T(8,128)S(1)} %bitcast.6, bf16[6,512,128]{2,1,0:T(8,128)(2,1)S(1)} %get-tuple-element.19.own_ref, bf16[6,512,128]{2,1,0:T(8,128)(2,1)S(1)} %collective-permute-done.mate_ref), custom_call_target="tpu_custom_call" | custom-call | tf_op jit(solution)/shard_map/pallas_call | solution.py:356
  16.8 4.8 %all-to-all-start.1 = ((bf16[8,192,128]{2,1,0:T(8,128)(2,1)}), bf16[8,192,128]{2,1,0:T(8,128)(2,1)S(1)}, u32[]{:S(2)}, u32[]{:S(2)}) async-start(bf16[8,192,128]{2,1,0:T(8,128)(2,1)} %shard_map.69.after_ref), calls=%async_computation.1 | async-start | bytes 786432 | tf_op jit(solution)/shard_map/all_to_all | solution.py:346
  22.3 0.0 copy-start
  22.3 0.7 %copy-done = s32[256]{0:T(256)S(1)} copy-done((s32[256]{0:T(256)S(1)}, s32[256]{0:T(256)}, u32[]{:S(2)}) %copy-start) | copy-done | bytes 1048
  23.0 1.1 %shard_map.70 = (bf16[256,256]{1,0:T(8,128)(2,1)S(1)}, bf16[128,256]{1,0:T(8,128)(2,1)S(1)}, bf16[32,256]{1,0:T(8,128)(2,1)S(1)}, s32[8,256]{1,0:T(8,128)S(4)}, f32[24,128]{1,0:T(8,128)S(1)}) custom-call(bf16[8,192,128]{2,1,0:T(8,128)(2,1)} %shard_map.69.after_ref, s32[1]{0:T(128)S(6)} %copy.8.live_ref, s32[8,256]{1,0:T(8,128)S(1)} %get-tuple-element.20.pos_ref, ...), custom_call_target="tpu_custom_call" | custom-call | flops 524288 | bytes 524288 | tf_op jit(solution)/shard_map/pallas_call | solution.py:363
  24.1 1.8 %shard_map.71.held_ref = bf16[88,128,128]{2,1,0:T(8,128)(2,1)S(1)} custom-call(s32[8,256]{1,0:T(8,128)S(4)} %get-tuple-element.21.order_ref.order, bf16[8,192,128]{2,1,0:T(8,128)(2,1)} %shard_map.69.after_ref, bf16[256,128,128]{2,1,0:T(8,128)(2,1)} %weight_hbm.5), custom_call_target="tpu_custom_call" | custom-call | flops 2883584 | bytes 2883584 | tf_op jit(solution)/shard_map/pallas_call | solution.py:380
  25.9 3.5 %all-to-all-done.1.recv_ref = bf16[8,192,128]{2,1,0:T(8,128)(2,1)S(1)} async-done(((bf16[8,192,128]{2,1,0:T(8,128)(2,1)}), bf16[8,192,128]{2,1,0:T(8,128)(2,1)S(1)}, u32[]{:S(2)}, u32[]{:S(2)}) %all-to-all-start.1) | async-done | bytes 393248 | tf_op jit(solution)/shard_map/all_to_all | solution.py:346
  29.4 0.9 %shard_map.72 = (bf16[32,128]{1,0:T(8,128)(2,1)S(1)}, bf16[32,128]{1,0:T(8,128)(2,1)S(1)}, f32[2,256,128]{2,1,0:T(8,128)S(1)}) custom-call(s32[8,256]{1,0:T(8,128)S(4)} %get-tuple-element.21.order_ref.order, bf16[8,192,128]{2,1,0:T(8,128)(2,1)S(1)} %all-to-all-done.1.recv_ref, bf16[256,256]{1,0:T(8,128)(2,1)S(1)} %get-tuple-element.22.perm_ref, ...), custom_call_target="tpu_custom_call" | custom-call | tf_op jit(solution)/shard_map/pallas_call | solution.py:393
  30.3 2.0 %collective-permute-start.1 = (bf16[32,128]{1,0:T(8,128)(2,1)S(1)}, bf16[32,128]{1,0:T(8,128)(2,1)S(1)}, u32[]{:S(2)}, u32[]{:S(2)}) collective-permute-start(bf16[32,128]{1,0:T(8,128)(2,1)S(1)} %get-tuple-element.28), channel_id=1, source_target_pairs={{0,1},{1,0},{2,3},{3,2},{4,5},{5,4},{6,7},{7,6},{8,9},{9,8},{10,11... | collective-permute-start | bytes 24584 | tf_op jit(solution)/shard_map/ppermute | solution.py:411
  32.3 2.6 %collective-permute-start.2 = (bf16[32,128]{1,0:T(8,128)(2,1)S(1)}, bf16[32,128]{1,0:T(8,128)(2,1)S(1)}, u32[]{:S(2)}, u32[]{:S(2)}) collective-permute-start(bf16[32,128]{1,0:T(8,128)(2,1)S(1)} %get-tuple-element.24.after_ref), channel_id=1, source_target_pairs={{0,7},{1,2},{2,1},{3,4},{4,3},{5,6},{6,5},{7,0},{8,15},{9,10},{10,... | collective-permute-start | bytes 24584 | tf_op jit(solution)/shard_map/ppermute | solution.py:412
  35.0 2.8 %shard_map.73 = (bf16[2,16,1024]{2,1,0:T(8,128)(2,1)S(1)}, f32[4,256,128]{2,1,0:T(8,128)S(1)}) custom-call(bf16[32,128]{1,0:T(8,128)(2,1)S(1)} %get-tuple-element.24.after_ref, s32[8,256]{1,0:T(8,128)S(4)} %get-tuple-element.21.order_ref.order, bf16[8,192,128]{2,1,0:T(8,128)(2,1)S(1)} %all-to-all-done.1.recv_ref, ...), custom_call_target="tpu_custom_call" | custom-call | flops 4194304 | bytes 4194304 | tf_op jit(solution)/shard_map/pallas_call | solution.py:400
  37.7 0.0 collective-permute-done.1.from_a_ref
  37.7 0.4 collective-permute-done.2.from_b_ref
  38.1 1.9 %collective-permute-start.4 = (bf16[8,1280]{1,0:T(8,128)(2,1)S(1)}, bf16[8,1280]{1,0:T(8,128)(2,1)S(1)}, u32[]{:S(2)}, u32[]{:S(2)}) collective-permute-start(bf16[8,1280]{1,0:T(8,128)(2,1)S(1)} %get-tuple-element.33), channel_id=1, source_target_pairs={{8,16},{16,8},{24,32},{32,24},{40,48},{48,40},{56,64},{64,56},{72,... | collective-permute-start | bytes 61448 | tf_op jit(solution)/shard_map/ppermute | solution.py:420
  40.1 1.6 %collective-permute-start.3 = (bf16[8,1280]{1,0:T(8,128)(2,1)S(1)}, bf16[8,1280]{1,0:T(8,128)(2,1)S(1)}, u32[]{:S(2)}, u32[]{:S(2)}) collective-permute-start(bf16[8,1280]{1,0:T(8,128)(2,1)S(1)} %get-tuple-element.29.after_ref), channel_id=1, source_target_pairs={{0,8},{8,0},{16,24},{24,16},{32,40},{40,32},{48,56},{56,48},{64,72... | collective-permute-start | bytes 61448 | tf_op jit(solution)/shard_map/ppermute | solution.py:419
  41.7 1.0 %shard_map.75 = bf16[6,16,1024]{2,1,0:T(8,128)(2,1)} custom-call(bf16[8,1280]{1,0:T(8,128)(2,1)S(1)} %get-tuple-element.29.after_ref, bf16[128,256]{1,0:T(8,128)(2,1)S(1)} %get-tuple-element.25.chosen_ref, f32[4,256,128]{2,1,0:T(8,128)S(1)} %get-tuple-element.30.others_ref, bf16[2,16,1024]{2,1,0:T(8,128)(2,1)S(1)} %get-tuple-element.27.wind_ref), custom_call_target="tpu_custom_call" | custom-call | flops 1048576 | bytes 1048576 | tf_op jit(solution)/shard_map/pallas_call | solution.py:416
  42.7 2.9 %collective-permute-done.4.from_b_ref = bf16[8,1280]{1,0:T(8,128)(2,1)S(1)} collective-permute-done((bf16[8,1280]{1,0:T(8,128)(2,1)S(1)}, bf16[8,1280]{1,0:T(8,128)(2,1)S(1)}, u32[]{:S(2)}, u32[]{:S(2)}) %collective-permute-start.4) | collective-permute-done | bytes 20512 | tf_op jit(solution)/shard_map/ppermute | solution.py:420
  45.6 0.0 collective-permute-done.3.from_a_ref
  45.6 1.0 %shard_map.76 = f32[16,1024]{1,0:T(8,128)} custom-call(f32[24,128]{1,0:T(8,128)S(1)} %get-tuple-element.31.cosine_ref, f32[2,16,1280]{2,1,0:T(8,128)S(1)} %get-tuple-element.32.ext_ref, bf16[8,1280]{1,0:T(8,128)(2,1)S(1)} %collective-permute-done.3.from_a_ref, bf16[8,1280]{1,0:T(8,128)(2,1)S(1)} %collective-permute-done.4.from_b_ref), custom_call_target="tpu_custom_call" | custom-call | tf_op jit(solution)/shard_map/pallas_call | solution.py:421
  (1 shorter events, 0.0 us)
Async XLA Ops:
  0.6 14.7 %collective-permute-start = (bf16[6,512,128]{2,1,0:T(8,128)(2,1)}, bf16[6,512,128]{2,1,0:T(8,128)(2,1)S(1)}, u32[]{:S(2)}, u32[]{:S(2)}) collective-permute-start(bf16[6,512,128]{2,1,0:T(8,128)(2,1)} %src_hbm.1), channel_id=1, source_target_pairs={{0,8},{8,0},{16,24},{24,16},{32,40},{40,32},{48,56},{56,48},{64,72... | collective-permute-start | bytes 2359304 | tf_op jit(solution)/shard_map/ppermute | solution.py:348
  16.8 12.6 %all-to-all-start.1 = ((bf16[8,192,128]{2,1,0:T(8,128)(2,1)}), bf16[8,192,128]{2,1,0:T(8,128)(2,1)S(1)}, u32[]{:S(2)}, u32[]{:S(2)}) async-start(bf16[8,192,128]{2,1,0:T(8,128)(2,1)} %shard_map.69.after_ref), calls=%async_computation.1 | async-start | bytes 786432 | tf_op jit(solution)/shard_map/all_to_all | solution.py:346
  22.3 0.7 %copy-start = (s32[256]{0:T(256)S(1)}, s32[256]{0:T(256)}, u32[]{:S(2)}) copy-start(s32[256]{0:T(256)} %param.7) | copy-start | bytes 3076
  30.3 7.4 %collective-permute-start.1 = (bf16[32,128]{1,0:T(8,128)(2,1)S(1)}, bf16[32,128]{1,0:T(8,128)(2,1)S(1)}, u32[]{:S(2)}, u32[]{:S(2)}) collective-permute-start(bf16[32,128]{1,0:T(8,128)(2,1)S(1)} %get-tuple-element.28), channel_id=1, source_target_pairs={{0,1},{1,0},{2,3},{3,2},{4,5},{5,4},{6,7},{7,6},{8,9},{9,8},{10,11... | collective-permute-start | bytes 24584 | tf_op jit(solution)/shard_map/ppermute | solution.py:411
  32.3 5.8 %collective-permute-start.2 = (bf16[32,128]{1,0:T(8,128)(2,1)S(1)}, bf16[32,128]{1,0:T(8,128)(2,1)S(1)}, u32[]{:S(2)}, u32[]{:S(2)}) collective-permute-start(bf16[32,128]{1,0:T(8,128)(2,1)S(1)} %get-tuple-element.24.after_ref), channel_id=1, source_target_pairs={{0,7},{1,2},{2,1},{3,4},{4,3},{5,6},{6,5},{7,0},{8,15},{9,10},{10,... | collective-permute-start | bytes 24584 | tf_op jit(solution)/shard_map/ppermute | solution.py:412
  38.1 7.5 %collective-permute-start.4 = (bf16[8,1280]{1,0:T(8,128)(2,1)S(1)}, bf16[8,1280]{1,0:T(8,128)(2,1)S(1)}, u32[]{:S(2)}, u32[]{:S(2)}) collective-permute-start(bf16[8,1280]{1,0:T(8,128)(2,1)S(1)} %get-tuple-element.33), channel_id=1, source_target_pairs={{8,16},{16,8},{24,32},{32,24},{40,48},{48,40},{56,64},{64,56},{72,... | collective-permute-start | bytes 61448 | tf_op jit(solution)/shard_map/ppermute | solution.py:420
  40.1 5.6 %collective-permute-start.3 = (bf16[8,1280]{1,0:T(8,128)(2,1)S(1)}, bf16[8,1280]{1,0:T(8,128)(2,1)S(1)}, u32[]{:S(2)}, u32[]{:S(2)}) collective-permute-start(bf16[8,1280]{1,0:T(8,128)(2,1)S(1)} %get-tuple-element.29.after_ref), channel_id=1, source_target_pairs={{0,8},{8,0},{16,24},{24,16},{32,40},{40,32},{48,56},{56,48},{64,72... | collective-permute-start | bytes 61448 | tf_op jit(solution)/shard_map/ppermute | solution.py:419

commit v7 on v6

--- a/solution.py
+++ b/solution.py
@@ -15,6 +15,7 @@
 LAT_START = 0.5
 HALO = 3
 HELD = 88
+FIRST = 56
 CHUNK = 24
 EXT = 24
 
@@ -226,8 +227,14 @@
         order_tiles(xs, perm_ref, recv_ref, (2, 3), half, half)
 
     for term in terms:
-        term[HELD:slots, :] = jnp.zeros((slots - HELD, 128), jnp.float32)
-    multiply(xs, lambda g: held_ref[g : g + 8].reshape(8 * 128, 128), terms, 0, HELD)
+        term[FIRST:slots, :] = jnp.zeros((slots - FIRST, 128), jnp.float32)
+    multiply(xs, lambda g: held_ref[g : g + 8].reshape(8 * 128, 128), terms, 0, FIRST)
+
+    @pl.when(order[1, 0] > FIRST)
+    def _():
+        eight = lambda g: held_ref[FIRST + g : FIRST + g + 8].reshape(8 * 128, 128)
+        multiply(xs, eight, terms, FIRST, HELD - FIRST)
+
     lax.fori_loop(0, chunks, step, 0)
     winds = [add_terms(rim_ref[...], term[...]) for term in terms]
     left = jnp.concatenate([w[:R_DEV] for w in winds], axis=0)
@@ -252,9 +259,10 @@
     for target in terms:
         target[HELD:slots, :] = jnp.zeros((slots - HELD, 128), jnp.float32)
     for w in range(2):
-        term[w, :HELD] = term_ref[w, :HELD]
+        term[w, :FIRST] = term_ref[w, :FIRST]
     eight = lambda g: held_ref[g : g + 8].reshape(8 * 128, 128)
-    multiply(xs, eight, terms, 0, HELD, [c for c in range(channels) if c not in (2, 3)])
+    multiply(xs, eight, terms, 0, FIRST, [c for c in range(channels) if c not in (2, 3)])
+    multiply(xs, lambda g: eight(FIRST + g), terms, FIRST, HELD - FIRST)
     lax.fori_loop(0, last, step, 0)
     for w in range(2):
         wind_ref[w] = add_blocks(chosen_ref[...], term[w])

time: 47.3 us -> 47.1 us (level)
  transfers between devices with their start and end apart: 6 -> 6, of which waited for: 3 -> 3; matrix products, arithmetic and copies ran while one was open for 0% -> 0% of each run, Pallas kernels for 17% -> 16%
where the time goes in v7:
time: 47.1 us; the launch traced here: 46.5 us
  blocking collectives  13.5 us (29%)
  starting transfers between devices  13.1 us (28%)
  Pallas kernels  10.9 us (23%)
  waiting for transfers between devices  7.1 us (15%)
  between operations  1.37 us (3%)
  local copies, waits for them, and re-layouts  0.67 us (1%)
    all_to_all x1, blocking collectives, on_device(): lax.all_to_all(x, 'band', 0, 0, tiled=True, axis_index_groups=same_core)  13.5 us
    all_to_all x1, starting transfers between devices, on_device(): lax.all_to_all(x, 'band', 0, 0, tiled=True, axis_index_groups=same_core)  4.83 us
    all_to_all x1, waiting for transfers between devices, on_device(): lax.all_to_all(x, 'band', 0, 0, tiled=True, axis_index_groups=same_core)  3.48 us
    ppermute x1, waiting for transfers between devices, on_device(): from_b = lax.ppermute(to_b, 'band', pairs_b)  2.93 us
    ppermute x1, starting transfers between devices, on_device(): from_b = lax.ppermute(to_b, 'lon', ring_b)  2.63 us
    pallas_call x1, Pallas kernels, on_device(): call(rest_kernel, (shape((2, R_DEV, C_DEV), bf16), shape((channels - 2, s...  2.43 us
    ppermute x1, starting transfers between devices, on_device(): from_a = lax.ppermute(to_a, 'lon', pairs_a(lons))  2 us
    ppermute x1, starting transfers between devices, on_device(): from_b = lax.ppermute(to_b, 'band', pairs_b)  1.92 us
  transfers between devices with their start and end apart: 6, of which 3 were waited for; matrix products, arithmetic and copies ran while one was open for 0% of the time, Pallas kernels for 16%

profile of v7, /device:TPU:2, one launch (start us, length us, event | category | flops | bytes accessed | tf_op | source)
XLA Modules:
  0.0 46.5 jit_solution(9571114515138541419)
XLA Ops:
  0.6 0.1 collective-permute-start
  0.7 1.2 %shard_map.68 = (s32[8,128]{1,0:T(8,128)S(1)}, s32[8,256]{1,0:T(8,128)S(1)}, bf16[6,512,128]{2,1,0:T(8,128)(2,1)S(1)}) custom-call(s32[1,256]{1,0:T(1,128)} %bitcast.9, bf16[6,512,128]{2,1,0:T(8,128)(2,1)} %src_hbm.1), custom_call_target="tpu_custom_call" | custom-call | tf_op jit(solution)/shard_map/pallas_call | solution.py:357
  1.9 13.5 %all_to_all.16 = s32[8,1,128]{2,1,0:T(1,128)S(1)} all-to-all(s32[8,1,128]{2,1,0:T(1,128)S(1)} %bitcast.7), channel_id=1, replica_groups={{0,16,32,48,64,80,96,112},{8,24,40,56,72,88,104,120},{1,17,33,49,65,81,..., dimensions={0} | all-to-all | bytes 8192 | tf_op jit(solution)/shard_map/all_to_all | solution.py:354
  15.3 0.0 collective-permute-done.mate_ref
  15.4 1.5 %shard_map.69.after_ref = bf16[8,192,128]{2,1,0:T(8,128)(2,1)} custom-call(s32[8,128]{1,0:T(8,128)S(1)} %bitcast.6, bf16[6,512,128]{2,1,0:T(8,128)(2,1)S(1)} %get-tuple-element.19.own_ref, bf16[6,512,128]{2,1,0:T(8,128)(2,1)S(1)} %collective-permute-done.mate_ref), custom_call_target="tpu_custom_call" | custom-call | tf_op jit(solution)/shard_map/pallas_call | solution.py:364
  16.8 4.8 %all-to-all-start.1 = ((bf16[8,192,128]{2,1,0:T(8,128)(2,1)}), bf16[8,192,128]{2,1,0:T(8,128)(2,1)S(1)}, u32[]{:S(2)}, u32[]{:S(2)}) async-start(bf16[8,192,128]{2,1,0:T(8,128)(2,1)} %shard_map.69.after_ref), calls=%async_computation.1 | async-start | bytes 786432 | tf_op jit(solution)/shard_map/all_to_all | solution.py:354
  22.3 0.0 copy-start
  22.3 0.7 %copy-done = s32[256]{0:T(256)S(1)} copy-done((s32[256]{0:T(256)S(1)}, s32[256]{0:T(256)}, u32[]{:S(2)}) %copy-start) | copy-done | bytes 1048
  23.0 1.1 %shard_map.70 = (bf16[256,256]{1,0:T(8,128)(2,1)S(1)}, bf16[128,256]{1,0:T(8,128)(2,1)S(1)}, bf16[32,256]{1,0:T(8,128)(2,1)S(1)}, s32[8,256]{1,0:T(8,128)S(4)}, f32[24,128]{1,0:T(8,128)S(1)}) custom-call(bf16[8,192,128]{2,1,0:T(8,128)(2,1)} %shard_map.69.after_ref, s32[1]{0:T(128)S(6)} %copy.8.live_ref, s32[8,256]{1,0:T(8,128)S(1)} %get-tuple-element.20.pos_ref, ...), custom_call_target="tpu_custom_call" | custom-call | flops 524288 | bytes 524288 | tf_op jit(solution)/shard_map/pallas_call | solution.py:371
  24.1 1.8 %shard_map.71.held_ref = bf16[88,128,128]{2,1,0:T(8,128)(2,1)S(1)} custom-call(s32[8,256]{1,0:T(8,128)S(4)} %get-tuple-element.21.order_ref.order, bf16[8,192,128]{2,1,0:T(8,128)(2,1)} %shard_map.69.after_ref, bf16[256,128,128]{2,1,0:T(8,128)(2,1)} %weight_hbm.5), custom_call_target="tpu_custom_call" | custom-call | flops 2883584 | bytes 2883584 | tf_op jit(solution)/shard_map/pallas_call | solution.py:388
  25.9 3.5 %all-to-all-done.1.recv_ref = bf16[8,192,128]{2,1,0:T(8,128)(2,1)S(1)} async-done(((bf16[8,192,128]{2,1,0:T(8,128)(2,1)}), bf16[8,192,128]{2,1,0:T(8,128)(2,1)S(1)}, u32[]{:S(2)}, u32[]{:S(2)}) %all-to-all-start.1) | async-done | bytes 393248 | tf_op jit(solution)/shard_map/all_to_all | solution.py:354
  29.4 0.8 %shard_map.72 = (bf16[32,128]{1,0:T(8,128)(2,1)S(1)}, bf16[32,128]{1,0:T(8,128)(2,1)S(1)}, f32[2,256,128]{2,1,0:T(8,128)S(1)}) custom-call(s32[8,256]{1,0:T(8,128)S(4)} %get-tuple-element.21.order_ref.order, bf16[8,192,128]{2,1,0:T(8,128)(2,1)S(1)} %all-to-all-done.1.recv_ref, bf16[256,256]{1,0:T(8,128)(2,1)S(1)} %get-tuple-element.22.perm_ref, ...), custom_call_target="tpu_custom_call" | custom-call | tf_op jit(solution)/shard_map/pallas_call | solution.py:401
  30.2 2.0 %collective-permute-start.1 = (bf16[32,128]{1,0:T(8,128)(2,1)S(1)}, bf16[32,128]{1,0:T(8,128)(2,1)S(1)}, u32[]{:S(2)}, u32[]{:S(2)}) collective-permute-start(bf16[32,128]{1,0:T(8,128)(2,1)S(1)} %get-tuple-element.28), channel_id=1, source_target_pairs={{0,1},{1,0},{2,3},{3,2},{4,5},{5,4},{6,7},{7,6},{8,9},{9,8},{10,11... | collective-permute-start | bytes 24584 | tf_op jit(solution)/shard_map/ppermute | solution.py:419
  32.2 2.6 %collective-permute-start.2 = (bf16[32,128]{1,0:T(8,128)(2,1)S(1)}, bf16[32,128]{1,0:T(8,128)(2,1)S(1)}, u32[]{:S(2)}, u32[]{:S(2)}) collective-permute-start(bf16[32,128]{1,0:T(8,128)(2,1)S(1)} %get-tuple-element.24.after_ref), channel_id=1, source_target_pairs={{0,7},{1,2},{2,1},{3,4},{4,3},{5,6},{6,5},{7,0},{8,15},{9,10},{10,... | collective-permute-start | bytes 24584 | tf_op jit(solution)/shard_map/ppermute | solution.py:420
  34.8 2.4 %shard_map.73 = (bf16[2,16,1024]{2,1,0:T(8,128)(2,1)S(1)}, f32[4,256,128]{2,1,0:T(8,128)S(1)}) custom-call(bf16[32,128]{1,0:T(8,128)(2,1)S(1)} %get-tuple-element.24.after_ref, s32[8,256]{1,0:T(8,128)S(4)} %get-tuple-element.21.order_ref.order, bf16[8,192,128]{2,1,0:T(8,128)(2,1)S(1)} %all-to-all-done.1.recv_ref, ...), custom_call_target="tpu_custom_call" | custom-call | flops 4194304 | bytes 4194304 | tf_op jit(solution)/shard_map/pallas_call | solution.py:408
  37.3 0.0 collective-permute-done.1.from_a_ref
  37.3 0.7 %collective-permute-done.2.from_b_ref = bf16[32,128]{1,0:T(8,128)(2,1)S(1)} collective-permute-done((bf16[32,128]{1,0:T(8,128)(2,1)S(1)}, bf16[32,128]{1,0:T(8,128)(2,1)S(1)}, u32[]{:S(2)}, u32[]{:S(2)}) %collective-permute-start.2) | collective-permute-done | bytes 8224 | tf_op jit(solution)/shard_map/ppermute | solution.py:420
  38.0 1.9 %collective-permute-start.4 = (bf16[8,1280]{1,0:T(8,128)(2,1)S(1)}, bf16[8,1280]{1,0:T(8,128)(2,1)S(1)}, u32[]{:S(2)}, u32[]{:S(2)}) collective-permute-start(bf16[8,1280]{1,0:T(8,128)(2,1)S(1)} %get-tuple-element.33), channel_id=1, source_target_pairs={{8,16},{16,8},{24,32},{32,24},{40,48},{48,40},{56,64},{64,56},{72,... | collective-permute-start | bytes 61448 | tf_op jit(solution)/shard_map/ppermute | solution.py:428
  39.9 1.6 %collective-permute-start.3 = (bf16[8,1280]{1,0:T(8,128)(2,1)S(1)}, bf16[8,1280]{1,0:T(8,128)(2,1)S(1)}, u32[]{:S(2)}, u32[]{:S(2)}) collective-permute-start(bf16[8,1280]{1,0:T(8,128)(2,1)S(1)} %get-tuple-element.29.after_ref), channel_id=1, source_target_pairs={{0,8},{8,0},{16,24},{24,16},{32,40},{40,32},{48,56},{56,48},{64,72... | collective-permute-start | bytes 61448 | tf_op jit(solution)/shard_map/ppermute | solution.py:427
  41.5 1.0 %shard_map.75 = bf16[6,16,1024]{2,1,0:T(8,128)(2,1)} custom-call(bf16[8,1280]{1,0:T(8,128)(2,1)S(1)} %get-tuple-element.29.after_ref, bf16[128,256]{1,0:T(8,128)(2,1)S(1)} %get-tuple-element.25.chosen_ref, f32[4,256,128]{2,1,0:T(8,128)S(1)} %get-tuple-element.30.others_ref, bf16[2,16,1024]{2,1,0:T(8,128)(2,1)S(1)} %get-tuple-element.27.wind_ref), custom_call_target="tpu_custom_call" | custom-call | flops 1048576 | bytes 1048576 | tf_op jit(solution)/shard_map/pallas_call | solution.py:424
  42.6 2.9 %collective-permute-done.4.from_b_ref = bf16[8,1280]{1,0:T(8,128)(2,1)S(1)} collective-permute-done((bf16[8,1280]{1,0:T(8,128)(2,1)S(1)}, bf16[8,1280]{1,0:T(8,128)(2,1)S(1)}, u32[]{:S(2)}, u32[]{:S(2)}) %collective-permute-start.4) | collective-permute-done | bytes 20512 | tf_op jit(solution)/shard_map/ppermute | solution.py:428
  45.5 0.0 collective-permute-done.3.from_a_ref
  45.5 1.0 %shard_map.76 = f32[16,1024]{1,0:T(8,128)} custom-call(f32[24,128]{1,0:T(8,128)S(1)} %get-tuple-element.31.cosine_ref, f32[2,16,1280]{2,1,0:T(8,128)S(1)} %get-tuple-element.32.ext_ref, bf16[8,1280]{1,0:T(8,128)(2,1)S(1)} %collective-permute-done.3.from_a_ref, bf16[8,1280]{1,0:T(8,128)(2,1)S(1)} %collective-permute-done.4.from_b_ref), custom_call_target="tpu_custom_call" | custom-call | tf_op jit(solution)/shard_map/pallas_call | solution.py:429
  (1 shorter events, 0.0 us)
Async XLA Ops:
  0.6 14.7 %collective-permute-start = (bf16[6,512,128]{2,1,0:T(8,128)(2,1)}, bf16[6,512,128]{2,1,0:T(8,128)(2,1)S(1)}, u32[]{:S(2)}, u32[]{:S(2)}) collective-permute-start(bf16[6,512,128]{2,1,0:T(8,128)(2,1)} %src_hbm.1), channel_id=1, source_target_pairs={{0,8},{8,0},{16,24},{24,16},{32,40},{40,32},{48,56},{56,48},{64,72... | collective-permute-start | bytes 2359304 | tf_op jit(solution)/shard_map/ppermute | solution.py:356
  16.8 12.6 %all-to-all-start.1 = ((bf16[8,192,128]{2,1,0:T(8,128)(2,1)}), bf16[8,192,128]{2,1,0:T(8,128)(2,1)S(1)}, u32[]{:S(2)}, u32[]{:S(2)}) async-start(bf16[8,192,128]{2,1,0:T(8,128)(2,1)} %shard_map.69.after_ref), calls=%async_computation.1 | async-start | bytes 786432 | tf_op jit(solution)/shard_map/all_to_all | solution.py:354
  22.3 0.7 %copy-start = (s32[256]{0:T(256)S(1)}, s32[256]{0:T(256)}, u32[]{:S(2)}) copy-start(s32[256]{0:T(256)} %param.7) | copy-start | bytes 3076
  30.2 7.1 %collective-permute-start.1 = (bf16[32,128]{1,0:T(8,128)(2,1)S(1)}, bf16[32,128]{1,0:T(8,128)(2,1)S(1)}, u32[]{:S(2)}, u32[]{:S(2)}) collective-permute-start(bf16[32,128]{1,0:T(8,128)(2,1)S(1)} %get-tuple-element.28), channel_id=1, source_target_pairs={{0,1},{1,0},{2,3},{3,2},{4,5},{5,4},{6,7},{7,6},{8,9},{9,8},{10,11... | collective-permute-start | bytes 24584 | tf_op jit(solution)/shard_map/ppermute | solution.py:419
  32.2 5.8 %collective-permute-start.2 = (bf16[32,128]{1,0:T(8,128)(2,1)S(1)}, bf16[32,128]{1,0:T(8,128)(2,1)S(1)}, u32[]{:S(2)}, u32[]{:S(2)}) collective-permute-start(bf16[32,128]{1,0:T(8,128)(2,1)S(1)} %get-tuple-element.24.after_ref), channel_id=1, source_target_pairs={{0,7},{1,2},{2,1},{3,4},{4,3},{5,6},{6,5},{7,0},{8,15},{9,10},{10,... | collective-permute-start | bytes 24584 | tf_op jit(solution)/shard_map/ppermute | solution.py:420
  38.0 7.5 %collective-permute-start.4 = (bf16[8,1280]{1,0:T(8,128)(2,1)S(1)}, bf16[8,1280]{1,0:T(8,128)(2,1)S(1)}, u32[]{:S(2)}, u32[]{:S(2)}) collective-permute-start(bf16[8,1280]{1,0:T(8,128)(2,1)S(1)} %get-tuple-element.33), channel_id=1, source_target_pairs={{8,16},{16,8},{24,32},{32,24},{40,48},{48,40},{56,64},{64,56},{72,... | collective-permute-start | bytes 61448 | tf_op jit(solution)/shard_map/ppermute | solution.py:428
  39.9 5.6 %collective-permute-start.3 = (bf16[8,1280]{1,0:T(8,128)(2,1)S(1)}, bf16[8,1280]{1,0:T(8,128)(2,1)S(1)}, u32[]{:S(2)}, u32[]{:S(2)}) collective-permute-start(bf16[8,1280]{1,0:T(8,128)(2,1)S(1)} %get-tuple-element.29.after_ref), channel_id=1, source_target_pairs={{0,8},{8,0},{16,24},{24,16},{32,40},{40,32},{48,56},{56,48},{64,72... | collective-permute-start | bytes 61448 | tf_op jit(solution)/shard_map/ppermute | solution.py:427

commit v8 on v7

--- a/solution.py
+++ b/solution.py
@@ -77,26 +77,24 @@
         copy.wait()
 
 
-def pick_kernel(req_ref, own_ref, mate_ref, send_hbm, picked, sems):
+def pick_kernel(req_ref, own_ref, mate_ref, send_hbm, picked, sem):
     channels, tiles, _ = own_ref.shape
-    _, chips, each, _ = picked.shape
+    chips, each = picked.shape[0], picked.shape[1] // channels
     asked = jnp.transpose(req_ref[...].astype(jnp.float32)).astype(jnp.int32)
     mine = jnp.where(is_odd("band"), tiles, 0)
     cell = iota((each, tiles), 1)
     columns = [jnp.broadcast_to(asked[:each, d : d + 1], (each, tiles)) for d in range(chips)]
     own = jnp.concatenate([as_bf16(column == cell + mine) for column in columns], axis=0)
     mate = jnp.concatenate([as_bf16(column == cell + (tiles - mine)) for column in columns], axis=0)
-    copies = []
     for c in range(0, channels, 2):
         pair = lambda ref: jnp.concatenate([ref[c], ref[c + 1]], axis=1)
         got = (dot(own, pair(own_ref)) + dot(mate, pair(mate_ref))).astype(jnp.bfloat16)
         for k in range(2):
-            picked[c + k] = got[:, k * 128 : (k + 1) * 128].reshape(chips, each, 128)
-            target = send_hbm.at[:, pl.ds((c + k) * each, each)]
-            copies.append(pltpu.make_async_copy(picked.at[c + k], target, sems.at[c + k]))
-            copies[-1].start()
-    for copy in copies:
-        copy.wait()
+            part = slice((c + k) * each, (c + k + 1) * each)
+            picked[:, part] = got[:, k * 128 : (k + 1) * 128].reshape(chips, each, 128)
+    copy = pltpu.make_async_copy(picked, send_hbm, sem)
+    copy.start()
+    copy.wait()
 
 
 def fetch_weights(order_ref, weight_hbm, target, sem, first, count, offset):
@@ -268,7 +266,21 @@
         wind_ref[w] = add_blocks(chosen_ref[...], term[w])
 
 
-def finish_kernel(after_ref, chosen_ref, others_ref, wind_ref, out_ref):
+def spread_lanes(x):
+    for _ in range(2):
+        x = 2.0 * x + (pltpu.roll(x, 1, 1) + pltpu.roll(x, x.shape[1] - 1, 1))
+    return x[:, 128 : 128 + C_DEV]
+
+
+def difference(x):
+    return pltpu.roll(x, x.shape[1] - 1, 1) - pltpu.roll(x, 1, 1)
+
+
+def finish_kernel(after_ref, chosen_ref, others_ref, wind_ref, ext_ref, out_ref, east_ref, north_ref):
+    east_ref[...] = jnp.zeros_like(east_ref)
+    north_ref[...] = jnp.zeros_like(north_ref)
+    east_ref[HALO : HALO + R_DEV, :] = spread_lanes(ext_ref[0])
+    north_ref[HALO : HALO + R_DEV, :] = spread_lanes(difference(ext_ref[1]))
     for c in range(out_ref.shape[0]):
         if c in (2, 3):
             out_ref[c] = wind_ref[c - 2]
@@ -288,43 +300,46 @@
         winds.append(jnp.concatenate([left[rows], wind_ref[w].astype(jnp.float32), right[rows]], axis=1))
         ext_ref[w] = winds[w]
     pad = jnp.zeros((8 - 2 * HALO, winds[0].shape[1]), jnp.float32)
-    first = jnp.concatenate([w[:HALO] for w in winds] + [pad], axis=0)
+    first = jnp.concatenate([w[:HALO] for w in winds[::-1]] + [pad], axis=0)
     last = jnp.concatenate([w[R_DEV - HALO :] for w in winds] + [pad], axis=0)
     odd = is_odd("band")
     a_ref[...] = jnp.where(odd, first, last).astype(jnp.bfloat16)
     b_ref[...] = jnp.where(odd, last, first).astype(jnp.bfloat16)
 
 
-def smooth(x):
-    rows, columns = x.shape
-    x = 2.0 * x + (pltpu.roll(x, 1, 0) + pltpu.roll(x, rows - 1, 0))
-    x = 2.0 * x + (pltpu.roll(x, 1, 1) + pltpu.roll(x, columns - 1, 1))
-    return x * (1.0 / 16.0)
-
-
-def smooth_kernel(all_rows, cosine_ref, ext_ref, from_a_ref, from_b_ref, out_ref):
+def spread_rows(x):
+    return 2.0 * x + (pltpu.roll(x, 1, 0) + pltpu.roll(x, x.shape[0] - 1, 0))
+
+
+def smooth_kernel(all_rows, cosine_ref, east_ref, north_ref, from_a_ref, from_b_ref, out_ref):
     from_a = from_a_ref[...].astype(jnp.float32)
     from_b = from_b_ref[...].astype(jnp.float32)
     odd = is_odd("band")
     above = jnp.where(odd, from_a, from_b)
     below = jnp.where(odd, from_b, from_a)
-    pad = jnp.zeros((EXT - R_DEV - 2 * HALO, above.shape[1]), jnp.float32)
-    east, north = (
-        jnp.concatenate([above[w * HALO : (w + 1) * HALO], ext_ref[w], below[w * HALO : (w + 1) * HALO], pad], axis=0)
-        for w in range(2)
-    )
+    top = iota(above.shape, 0) < HALO
+    east = spread_lanes(jnp.where(top, above, below))
+    north = spread_lanes(difference(jnp.where(top, below, above)))
+    top = iota(east.shape, 0) < HALO
+
+    def framed(ref, above, below):
+        last = EXT - 8
+        return jnp.concatenate(
+            [jnp.where(top, above, ref[:8]), ref[8:last], jnp.where(top, ref[last:], below)], axis=0
+        )
+
+    east = framed(east_ref, east, east)
+    north = framed(north_ref, pltpu.roll(north, 8 - HALO, 0), pltpu.roll(north, HALO, 0))
     rows, columns = east.shape
     row = first_row() - HALO + iota((rows, 128), 0)
     inside = jnp.tile((row >= 0) & (row < all_rows), (1, columns // 128))
     cosine = cosine_ref[...]
     scaled = east * jnp.tile(cosine, (1, columns // 128))
     half = jnp.tile(0.5 / cosine, (1, columns // 128))
-    along = pltpu.roll(north, columns - 1, 1) - pltpu.roll(north, 1, 1)
     across = pltpu.roll(scaled, rows - 1, 0) - pltpu.roll(scaled, 1, 0)
-    field = jnp.where(inside, (along - across) * half, 0.0)
-    field = jnp.where(inside, smooth(field), 0.0)
-    field = smooth(field)
-    out_ref[...] = field[HALO : HALO + R_DEV, 128 : 128 + C_DEV]
+    field = jnp.where(inside, (north - across) * half, 0.0)
+    field = spread_rows(jnp.where(inside, spread_rows(field), 0.0))
+    out_ref[...] = field[HALO : HALO + R_DEV] * (1.0 / 256.0)
 
 
 def call(kernel, outs, ins, scratch=(), vmem=2 << 20, cycles=0, out_specs=None):
@@ -365,7 +380,7 @@
         pick_kernel,
         pltpu.HBM((chips, channels * each, pixels), bf16),
         [VM, VM, VM],
-        [pltpu.VMEM((channels, chips, each, pixels), bf16), dmas((channels,))],
+        [pltpu.VMEM((chips, channels * each, pixels), bf16), dmas],
         out_specs=HB,
     )(asked, held(own_tiles, pltpu.VMEM), held(mate_tiles, pltpu.VMEM))
     perm, chosen, rim, order, cosine = call(
@@ -421,16 +436,19 @@
     ext, to_a, to_b = call(extend_kernel, (shape((2, R_DEV, C_DEV + 256), f32), rows, rows), [VM, VM, VM])(
         wind, from_a, from_b
     )
-    remapped = call(
-        finish_kernel, shape((channels, R_DEV, C_DEV), bf16), [ANY, VM, VM, VM], cycles=slots * slots * 16
-    )(to_a, chosen, others, wind)
+    remapped, east, north = call(
+        finish_kernel,
+        (shape((channels, R_DEV, C_DEV), bf16), shape((EXT, C_DEV), f32), shape((EXT, C_DEV), f32)),
+        [ANY, VM, VM, VM, VM],
+        cycles=slots * slots * 16,
+    )(to_a, chosen, others, wind, ext)
     from_a = lax.ppermute(to_a, "band", pairs_a(bands))
     from_b = lax.ppermute(to_b, "band", pairs_b)
     smoothed = call(
         functools.partial(smooth_kernel, R_DEV * bands),
         shape((R_DEV, C_DEV), f32),
-        [VM, VM, VM, VM],
-    )(cosine, ext, from_a, from_b)
+        [VM, VM, VM, VM, VM],
+    )(cosine, east, north, from_a, from_b)
     return remapped, smoothed
 
 

time: 47.1 us -> 47 us (level)
  no operation moved by 1% of the time
where the time goes in v8:
time: 47 us; the launch traced here: 46.4 us
  blocking collectives  13.5 us (29%)
  starting transfers between devices  13.1 us (28%)
  Pallas kernels  10.8 us (23%)
  waiting for transfers between devices  7.08 us (15%)
  between operations  1.37 us (3%)
  local copies, waits for them, and re-layouts  0.67 us (1%)
    all_to_all x1, blocking collectives, on_device(): lax.all_to_all(x, 'band', 0, 0, tiled=True, axis_index_groups=same_core)  13.5 us
    all_to_all x1, starting transfers between devices, on_device(): lax.all_to_all(x, 'band', 0, 0, tiled=True, axis_index_groups=same_core)  4.83 us
    all_to_all x1, waiting for transfers between devices, on_device(): lax.all_to_all(x, 'band', 0, 0, tiled=True, axis_index_groups=same_core)  3.48 us
    ppermute x1, waiting for transfers between devices, on_device(): from_b = lax.ppermute(to_b, 'band', pairs_b)  2.9 us
    ppermute x1, starting transfers between devices, on_device(): from_b = lax.ppermute(to_b, 'lon', ring_b)  2.63 us
    pallas_call x1, Pallas kernels, on_device(): call(rest_kernel, (shape((2, R_DEV, C_DEV), bf16), shape((channels - 2, s...  2.42 us
    ppermute x1, starting transfers between devices, on_device(): from_a = lax.ppermute(to_a, 'lon', pairs_a(lons))  2 us
    ppermute x1, starting transfers between devices, on_device(): from_b = lax.ppermute(to_b, 'band', pairs_b)  1.92 us
  transfers between devices with their start and end apart: 6, of which 3 were waited for; matrix products, arithmetic and copies ran while one was open for 0% of the time, Pallas kernels for 16%

profile of v8, /device:TPU:2, one launch (start us, length us, event | category | flops | bytes accessed | tf_op | source)
XLA Modules:
  0.0 46.4 jit_solution(967520125989646178)
XLA Ops:
  0.6 0.1 collective-permute-start
  0.7 1.2 %shard_map.68 = (s32[8,128]{1,0:T(8,128)S(1)}, s32[8,256]{1,0:T(8,128)S(1)}, bf16[6,512,128]{2,1,0:T(8,128)(2,1)S(1)}) custom-call(s32[1,256]{1,0:T(1,128)} %bitcast.9, bf16[6,512,128]{2,1,0:T(8,128)(2,1)} %src_hbm.1), custom_call_target="tpu_custom_call" | custom-call | tf_op jit(solution)/shard_map/pallas_call | solution.py:372
  1.9 13.5 %all_to_all.16 = s32[8,1,128]{2,1,0:T(1,128)S(1)} all-to-all(s32[8,1,128]{2,1,0:T(1,128)S(1)} %bitcast.7), channel_id=1, replica_groups={{0,16,32,48,64,80,96,112},{8,24,40,56,72,88,104,120},{1,17,33,49,65,81,..., dimensions={0} | all-to-all | bytes 8192 | tf_op jit(solution)/shard_map/all_to_all | solution.py:369
  15.3 0.0 collective-permute-done.mate_ref
  15.4 1.4 %shard_map.69.after_ref = bf16[8,192,128]{2,1,0:T(8,128)(2,1)} custom-call(s32[8,128]{1,0:T(8,128)S(1)} %bitcast.6, bf16[6,512,128]{2,1,0:T(8,128)(2,1)S(1)} %get-tuple-element.22.own_ref, bf16[6,512,128]{2,1,0:T(8,128)(2,1)S(1)} %collective-permute-done.mate_ref), custom_call_target="tpu_custom_call" | custom-call | tf_op jit(solution)/shard_map/pallas_call | solution.py:379
  16.8 4.8 %all-to-all-start.1 = ((bf16[8,192,128]{2,1,0:T(8,128)(2,1)}), bf16[8,192,128]{2,1,0:T(8,128)(2,1)S(1)}, u32[]{:S(2)}, u32[]{:S(2)}) async-start(bf16[8,192,128]{2,1,0:T(8,128)(2,1)} %shard_map.69.after_ref), calls=%async_computation.1 | async-start | bytes 786432 | tf_op jit(solution)/shard_map/all_to_all | solution.py:369
  22.3 0.0 copy-start
  22.3 0.7 %copy-done = s32[256]{0:T(256)S(1)} copy-done((s32[256]{0:T(256)S(1)}, s32[256]{0:T(256)}, u32[]{:S(2)}) %copy-start) | copy-done | bytes 1048
  23.0 1.1 %shard_map.70 = (bf16[256,256]{1,0:T(8,128)(2,1)S(1)}, bf16[128,256]{1,0:T(8,128)(2,1)S(1)}, bf16[32,256]{1,0:T(8,128)(2,1)S(1)}, s32[8,256]{1,0:T(8,128)S(4)}, f32[24,128]{1,0:T(8,128)S(1)}) custom-call(bf16[8,192,128]{2,1,0:T(8,128)(2,1)} %shard_map.69.after_ref, s32[1]{0:T(128)S(6)} %copy.8.live_ref, s32[8,256]{1,0:T(8,128)S(1)} %get-tuple-element.23.pos_ref, ...), custom_call_target="tpu_custom_call" | custom-call | flops 524288 | bytes 524288 | tf_op jit(solution)/shard_map/pallas_call | solution.py:386
  24.1 1.8 %shard_map.71.held_ref = bf16[88,128,128]{2,1,0:T(8,128)(2,1)S(1)} custom-call(s32[8,256]{1,0:T(8,128)S(4)} %get-tuple-element.24.order_ref.order, bf16[8,192,128]{2,1,0:T(8,128)(2,1)} %shard_map.69.after_ref, bf16[256,128,128]{2,1,0:T(8,128)(2,1)} %weight_hbm.5), custom_call_target="tpu_custom_call" | custom-call | flops 2883584 | bytes 2883584 | tf_op jit(solution)/shard_map/pallas_call | solution.py:403
  25.9 3.5 %all-to-all-done.1.recv_ref = bf16[8,192,128]{2,1,0:T(8,128)(2,1)S(1)} async-done(((bf16[8,192,128]{2,1,0:T(8,128)(2,1)}), bf16[8,192,128]{2,1,0:T(8,128)(2,1)S(1)}, u32[]{:S(2)}, u32[]{:S(2)}) %all-to-all-start.1) | async-done | bytes 393248 | tf_op jit(solution)/shard_map/all_to_all | solution.py:369
  29.4 0.8 %shard_map.72 = (bf16[32,128]{1,0:T(8,128)(2,1)S(1)}, bf16[32,128]{1,0:T(8,128)(2,1)S(1)}, f32[2,256,128]{2,1,0:T(8,128)S(1)}) custom-call(s32[8,256]{1,0:T(8,128)S(4)} %get-tuple-element.24.order_ref.order, bf16[8,192,128]{2,1,0:T(8,128)(2,1)S(1)} %all-to-all-done.1.recv_ref, bf16[256,256]{1,0:T(8,128)(2,1)S(1)} %get-tuple-element.25.perm_ref, ...), custom_call_target="tpu_custom_call" | custom-call | tf_op jit(solution)/shard_map/pallas_call | solution.py:416
  30.2 2.0 %collective-permute-start.1 = (bf16[32,128]{1,0:T(8,128)(2,1)S(1)}, bf16[32,128]{1,0:T(8,128)(2,1)S(1)}, u32[]{:S(2)}, u32[]{:S(2)}) collective-permute-start(bf16[32,128]{1,0:T(8,128)(2,1)S(1)} %get-tuple-element.31), channel_id=1, source_target_pairs={{0,1},{1,0},{2,3},{3,2},{4,5},{5,4},{6,7},{7,6},{8,9},{9,8},{10,11... | collective-permute-start | bytes 24584 | tf_op jit(solution)/shard_map/ppermute | solution.py:434
  32.2 2.6 %collective-permute-start.2 = (bf16[32,128]{1,0:T(8,128)(2,1)S(1)}, bf16[32,128]{1,0:T(8,128)(2,1)S(1)}, u32[]{:S(2)}, u32[]{:S(2)}) collective-permute-start(bf16[32,128]{1,0:T(8,128)(2,1)S(1)} %get-tuple-element.27.after_ref), channel_id=1, source_target_pairs={{0,7},{1,2},{2,1},{3,4},{4,3},{5,6},{6,5},{7,0},{8,15},{9,10},{10,... | collective-permute-start | bytes 24584 | tf_op jit(solution)/shard_map/ppermute | solution.py:435
  34.8 2.4 %shard_map.73 = (bf16[2,16,1024]{2,1,0:T(8,128)(2,1)S(1)}, f32[4,256,128]{2,1,0:T(8,128)S(1)}) custom-call(bf16[32,128]{1,0:T(8,128)(2,1)S(1)} %get-tuple-element.27.after_ref, s32[8,256]{1,0:T(8,128)S(4)} %get-tuple-element.24.order_ref.order, bf16[8,192,128]{2,1,0:T(8,128)(2,1)S(1)} %all-to-all-done.1.recv_ref, ...), custom_call_target="tpu_custom_call" | custom-call | flops 4194304 | bytes 4194304 | tf_op jit(solution)/shard_map/pallas_call | solution.py:423
  37.2 0.0 collective-permute-done.1.from_a_ref
  37.3 0.7 %collective-permute-done.2.from_b_ref = bf16[32,128]{1,0:T(8,128)(2,1)S(1)} collective-permute-done((bf16[32,128]{1,0:T(8,128)(2,1)S(1)}, bf16[32,128]{1,0:T(8,128)(2,1)S(1)}, u32[]{:S(2)}, u32[]{:S(2)}) %collective-permute-start.2) | collective-permute-done | bytes 8224 | tf_op jit(solution)/shard_map/ppermute | solution.py:435
  38.0 1.9 %collective-permute-start.4 = (bf16[8,1280]{1,0:T(8,128)(2,1)S(1)}, bf16[8,1280]{1,0:T(8,128)(2,1)S(1)}, u32[]{:S(2)}, u32[]{:S(2)}) collective-permute-start(bf16[8,1280]{1,0:T(8,128)(2,1)S(1)} %get-tuple-element.39), channel_id=1, source_target_pairs={{8,16},{16,8},{24,32},{32,24},{40,48},{48,40},{56,64},{64,56},{72,... | collective-permute-start | bytes 61448 | tf_op jit(solution)/shard_map/ppermute | solution.py:446
  39.9 1.6 %collective-permute-start.3 = (bf16[8,1280]{1,0:T(8,128)(2,1)S(1)}, bf16[8,1280]{1,0:T(8,128)(2,1)S(1)}, u32[]{:S(2)}, u32[]{:S(2)}) collective-permute-start(bf16[8,1280]{1,0:T(8,128)(2,1)S(1)} %get-tuple-element.32.after_ref), channel_id=1, source_target_pairs={{0,8},{8,0},{16,24},{24,16},{32,40},{40,32},{48,56},{56,48},{64,72... | collective-permute-start | bytes 61448 | tf_op jit(solution)/shard_map/ppermute | solution.py:445
  41.5 1.1 %shard_map.75 = (bf16[6,16,1024]{2,1,0:T(8,128)(2,1)}, f32[24,1024]{1,0:T(8,128)S(1)}, f32[24,1024]{1,0:T(8,128)S(1)}) custom-call(bf16[8,1280]{1,0:T(8,128)(2,1)S(1)} %get-tuple-element.32.after_ref, bf16[128,256]{1,0:T(8,128)(2,1)S(1)} %get-tuple-element.28.chosen_ref, f32[4,256,128]{2,1,0:T(8,128)S(1)} %get-tuple-element.33.others_ref, ...), custom_call_target="tpu_custom_call" | custom-call | flops 1048576 | bytes 1048576 | tf_op jit(solution)/shard_map/pallas_call | solution.py:439
  42.6 2.9 %collective-permute-done.4.from_b_ref = bf16[8,1280]{1,0:T(8,128)(2,1)S(1)} collective-permute-done((bf16[8,1280]{1,0:T(8,128)(2,1)S(1)}, bf16[8,1280]{1,0:T(8,128)(2,1)S(1)}, u32[]{:S(2)}, u32[]{:S(2)}) %collective-permute-start.4) | collective-permute-done | bytes 20512 | tf_op jit(solution)/shard_map/ppermute | solution.py:446
  45.5 0.0 collective-permute-done.3.from_a_ref
  45.5 1.0 %shard_map.76 = f32[16,1024]{1,0:T(8,128)} custom-call(f32[24,128]{1,0:T(8,128)S(1)} %get-tuple-element.36.cosine_ref, f32[24,1024]{1,0:T(8,128)S(1)} %get-tuple-element.37.east_ref, f32[24,1024]{1,0:T(8,128)S(1)} %get-tuple-element.38.north_ref, bf16[8,1280]{1,0:T(8,128)(2,1)S(1)} %collective-permute-done.3.from_a_ref, ...), custom_call_target="tpu_custom_call" | custom-call | tf_op jit(solution)/shard_map/pallas_call | solution.py:447
  (1 shorter events, 0.0 us)
Async XLA Ops:
  0.6 14.7 %collective-permute-start = (bf16[6,512,128]{2,1,0:T(8,128)(2,1)}, bf16[6,512,128]{2,1,0:T(8,128)(2,1)S(1)}, u32[]{:S(2)}, u32[]{:S(2)}) collective-permute-start(bf16[6,512,128]{2,1,0:T(8,128)(2,1)} %src_hbm.1), channel_id=1, source_target_pairs={{0,8},{8,0},{16,24},{24,16},{32,40},{40,32},{48,56},{56,48},{64,72... | collective-permute-start | bytes 2359304 | tf_op jit(solution)/shard_map/ppermute | solution.py:371
  16.8 12.6 %all-to-all-start.1 = ((bf16[8,192,128]{2,1,0:T(8,128)(2,1)}), bf16[8,192,128]{2,1,0:T(8,128)(2,1)S(1)}, u32[]{:S(2)}, u32[]{:S(2)}) async-start(bf16[8,192,128]{2,1,0:T(8,128)(2,1)} %shard_map.69.after_ref), calls=%async_computation.1 | async-start | bytes 786432 | tf_op jit(solution)/shard_map/all_to_all | solution.py:369
  22.3 0.7 %copy-start = (s32[256]{0:T(256)S(1)}, s32[256]{0:T(256)}, u32[]{:S(2)}) copy-start(s32[256]{0:T(256)} %param.7) | copy-start | bytes 3076
  30.2 7.1 %collective-permute-start.1 = (bf16[32,128]{1,0:T(8,128)(2,1)S(1)}, bf16[32,128]{1,0:T(8,128)(2,1)S(1)}, u32[]{:S(2)}, u32[]{:S(2)}) collective-permute-start(bf16[32,128]{1,0:T(8,128)(2,1)S(1)} %get-tuple-element.31), channel_id=1, source_target_pairs={{0,1},{1,0},{2,3},{3,2},{4,5},{5,4},{6,7},{7,6},{8,9},{9,8},{10,11... | collective-permute-start | bytes 24584 | tf_op jit(solution)/shard_map/ppermute | solution.py:434
  32.2 5.8 %collective-permute-start.2 = (bf16[32,128]{1,0:T(8,128)(2,1)S(1)}, bf16[32,128]{1,0:T(8,128)(2,1)S(1)}, u32[]{:S(2)}, u32[]{:S(2)}) collective-permute-start(bf16[32,128]{1,0:T(8,128)(2,1)S(1)} %get-tuple-element.27.after_ref), channel_id=1, source_target_pairs={{0,7},{1,2},{2,1},{3,4},{4,3},{5,6},{6,5},{7,0},{8,15},{9,10},{10,... | collective-permute-start | bytes 24584 | tf_op jit(solution)/shard_map/ppermute | solution.py:435
  38.0 7.5 %collective-permute-start.4 = (bf16[8,1280]{1,0:T(8,128)(2,1)S(1)}, bf16[8,1280]{1,0:T(8,128)(2,1)S(1)}, u32[]{:S(2)}, u32[]{:S(2)}) collective-permute-start(bf16[8,1280]{1,0:T(8,128)(2,1)S(1)} %get-tuple-element.39), channel_id=1, source_target_pairs={{8,16},{16,8},{24,32},{32,24},{40,48},{48,40},{56,64},{64,56},{72,... | collective-permute-start | bytes 61448 | tf_op jit(solution)/shard_map/ppermute | solution.py:446
  39.9 5.6 %collective-permute-start.3 = (bf16[8,1280]{1,0:T(8,128)(2,1)S(1)}, bf16[8,1280]{1,0:T(8,128)(2,1)S(1)}, u32[]{:S(2)}, u32[]{:S(2)}) collective-permute-start(bf16[8,1280]{1,0:T(8,128)(2,1)S(1)} %get-tuple-element.32.after_ref), channel_id=1, source_target_pairs={{0,8},{8,0},{16,24},{24,16},{32,40},{40,32},{48,56},{56,48},{64,72... | collective-permute-start | bytes 61448 | tf_op jit(solution)/shard_map/ppermute | solution.py:445

commit v9 on v8

--- a/solution.py
+++ b/solution.py
@@ -15,7 +15,7 @@
 LAT_START = 0.5
 HALO = 3
 HELD = 88
-FIRST = 56
+FIRST = 48
 CHUNK = 24
 EXT = 24
 

time: 47 us -> 47 us (level)
  Pallas kernels: 10.8 us -> 10.2 us
  waiting for transfers between devices: 7.08 us -> 7.59 us
    ppermute x1, waiting for transfers between devices: 0.69 us -> 1.2 us  [on_device(): from_b = lax.ppermute(to_b, 'lon', ring_b)]
    pallas_call x1, Pallas kernels: 2.42 us -> 1.91 us  [on_device(): call(rest_kernel, (shape((2, R_DEV, C_DEV), bf16), shape((channels - 2, s...]
  transfers between devices with their start and end apart: 6 -> 6, of which waited for: 3 -> 3; matrix products, arithmetic and copies ran while one was open for 0% -> 0% of each run, Pallas kernels for 16% -> 15%
where the time goes in v9:
time: 47 us; the launch traced here: 46.4 us
  blocking collectives  13.5 us (29%)
  starting transfers between devices  13.1 us (28%)
  Pallas kernels  10.2 us (22%)
  waiting for transfers between devices  7.59 us (16%)
  between operations  1.37 us (3%)
  local copies, waits for them, and re-layouts  0.67 us (1%)
    all_to_all x1, blocking collectives, on_device(): lax.all_to_all(x, 'band', 0, 0, tiled=True, axis_index_groups=same_core)  13.5 us
    all_to_all x1, starting transfers between devices, on_device(): lax.all_to_all(x, 'band', 0, 0, tiled=True, axis_index_groups=same_core)  4.83 us
    all_to_all x1, waiting for transfers between devices, on_device(): lax.all_to_all(x, 'band', 0, 0, tiled=True, axis_index_groups=same_core)  3.48 us
    ppermute x1, waiting for transfers between devices, on_device(): from_b = lax.ppermute(to_b, 'band', pairs_b)  2.9 us
    ppermute x1, starting transfers between devices, on_device(): from_b = lax.ppermute(to_b, 'lon', ring_b)  2.63 us
    ppermute x1, starting transfers between devices, on_device(): from_a = lax.ppermute(to_a, 'lon', pairs_a(lons))  2 us
    ppermute x1, starting transfers between devices, on_device(): from_b = lax.ppermute(to_b, 'band', pairs_b)  1.92 us
    pallas_call x1, Pallas kernels, on_device(): call(rest_kernel, (shape((2, R_DEV, C_DEV), bf16), shape((channels - 2, s...  1.91 us
  transfers between devices with their start and end apart: 6, of which 3 were waited for; matrix products, arithmetic and copies ran while one was open for 0% of the time, Pallas kernels for 15%

profile of v9, /device:TPU:2, one launch (start us, length us, event | category | flops | bytes accessed | tf_op | source)
XLA Modules:
  0.0 46.4 jit_solution(2960651005454314873)
XLA Ops:
  0.6 0.1 collective-permute-start
  0.7 1.2 %shard_map.68 = (s32[8,128]{1,0:T(8,128)S(1)}, s32[8,256]{1,0:T(8,128)S(1)}, bf16[6,512,128]{2,1,0:T(8,128)(2,1)S(1)}) custom-call(s32[1,256]{1,0:T(1,128)} %bitcast.9, bf16[6,512,128]{2,1,0:T(8,128)(2,1)} %src_hbm.1), custom_call_target="tpu_custom_call" | custom-call | tf_op jit(solution)/shard_map/pallas_call | solution.py:372
  1.9 13.5 %all_to_all.16 = s32[8,1,128]{2,1,0:T(1,128)S(1)} all-to-all(s32[8,1,128]{2,1,0:T(1,128)S(1)} %bitcast.7), channel_id=1, replica_groups={{0,16,32,48,64,80,96,112},{8,24,40,56,72,88,104,120},{1,17,33,49,65,81,..., dimensions={0} | all-to-all | bytes 8192 | tf_op jit(solution)/shard_map/all_to_all | solution.py:369
  15.3 0.0 collective-permute-done.mate_ref
  15.4 1.4 %shard_map.69.after_ref = bf16[8,192,128]{2,1,0:T(8,128)(2,1)} custom-call(s32[8,128]{1,0:T(8,128)S(1)} %bitcast.6, bf16[6,512,128]{2,1,0:T(8,128)(2,1)S(1)} %get-tuple-element.22.own_ref, bf16[6,512,128]{2,1,0:T(8,128)(2,1)S(1)} %collective-permute-done.mate_ref), custom_call_target="tpu_custom_call" | custom-call | tf_op jit(solution)/shard_map/pallas_call | solution.py:379
  16.8 4.8 %all-to-all-start.1 = ((bf16[8,192,128]{2,1,0:T(8,128)(2,1)}), bf16[8,192,128]{2,1,0:T(8,128)(2,1)S(1)}, u32[]{:S(2)}, u32[]{:S(2)}) async-start(bf16[8,192,128]{2,1,0:T(8,128)(2,1)} %shard_map.69.after_ref), calls=%async_computation.1 | async-start | bytes 786432 | tf_op jit(solution)/shard_map/all_to_all | solution.py:369
  22.3 0.0 copy-start
  22.3 0.7 %copy-done = s32[256]{0:T(256)S(1)} copy-done((s32[256]{0:T(256)S(1)}, s32[256]{0:T(256)}, u32[]{:S(2)}) %copy-start) | copy-done | bytes 1048
  23.0 1.1 %shard_map.70 = (bf16[256,256]{1,0:T(8,128)(2,1)S(1)}, bf16[128,256]{1,0:T(8,128)(2,1)S(1)}, bf16[32,256]{1,0:T(8,128)(2,1)S(1)}, s32[8,256]{1,0:T(8,128)S(4)}, f32[24,128]{1,0:T(8,128)S(1)}) custom-call(bf16[8,192,128]{2,1,0:T(8,128)(2,1)} %shard_map.69.after_ref, s32[1]{0:T(128)S(6)} %copy.8.live_ref, s32[8,256]{1,0:T(8,128)S(1)} %get-tuple-element.23.pos_ref, ...), custom_call_target="tpu_custom_call" | custom-call | flops 524288 | bytes 524288 | tf_op jit(solution)/shard_map/pallas_call | solution.py:386
  24.1 1.8 %shard_map.71.held_ref = bf16[88,128,128]{2,1,0:T(8,128)(2,1)S(1)} custom-call(s32[8,256]{1,0:T(8,128)S(4)} %get-tuple-element.24.order_ref.order, bf16[8,192,128]{2,1,0:T(8,128)(2,1)} %shard_map.69.after_ref, bf16[256,128,128]{2,1,0:T(8,128)(2,1)} %weight_hbm.5), custom_call_target="tpu_custom_call" | custom-call | flops 2883584 | bytes 2883584 | tf_op jit(solution)/shard_map/pallas_call | solution.py:403
  25.9 3.5 %all-to-all-done.1.recv_ref = bf16[8,192,128]{2,1,0:T(8,128)(2,1)S(1)} async-done(((bf16[8,192,128]{2,1,0:T(8,128)(2,1)}), bf16[8,192,128]{2,1,0:T(8,128)(2,1)S(1)}, u32[]{:S(2)}, u32[]{:S(2)}) %all-to-all-start.1) | async-done | bytes 393248 | tf_op jit(solution)/shard_map/all_to_all | solution.py:369
  29.4 0.8 %shard_map.72 = (bf16[32,128]{1,0:T(8,128)(2,1)S(1)}, bf16[32,128]{1,0:T(8,128)(2,1)S(1)}, f32[2,256,128]{2,1,0:T(8,128)S(1)}) custom-call(s32[8,256]{1,0:T(8,128)S(4)} %get-tuple-element.24.order_ref.order, bf16[8,192,128]{2,1,0:T(8,128)(2,1)S(1)} %all-to-all-done.1.recv_ref, bf16[256,256]{1,0:T(8,128)(2,1)S(1)} %get-tuple-element.25.perm_ref, ...), custom_call_target="tpu_custom_call" | custom-call | tf_op jit(solution)/shard_map/pallas_call | solution.py:416
  30.1 2.0 %collective-permute-start.1 = (bf16[32,128]{1,0:T(8,128)(2,1)S(1)}, bf16[32,128]{1,0:T(8,128)(2,1)S(1)}, u32[]{:S(2)}, u32[]{:S(2)}) collective-permute-start(bf16[32,128]{1,0:T(8,128)(2,1)S(1)} %get-tuple-element.31), channel_id=1, source_target_pairs={{0,1},{1,0},{2,3},{3,2},{4,5},{5,4},{6,7},{7,6},{8,9},{9,8},{10,11... | collective-permute-start | bytes 24584 | tf_op jit(solution)/shard_map/ppermute | solution.py:434
  32.1 2.6 %collective-permute-start.2 = (bf16[32,128]{1,0:T(8,128)(2,1)S(1)}, bf16[32,128]{1,0:T(8,128)(2,1)S(1)}, u32[]{:S(2)}, u32[]{:S(2)}) collective-permute-start(bf16[32,128]{1,0:T(8,128)(2,1)S(1)} %get-tuple-element.27.after_ref), channel_id=1, source_target_pairs={{0,7},{1,2},{2,1},{3,4},{4,3},{5,6},{6,5},{7,0},{8,15},{9,10},{10,... | collective-permute-start | bytes 24584 | tf_op jit(solution)/shard_map/ppermute | solution.py:435
  34.8 1.9 %shard_map.73 = (bf16[2,16,1024]{2,1,0:T(8,128)(2,1)S(1)}, f32[4,256,128]{2,1,0:T(8,128)S(1)}) custom-call(bf16[32,128]{1,0:T(8,128)(2,1)S(1)} %get-tuple-element.27.after_ref, s32[8,256]{1,0:T(8,128)S(4)} %get-tuple-element.24.order_ref.order, bf16[8,192,128]{2,1,0:T(8,128)(2,1)S(1)} %all-to-all-done.1.recv_ref, ...), custom_call_target="tpu_custom_call" | custom-call | flops 4194304 | bytes 4194304 | tf_op jit(solution)/shard_map/pallas_call | solution.py:423
  36.7 0.0 collective-permute-done.1.from_a_ref
  36.7 1.2 %collective-permute-done.2.from_b_ref = bf16[32,128]{1,0:T(8,128)(2,1)S(1)} collective-permute-done((bf16[32,128]{1,0:T(8,128)(2,1)S(1)}, bf16[32,128]{1,0:T(8,128)(2,1)S(1)}, u32[]{:S(2)}, u32[]{:S(2)}) %collective-permute-start.2) | collective-permute-done | bytes 8224 | tf_op jit(solution)/shard_map/ppermute | solution.py:435
  37.9 1.9 %collective-permute-start.4 = (bf16[8,1280]{1,0:T(8,128)(2,1)S(1)}, bf16[8,1280]{1,0:T(8,128)(2,1)S(1)}, u32[]{:S(2)}, u32[]{:S(2)}) collective-permute-start(bf16[8,1280]{1,0:T(8,128)(2,1)S(1)} %get-tuple-element.39), channel_id=1, source_target_pairs={{8,16},{16,8},{24,32},{32,24},{40,48},{48,40},{56,64},{64,56},{72,... | collective-permute-start | bytes 61448 | tf_op jit(solution)/shard_map/ppermute | solution.py:446
  39.9 1.6 %collective-permute-start.3 = (bf16[8,1280]{1,0:T(8,128)(2,1)S(1)}, bf16[8,1280]{1,0:T(8,128)(2,1)S(1)}, u32[]{:S(2)}, u32[]{:S(2)}) collective-permute-start(bf16[8,1280]{1,0:T(8,128)(2,1)S(1)} %get-tuple-element.32.after_ref), channel_id=1, source_target_pairs={{0,8},{8,0},{16,24},{24,16},{32,40},{40,32},{48,56},{56,48},{64,72... | collective-permute-start | bytes 61448 | tf_op jit(solution)/shard_map/ppermute | solution.py:445
  41.5 1.1 %shard_map.75 = (bf16[6,16,1024]{2,1,0:T(8,128)(2,1)}, f32[24,1024]{1,0:T(8,128)S(1)}, f32[24,1024]{1,0:T(8,128)S(1)}) custom-call(bf16[8,1280]{1,0:T(8,128)(2,1)S(1)} %get-tuple-element.32.after_ref, bf16[128,256]{1,0:T(8,128)(2,1)S(1)} %get-tuple-element.28.chosen_ref, f32[4,256,128]{2,1,0:T(8,128)S(1)} %get-tuple-element.33.others_ref, ...), custom_call_target="tpu_custom_call" | custom-call | flops 1048576 | bytes 1048576 | tf_op jit(solution)/shard_map/pallas_call | solution.py:439
  42.5 2.9 %collective-permute-done.4.from_b_ref = bf16[8,1280]{1,0:T(8,128)(2,1)S(1)} collective-permute-done((bf16[8,1280]{1,0:T(8,128)(2,1)S(1)}, bf16[8,1280]{1,0:T(8,128)(2,1)S(1)}, u32[]{:S(2)}, u32[]{:S(2)}) %collective-permute-start.4) | collective-permute-done | bytes 20512 | tf_op jit(solution)/shard_map/ppermute | solution.py:446
  45.4 0.0 collective-permute-done.3.from_a_ref
  45.4 1.0 %shard_map.76 = f32[16,1024]{1,0:T(8,128)} custom-call(f32[24,128]{1,0:T(8,128)S(1)} %get-tuple-element.36.cosine_ref, f32[24,1024]{1,0:T(8,128)S(1)} %get-tuple-element.37.east_ref, f32[24,1024]{1,0:T(8,128)S(1)} %get-tuple-element.38.north_ref, bf16[8,1280]{1,0:T(8,128)(2,1)S(1)} %collective-permute-done.3.from_a_ref, ...), custom_call_target="tpu_custom_call" | custom-call | tf_op jit(solution)/shard_map/pallas_call | solution.py:447
  (1 shorter events, 0.0 us)
Async XLA Ops:
  0.6 14.7 %collective-permute-start = (bf16[6,512,128]{2,1,0:T(8,128)(2,1)}, bf16[6,512,128]{2,1,0:T(8,128)(2,1)S(1)}, u32[]{:S(2)}, u32[]{:S(2)}) collective-permute-start(bf16[6,512,128]{2,1,0:T(8,128)(2,1)} %src_hbm.1), channel_id=1, source_target_pairs={{0,8},{8,0},{16,24},{24,16},{32,40},{40,32},{48,56},{56,48},{64,72... | collective-permute-start | bytes 2359304 | tf_op jit(solution)/shard_map/ppermute | solution.py:371
  16.8 12.6 %all-to-all-start.1 = ((bf16[8,192,128]{2,1,0:T(8,128)(2,1)}), bf16[8,192,128]{2,1,0:T(8,128)(2,1)S(1)}, u32[]{:S(2)}, u32[]{:S(2)}) async-start(bf16[8,192,128]{2,1,0:T(8,128)(2,1)} %shard_map.69.after_ref), calls=%async_computation.1 | async-start | bytes 786432 | tf_op jit(solution)/shard_map/all_to_all | solution.py:369
  22.3 0.7 %copy-start = (s32[256]{0:T(256)S(1)}, s32[256]{0:T(256)}, u32[]{:S(2)}) copy-start(s32[256]{0:T(256)} %param.7) | copy-start | bytes 3076
  30.1 6.6 %collective-permute-start.1 = (bf16[32,128]{1,0:T(8,128)(2,1)S(1)}, bf16[32,128]{1,0:T(8,128)(2,1)S(1)}, u32[]{:S(2)}, u32[]{:S(2)}) collective-permute-start(bf16[32,128]{1,0:T(8,128)(2,1)S(1)} %get-tuple-element.31), channel_id=1, source_target_pairs={{0,1},{1,0},{2,3},{3,2},{4,5},{5,4},{6,7},{7,6},{8,9},{9,8},{10,11... | collective-permute-start | bytes 24584 | tf_op jit(solution)/shard_map/ppermute | solution.py:434
  32.1 5.8 %collective-permute-start.2 = (bf16[32,128]{1,0:T(8,128)(2,1)S(1)}, bf16[32,128]{1,0:T(8,128)(2,1)S(1)}, u32[]{:S(2)}, u32[]{:S(2)}) collective-permute-start(bf16[32,128]{1,0:T(8,128)(2,1)S(1)} %get-tuple-element.27.after_ref), channel_id=1, source_target_pairs={{0,7},{1,2},{2,1},{3,4},{4,3},{5,6},{6,5},{7,0},{8,15},{9,10},{10,... | collective-permute-start | bytes 24584 | tf_op jit(solution)/shard_map/ppermute | solution.py:435
  37.9 7.5 %collective-permute-start.4 = (bf16[8,1280]{1,0:T(8,128)(2,1)S(1)}, bf16[8,1280]{1,0:T(8,128)(2,1)S(1)}, u32[]{:S(2)}, u32[]{:S(2)}) collective-permute-start(bf16[8,1280]{1,0:T(8,128)(2,1)S(1)} %get-tuple-element.39), channel_id=1, source_target_pairs={{8,16},{16,8},{24,32},{32,24},{40,48},{48,40},{56,64},{64,56},{72,... | collective-permute-start | bytes 61448 | tf_op jit(solution)/shard_map/ppermute | solution.py:446
  39.9 5.6 %collective-permute-start.3 = (bf16[8,1280]{1,0:T(8,128)(2,1)S(1)}, bf16[8,1280]{1,0:T(8,128)(2,1)S(1)}, u32[]{:S(2)}, u32[]{:S(2)}) collective-permute-start(bf16[8,1280]{1,0:T(8,128)(2,1)S(1)} %get-tuple-element.32.after_ref), channel_id=1, source_target_pairs={{0,8},{8,0},{16,24},{24,16},{32,40},{40,32},{48,56},{56,48},{64,72... | collective-permute-start | bytes 61448 | tf_op jit(solution)/shard_map/ppermute | solution.py:445
